TPU v7x, 128 devices: a whole 4x4x4 slice. The times are simulated.
128 devices in a mesh: ctx: 32 (over x, z, core), head: 4 (over y).
Axes of the slice: x: 4, y: 4, z: 4, core: 2. Of those that a mesh axis runs over, the one named last changes fastest.
Arguments:
- tokens: bfloat16 [16384, 2560], P('ctx', 'head'), may hold values from -6 to 6
- send_rows: int32 [32, 32, 32], P('ctx'), may hold values from 0 to 511, as said below
- send_counts: int32 [32, 32], replicated, may hold values from 0 to 32, as said below
- stretch_segments: int32 [64], replicated, may hold values from 0 to 12, never falling along the last dimension, each value on 1 to 6 neighbouring positions
- main_proj: bfloat16 [2560, 2, 5120], P(None, None, 'head'), may hold values from -0.125 to 0.125
- state_proj: bfloat16 [2560, 256], replicated, may hold values from -0.125 to 0.125
- step_proj: bfloat16 [2560, 80], P(None, 'head'), may hold values from -0.125 to 0.125
- conv_main: float32 [4, 5120], P(None, 'head'), may hold values from -3 to 3
- conv_state: float32 [4, 256], replicated, may hold values from -3 to 3
- step_bias: float32 [80], P('head'), may hold values from -11 to -3.5
- decay_log: float32 [80], P('head'), may hold values from 0 to 1.39
- skip_gain: float32 [80], P('head'), may hold values from 0.05 to 0.8
- norm_gain: float32 [5120], P('head'), may hold values from 0.5 to 1.5
- out_proj: bfloat16 [5120, 2560], P('head'), may hold values from -0.078125 to 0.078125
Outputs:
- mixed: bfloat16 [16384, 2560], P('ctx', 'head')
Inputs may be any that keep to these rules, and one draw needn't show every extreme that they name: Entries 0 to send_counts[s, d] - 1 of send_rows[s, d] name distinct rows of generator s's 512; over all d every row of s is named once; other entries are 0. `send_counts`: every row and every column sums to 512. `stretch_segments`: Non-decreasing; a document spans 1 to 6 blocks.
All inputs are finite; a program needn't handle non-finite values.
Results may differ from a plain program's by a relative error of at most 0.015.
Values may be sent and summed in bfloat16 or wider, within the bound.
No kernel may reach another device: no remote copies, remote signals or barrier semaphores. Data moves between devices by JAX's collectives and lax.ppermute only.
A program may use at most 128 MiB of HBM per device.

v0:
```python
import jax
import jax.numpy as jnp
from jax import lax
from jax.sharding import PartitionSpec as P

HEADS = 80
HEAD_DIM = 64
STRETCH = 256


def shifted(value, axis, steps):
    count = lax.axis_size(axis)
    first, last = (max(0, -steps), min(count, count - steps))
    return lax.ppermute(value, axis, [(source, source + steps) for source in range(first, last)])


def carried_in(array, axis, join, neutral):
    place = lax.axis_index(axis)
    gathered = jax.tree.map(
        lambda a, kind: lax.all_gather(a.astype(kind), axis), array, (jnp.bfloat16, jnp.bfloat16)
    )
    state = jax.tree.map(lambda a, e: jnp.zeros_like(a) + jnp.asarray(e, a.dtype), array, neutral)

    def one(turn, state):
        return join(
            state,
            jax.tree.map(
                lambda a, own: lax.dynamic_index_in_dim(a, turn, 0, False).astype(own.dtype),
                gathered,
                array,
            ),
        )

    return lax.fori_loop(0, place, one, state)


def arrange_rows(arrived, send_counts, ctx_index, tok_dev):
    sources = arrived.shape[0]
    slots_each = arrived.shape[1]
    column = lax.dynamic_slice_in_dim(send_counts, ctx_index, 1, 1)[:, 0]
    source_ends = jnp.cumsum(column)
    begins = source_ends - column
    slot_pos = jnp.arange(tok_dev, dtype=jnp.int32)
    source_of = jnp.sum((slot_pos[:, None] >= source_ends[None, :]).astype(jnp.int32), axis=1)
    source_match = source_of[:, None] == jnp.arange(sources, dtype=jnp.int32)[None, :]
    source_start = jnp.sum(jnp.where(source_match, begins[None, :], 0), axis=1)
    flat_index = source_of * slots_each + slot_pos - source_start
    return arrived.reshape(sources * slots_each, arrived.shape[2])[flat_index]


def on_device(
    tokens,
    send_rows,
    send_counts,
    stretch_segments,
    main_proj,
    state_proj,
    step_proj,
    conv_main,
    conv_state,
    step_bias,
    decay_log,
    skip_gain,
    norm_gain,
    out_proj,
):
    ctx_index = lax.axis_index("ctx")
    tok_dev = tokens.shape[0]
    sources = send_rows.shape[1]
    slots_each = send_rows.shape[2]
    send_list = send_rows[0].reshape(sources * slots_each)
    model_width = main_proj.shape[0]
    inner_width = main_proj.shape[2]
    heads_dev = step_bias.shape[0]
    head_dim = inner_width // heads_dev
    state_width = state_proj.shape[1] // 2
    main_flat = main_proj.reshape(model_width, 2 * inner_width)
    outgoing = tokens[send_list].reshape(sources, slots_each, tokens.shape[1])
    arrived = lax.all_to_all(outgoing, "ctx", split_axis=0, concat_axis=0, tiled=True)
    packed = arrange_rows(arrived, send_counts, ctx_index, tok_dev)
    piece_cols = lax.all_gather(packed, "head", axis=1, tiled=True)
    gate_up = jnp.dot(piece_cols, main_flat, preferred_element_type=jnp.float32)
    state_raw = jnp.dot(piece_cols, state_proj, preferred_element_type=jnp.float32)
    step_raw = jnp.dot(piece_cols, step_proj, preferred_element_type=jnp.float32)
    gate_in = gate_up[:, :inner_width].astype(jnp.bfloat16)
    channels = jnp.concatenate(
        [gate_up[:, inner_width:].astype(jnp.bfloat16), state_raw.astype(jnp.bfloat16)], axis=1
    )
    block_len = STRETCH
    blocks_here = tok_dev // block_len
    first_block = ctx_index * blocks_here
    local_ids = lax.dynamic_slice_in_dim(stretch_segments, first_block, blocks_here)
    prior_id = lax.dynamic_slice_in_dim(stretch_segments, jnp.maximum(first_block - 1, 0), 1)
    before_ids = jnp.concatenate([prior_id, local_ids[:-1]])
    global_block = first_block + jnp.arange(blocks_here, dtype=jnp.int32)
    carry_on = ((local_ids == before_ids) & (global_block > 0)).astype(jnp.float32)
    conv_taps = jnp.concatenate([conv_main, conv_state], axis=1)
    kernel_len = conv_taps.shape[0]
    prev_rows = shifted(channels[tok_dev - kernel_len + 1 :], "ctx", 1)
    extended = jnp.concatenate([prev_rows, channels], axis=0)
    offset = jnp.arange(tok_dev, dtype=jnp.int32) % block_len
    row_carry = jnp.repeat(carry_on, block_len)
    conv_sum = jnp.zeros((tok_dev, channels.shape[1]), jnp.float32)
    for tap_index in range(kernel_len):
        allowed = (offset - kernel_len + 1 + tap_index >= 0) | (row_carry > 0)
        conv_sum = (
            conv_sum
            + jnp.where(
                allowed[:, None], extended[tap_index : tap_index + tok_dev].astype(jnp.float32), 0.0
            )
            * conv_taps[tap_index]
        )
    activated = jax.nn.silu(conv_sum).astype(jnp.bfloat16)
    values_all = activated[:, :inner_width]
    b_all = activated[:, inner_width : inner_width + state_width]
    c_all = activated[:, inner_width + state_width :]
    step_size = jax.nn.softplus(step_raw + step_bias)
    log_decay = -jnp.exp(decay_log) * step_size
    causal = jnp.arange(block_len)[:, None] >= jnp.arange(block_len)[None, :]
    kept = []
    decay_dev = jnp.ones((heads_dev,), jnp.float32)
    carry_dev = jnp.zeros((heads_dev, state_width, head_dim), jnp.float32)
    for block_num in range(blocks_here):
        low_row = block_num * block_len
        step_block = step_size[low_row : low_row + block_len]
        cum_decay = jnp.cumsum(log_decay[low_row : low_row + block_len], axis=0)
        b_rows = b_all[low_row : low_row + block_len]
        c_rows = c_all[low_row : low_row + block_len]
        values_in = values_all[low_row : low_row + block_len].reshape(
            block_len, heads_dev, head_dim
        )
        scores = jnp.dot(c_rows, b_rows.T, preferred_element_type=jnp.float32)
        gaps = cum_decay.T[:, :, None] - cum_decay.T[:, None, :]
        decays = jnp.exp(jnp.where(causal[None], gaps, -1e30))
        mixing = (scores[None] * decays * step_block.T[:, None, :]).astype(jnp.bfloat16)
        intra = jnp.einsum("hts,shp->thp", mixing, values_in, preferred_element_type=jnp.float32)
        weights = jnp.exp(cum_decay[-1][None, :] - cum_decay) * step_block
        weighted_b = (weights[:, :, None] * b_rows[:, None, :].astype(jnp.float32)).astype(
            jnp.bfloat16
        )
        block_state = jnp.einsum(
            "shn,shp->hnp", weighted_b, values_in, preferred_element_type=jnp.float32
        )
        block_decay = jnp.exp(cum_decay[-1]) * carry_on[block_num]
        decay_dev = block_decay * decay_dev
        carry_dev = block_decay[:, None, None] * carry_dev + block_state
        kept.append((cum_decay, intra, block_state, c_rows, values_in))

    def combine(earlier, later_one):
        return (earlier[0] * later_one[0], later_one[0][:, None, None] * earlier[1] + later_one[1])

    prefix = carried_in(
        (decay_dev, carry_dev),
        "ctx",
        combine,
        (jnp.ones_like(decay_dev), jnp.zeros_like(carry_dev)),
    )
    entering = prefix[1]
    state_now = entering
    pieces_out = []
    for block_num in range(blocks_here):
        cum_decay, intra, block_state, c_rows, values_in = kept[block_num]
        start_state = state_now * carry_on[block_num]
        start_low = start_state.astype(jnp.bfloat16)
        inter = jnp.exp(cum_decay)[:, :, None] * jnp.einsum(
            "tn,hnp->thp", c_rows, start_low, preferred_element_type=jnp.float32
        )
        combined = intra + inter + skip_gain[None, :, None] * values_in.astype(jnp.float32)
        state_now = jnp.exp(cum_decay[-1])[:, None, None] * start_state + block_state
        pieces_out.append(combined.reshape(block_len, inner_width))
    combined_all = jnp.concatenate(pieces_out, axis=0)
    gated = combined_all * jax.nn.silu(gate_in.astype(jnp.float32))
    square_sum = lax.psum(jnp.sum(gated * gated, axis=1), "head")
    inv_rms = lax.rsqrt(square_sum / (HEADS * HEAD_DIM) + 1e-05)
    normed = (gated * inv_rms[:, None] * norm_gain).astype(jnp.bfloat16)
    partial_value = jnp.dot(normed, out_proj, preferred_element_type=jnp.float32)
    mixed = lax.psum_scatter(
        partial_value.astype(jnp.bfloat16), "head", scatter_dimension=1, tiled=True
    )
    return mixed


def solution(mesh):
    return jax.shard_map(
        on_device,
        mesh=mesh,
        in_specs=(
            P("ctx", "head"),
            P("ctx", None, None),
            P(),
            P(),
            P(None, None, "head"),
            P(),
            P(None, "head"),
            P(None, "head"),
            P(),
            P("head"),
            P("head"),
            P("head"),
            P("head"),
            P("head", None),
        ),
        out_specs=P("ctx", "head"),
        check_vma=False,
    )
```

profile of v0, /device:TPU:0, one launch (start us, length us, event | category | flops | bytes accessed | tf_op | source)
XLA Modules:
  0.0 300.7 jit_solution(1855621404119942553)
XLA Ops:
  6.5 0.9 reshape_squeeze.3
  7.5 6.4 %gather_fusion = bf16[1024,640]{1,0:T(8,128)(2,1)} fusion(bf16[512,640]{1,0:T(8,128)(2,1)} %param.16, s32[1024]{0:T(1024)S(1)} %broadcast_clamp_fusion), kind=kCustom, calls=%fused_computation | custom fusion | bytes 2625536 | tf_op jit(solution)/shard_map/gather | solution.py:78
  13.9 8.4 %all-to-all-start = ((bf16[32,32,640]{2,1,0:T(8,128)(2,1)}), bf16[32,32,640]{2,1,0:T(8,128)(2,1)S(1)}, u32[]{:S(2)}, u32[]{:S(2)}) async-start(bf16[32,32,640]{2,1,0:T(8,128)(2,1)} %bitcast.92), calls=%async_computation | async-start | bytes 2621440 | tf_op jit(solution)/shard_map/all_to_all | solution.py:79
  22.9 19.3 %all-to-all-done = bf16[32,32,640]{2,1,0:T(8,128)(2,1)S(1)} async-done(((bf16[32,32,640]{2,1,0:T(8,128)(2,1)}), bf16[32,32,640]{2,1,0:T(8,128)(2,1)S(1)}, u32[]{:S(2)}, u32[]{:S(2)}) %all-to-all-start) | async-done | bytes 1310752 | tf_op jit(solution)/shard_map/all_to_all | solution.py:79
  42.2 2.7 gather_fusion.1
  45.1 12.6 %copy.74 = bf16[320,8,2,1280]{3,1,2,0:T(8,128)(2,1)} copy(bf16[320,8,2,1280]{3,2,1,0:T(2,128)(2,1)} %bitcast.89) | data formatting | bytes 26214400
  57.7 0.6 dynamic_slice.20
  58.3 0.7 broadcast_compare_fusion
  59.2 0.6 fusion.60
  59.9 18.3 %all-gather.6.cloned.1.call-done = bf16[512,2560]{1,0:T(8,128)(2,1)} async-done(((bf16[512,640]{1,0:T(8,128)(2,1)}), bf16[512,2560]{1,0:T(8,128)(2,1)}) %all-gather.6.cloned.1.call-update) | async-done | bytes 2621456 | tf_op jit(solution)/shard_map/all_gather | solution.py:81
  78.3 2.6 broadcast_multiply_fusion
  80.9 0.6 reduce-window.21
  81.9 0.6 reduce-window.30
  82.8 10.8 %convolution_convert_fusion.1 = bf16[512,2560]{1,0:T(8,128)(2,1)S(1)} fusion(bf16[512,2560]{1,0:T(8,128)(2,1)} %all-gather.6.cloned.1.call-done, bf16[2560,2560]{1,0:T(8,128)(2,1)} %bitcast.90), kind=kOutput, calls=%fused_computation.8 | convolution fusion | flops 6712197120 | bytes 18350080 | tf_op jit(solution)/shard_map/dot_general | solution.py:82
  93.7 2.6 copy-done.4
  96.3 0.8 convolution_convert_fusion.2
  97.1 1.7 collective-permute-start
  98.9 0.2 slice_reduce_fusion.2
  99.1 0.6 fusion.59
  99.7 0.7 slice_bitcast_fusion.3
  100.5 0.6 exponential_multiply_fusion.2
  101.1 0.4 maximum_maximum_fusion
  101.5 3.4 %multiply_convert_fusion.2 = bf16[512,1536]{1,0:T(8,128)(2,1)S(1)} fusion(bf16[512,256]{1,0:T(8,128)(2,1)S(1)} %convolution_convert_fusion.2, bf16[515,1536]{1,0:T(8,128)(2,1)S(1)} %maximum_maximum_fusion, f32[1536]{0:T(1024)S(1)} %get-tuple-element.71, f32[1536]{0:T(1024)S(1)} %get-tuple-element.72, f32[1536]{0:T(1024)S(1)} %get-tuple-element.73, ...), kind=kLoop, calls=%fused_computation.11 | loop fusion | flops 18087936 | bytes 7890944 | tf_op jit(solution)/shard_map/convert_element_type | solution.py:113
  105.0 0.9 slice_convert_fusion
  105.9 0.2 copy.57
  106.2 0.2 copy.63
  106.4 2.0 fusion.24
  108.5 3.0 %fusion.33 = bf16[20,128,64]{1,2,0:T(8,128)(2,1)} fusion(bf16[256,20,64]{0,2,1:T(8,128)(2,1)S(1)} %bitcast.99, f32[256,128]{1,0:T(8,128)} %get-tuple-element.88, f32[256,20]{0,1:T(8,128)} %get-tuple-element.97, f32[20,128,64]{1,2,0:T(8,128)S(1)} %fusion.24, f32[20]{0:T(128)S(1)} %get-tuple-element.103, f32[20]{0:T(128)S(1)} %exponential_multiply_fusion.2), kind=kOutput, calls=%fused_computation.53 | convolution fusion | flops 85852160 | bytes 1790112 | tf_op jit(solution)/shard_map/shn,shp->hnp/dot_general | solution.py:141
  111.6 0.6 iota_compare_fusion
  112.2 2.2 fusion.45
  114.4 24.0 %all-gather.2 = bf16[32,1,20]{2,1,0:T(2,128)(2,1)S(1)} all-gather(bf16[1,1,20]{2,1,0:T(2,128)(2,1)S(1)} %bitcast.120), channel_id=1, replica_groups=mesh['ctx'=32,'head'=4] {'ctx'}, dimensions={0}, use_global_device_ids=true | all-gather | bytes 1320 | tf_op jit(solution)/shard_map/all_gather | solution.py:20
  138.5 0.2 fusion.36
  138.7 32.2 %all-gather.8.cloned.1.call-done = bf16[640,128,64]{1,2,0:T(8,128)(2,1)} async-done(((bf16[20,128,64]{1,2,0:T(8,128)(2,1)}), bf16[640,128,64]{1,2,0:T(8,128)(2,1)}) %all-gather.8.cloned.1.call-update) | async-done | bytes 10485776 | tf_op jit(solution)/shard_map/all_gather | solution.py:20
  171.0 0.2 while.12
  171.3 0.4 copy.66
  171.7 2.6 multiply_convert_fusion.28
  174.2 1.2 fusion.41
  175.5 1.7 fusion.23
  177.2 0.4 copy.67
  177.6 1.2 fusion.34
  178.8 4.1 %fusion.22 = f32[256,20,64]{0,2,1:T(8,128)} fusion(bf16[256,20,64]{0,2,1:T(8,128)(2,1)} %bitcast.100, f32[20,256]{1,0:T(8,128)S(1)} %copy-done.16, f32[20,256]{1,0:T(8,128)S(1)} %bitcast.112, f32[256,256]{1,0:T(8,128)S(1)} %fusion.36, pred[256,256]{1,0:T(8,128)(4,1)S(1)} %copy-done.15, f32[256,20,64]{0,2,1:T(8,128)S(1)} %bitcast.95, ...), kind=kOutput, calls=%fused_computation.42 | convolution fusion | flops 175964160 | bytes 3666000 | tf_op jit(solution)/shard_map/hts,shp->thp/dot_general | solution.py:136
  182.9 1.7 copy.68
  184.6 2.2 multiply_reduce_fusion
  186.8 10.5 %psum.7 = f32[512]{0:T(512)S(1)} all-reduce(f32[512]{0:T(512)S(1)} %multiply_reduce_fusion), channel_id=1, replica_groups=mesh['ctx'=32,'head'=4] {'head'}, use_global_device_ids=true, to_apply=%region_10.11 | all-reduce | flops 512 | bytes 4096 | tf_op jit(solution)/shard_map/psum | solution.py:173
  197.3 8.9 %convolution_convert_fusion = bf16[512,2560]{1,0:T(8,128)(2,1)} fusion(bf16[1280,2560]{1,0:T(8,128)(2,1)} %param.29, f32[1280]{0:T(1024)S(1)} %copy-done.25, f32[512]{0:T(512)S(1)} %add_rsqrt_fusion, f32[256,1280]{1,0:T(8,128)S(1)} %copy.68, f32[256,1280]{1,0:T(8,128)S(1)} %copy.67, bf16[512,2560]{1,0:T(8,128)(2,1)} %copy-done.3), kind=kOutput, calls=%fused_computation.7 | convolution fusion | flops 3363307520 | bytes 13114368 | tf_op jit(solution)/shard_map/dot_general | solution.py:176
  206.2 4.5 %copy.71 = bf16[512,2560]{0,1:T(8,128)(2,1)} copy(bf16[512,2560]{1,0:T(8,128)(2,1)} %convolution_convert_fusion) | data formatting | bytes 5242880
  210.7 81.3 %reduce-scatter.4.cloned.1.call-done = bf16[640,512]{1,0:T(8,128)(2,1)} async-done(((bf16[2560,512]{1,0:T(8,128)(2,1)}), bf16[640,512]{1,0:T(8,128)(2,1)}) %reduce-scatter.4.cloned.1.call-update) | async-done | bytes 655376
  292.0 2.2 copy.72
  (107 shorter events, 2.3 us)
Async XLA Ops:
  6.5 87.2 %copy-start = (bf16[2560,256]{1,0:T(8,128)(2,1)S(1)}, bf16[2560,256]{1,0:T(8,128)(2,1)}, u32[]{:S(2)}) copy-start(bf16[2560,256]{1,0:T(8,128)(2,1)} %param.21) | copy-start | bytes 3932164
  13.9 8.4 %copy-start.21 = (s32[32,32]{1,0:T(8,128)S(1)}, s32[32,32]{1,0:T(8,128)}, u32[]{:S(2)}) copy-start(s32[32,32]{1,0:T(8,128)} %param.18) | copy-start | bytes 12292
  13.9 28.3 %all-to-all-start = ((bf16[32,32,640]{2,1,0:T(8,128)(2,1)}), bf16[32,32,640]{2,1,0:T(8,128)(2,1)S(1)}, u32[]{:S(2)}, u32[]{:S(2)}) async-start(bf16[32,32,640]{2,1,0:T(8,128)(2,1)} %bitcast.92), calls=%async_computation | async-start | bytes 2621440 | tf_op jit(solution)/shard_map/all_to_all | solution.py:79
  22.3 56.0 %all-gather.6.cloned.1.call-start = ((), (), s32[]{:S(2)}) async-start(), calls=%async_computation.2 | async-start | bytes 3276800 | tf_op jit(solution)/shard_map/all_gather | solution.py:81
  44.9 125.9 %all-gather.8.cloned.1.call-start = ((), (), s32[]{:S(2)}) async-start(), calls=%async_computation.3 | async-start | bytes 10813440 | tf_op jit(solution)/shard_map/all_gather | solution.py:20
  45.0 12.7 %copy-start.23 = (s32[64]{0:T(128)S(1)}, s32[64]{0:T(128)}, u32[]{:S(2)}) copy-start(s32[64]{0:T(128)} %param.19) | copy-start | bytes 772
  45.0 14.2 %copy-start.20 = (f32[4,1280]{1,0:T(4,128)S(1)}, f32[4,1280]{1,0:T(4,128)}, u32[]{:S(2)}) copy-start(f32[4,1280]{1,0:T(4,128)} %param.23) | copy-start | bytes 61444
  45.0 14.2 %copy-start.22 = (f32[4,256]{1,0:T(4,128)S(1)}, f32[4,256]{1,0:T(4,128)}, u32[]{:S(2)}) copy-start(f32[4,256]{1,0:T(4,128)} %param.24) | copy-start | bytes 12292
  45.0 14.9 %copy-start.26 = (f32[20]{0:T(128)S(1)}, f32[20]{0:T(128)}, u32[]{:S(2)}) copy-start(f32[20]{0:T(128)} %param.26) | copy-start | bytes 244
  45.0 33.2 %copy-start.13 = (bf16[2560,20]{0,1:T(8,128)(2,1)S(1)}, bf16[2560,20]{0,1:T(8,128)(2,1)}, u32[]{:S(2)}) copy-start(bf16[2560,20]{0,1:T(8,128)(2,1)} %param.22) | copy-start | bytes 307204
  45.1 33.2 %copy-start.24 = (f32[20]{0:T(128)S(1)}, f32[20]{0:T(128)}, u32[]{:S(2)}) copy-start(f32[20]{0:T(128)} %param.25) | copy-start | bytes 244
  81.8 17.9 %copy-start.9 = (f32[3,8,2,128]{3,1,2,0:T(8,128)}, f32[3,8,2,128]{3,1,2,0:T(8,128)S(1)}, u32[]{:S(2)}) copy-start(f32[3,8,2,128]{3,1,2,0:T(8,128)S(1)} %copy.75) | copy-start | bytes 73732
  82.8 16.9 %copy-start.11 = (f32[3,8,2,128]{3,1,2,0:T(8,128)}, f32[3,8,2,128]{3,1,2,0:T(8,128)S(1)}, u32[]{:S(2)}) copy-start(f32[3,8,2,128]{3,1,2,0:T(8,128)S(1)} %copy.76) | copy-start | bytes 73732
  93.6 3.5 %copy-start.3 = (bf16[512,2560]{1,0:T(8,128)(2,1)}, bf16[512,2560]{1,0:T(8,128)(2,1)S(1)}, u32[]{:S(2)}) copy-start(bf16[512,2560]{1,0:T(8,128)(2,1)S(1)} %convolution_convert_fusion.1) | copy-start | bytes 7864324
  93.6 2.7 copy-start.4
  97.1 3.9 %collective-permute-start = (bf16[3,1536]{1,0:T(4,128)(2,1)S(1)}, bf16[3,1536]{1,0:T(4,128)(2,1)S(1)}, u32[]{:S(2)}, u32[]{:S(2)}) collective-permute-start(bf16[3,1536]{1,0:T(4,128)(2,1)S(1)} %fusion.44), channel_id=1, source_target_pairs={{0,4},{4,8},{8,12},{12,16},{16,20},{20,24},{24,28},{28,32},{32,36}... | collective-permute-start | bytes 27656 | tf_op jit(solution)/shard_map/ppermute | solution.py:14
  104.9 33.6 %copy-start.2 = (bf16[512,1536]{1,0:T(8,128)(2,1)}, bf16[512,1536]{1,0:T(8,128)(2,1)S(1)}, u32[]{:S(2)}) copy-start(bf16[512,1536]{1,0:T(8,128)(2,1)S(1)} %multiply_convert_fusion.2) | copy-start | bytes 4718596
  106.2 5.3 %copy-start.6 = (bf16[256,1280]{0,1:T(8,128)(2,1)}, bf16[256,1280]{0,1:T(8,128)(2,1)S(1)}, u32[]{:S(2)}) copy-start(bf16[256,1280]{0,1:T(8,128)(2,1)S(1)} %copy.57) | copy-start | bytes 1966084
  106.4 64.5 %copy-start.5 = (bf16[256,1280]{0,1:T(8,128)(2,1)}, bf16[256,1280]{0,1:T(8,128)(2,1)S(1)}, u32[]{:S(2)}) copy-start(bf16[256,1280]{0,1:T(8,128)(2,1)S(1)} %copy.63) | copy-start | bytes 1966084
  108.4 62.4 %copy-start.8 = (f32[20,128,64]{1,2,0:T(8,128)}, f32[20,128,64]{1,2,0:T(8,128)S(1)}, u32[]{:S(2)}) copy-start(f32[20,128,64]{1,2,0:T(8,128)S(1)} %fusion.24) | copy-start | bytes 1966084
  111.5 180.5 %reduce-scatter.4.cloned.1.call-start = ((), (), s32[]{:S(2)}) async-start(), calls=%async_computation.4 | async-start | bytes 3276800
  171.2 4.2 %copy-start.10 = (f32[3,8,2,128]{3,1,2,0:T(8,128)S(1)}, f32[3,8,2,128]{3,1,2,0:T(8,128)}, u32[]{:S(2)}) copy-start(f32[3,8,2,128]{3,1,2,0:T(8,128)} %copy-done.9) | copy-start | bytes 73732
  171.2 4.2 %copy-start.18 = (f32[20,256]{1,0:T(8,128)S(1)}, f32[20,256]{1,0:T(8,128)}, u32[]{:S(2)}) copy-start(f32[20,256]{1,0:T(8,128)} %get-tuple-element.94) | copy-start | bytes 61444
  171.2 4.2 %copy-start.19 = (f32[256,20]{0,1:T(8,128)S(1)}, f32[256,20]{0,1:T(8,128)}, u32[]{:S(2)}) copy-start(f32[256,20]{0,1:T(8,128)} %get-tuple-element.101) | copy-start | bytes 61444
  171.2 4.2 %copy-start.27 = (f32[20]{0:T(128)S(1)}, f32[20]{0:T(128)}, u32[]{:S(2)}) copy-start(f32[20]{0:T(128)} %param.27) | copy-start | bytes 244
  171.6 3.8 %copy-start.7 = (bf16[256,1280]{0,1:T(8,128)(2,1)S(1)}, bf16[256,1280]{0,1:T(8,128)(2,1)}, u32[]{:S(2)}) copy-start(bf16[256,1280]{0,1:T(8,128)(2,1)} %copy-done.6) | copy-start | bytes 1966084
  171.7 3.8 %copy-start.14 = (pred[256,256]{1,0:T(8,128)(4,1)S(1)}, pred[256,256]{1,0:T(8,128)(4,1)}, u32[]{:S(2)}) copy-start(pred[256,256]{1,0:T(8,128)(4,1)} %iota_compare_fusion) | copy-start | bytes 196612
  177.1 1.6 copy-start.12
  177.1 1.6 copy-start.15
  177.2 1.6 copy-start.16
  177.2 1.6 copy-start.17
  184.6 12.7 %copy-start.25 = (f32[1280]{0:T(1024)S(1)}, f32[1280]{0:T(1024)}, u32[]{:S(2)}) copy-start(f32[1280]{0:T(1024)} %param.28) | copy-start | bytes 15364
  206.2 88.0 %copy-start.1 = (bf16[2560,256]{1,0:T(8,128)(2,1)S(1)}, bf16[2560,256]{1,0:T(8,128)(2,1)}, u32[]{:S(2)}) copy-start(bf16[2560,256]{1,0:T(8,128)(2,1)} %param.21) | copy-start | bytes 3932164
Sparse Core Ops, SparseCore 0:
  45.1 33.1 all-gather.5
  111.6 59.2 all-gather.7
  210.8 81.1 reduce-scatter.3
where the time goes:
time: 304 us; the launch traced here: 301 us
  waiting for transfers between devices  151 us (50%)
  local copies, waits for them, and re-layouts  37.5 us (12%)
  matrix products  36.6 us (12%)
  blocking collectives  34.4 us (11%)
  other arithmetic  16.8 us (6%)
  between operations  13.8 us (5%)
  starting transfers between devices  10.2 us (3%)
    unnamed x4, waiting for transfers between devices  81.3 us
    all_gather x1, waiting for transfers between devices, carried_in(): lax.all_gather(a.astype(kind), axis)  32.2 us
    all_gather x1, blocking collectives, carried_in(): lax.all_gather(a.astype(kind), axis)  24 us
    unnamed x64, local copies, waits for them, and re-layouts  22 us
    all_to_all x1, waiting for transfers between devices, on_device(): lax.all_to_all(outgoing, 'ctx', split_axis=0, concat_axis=0, tiled=True)  19.3 us
    all_gather x1, waiting for transfers between devices, on_device(): piece_cols = lax.all_gather(packed, 'head', axis=1, tiled=True)  18.3 us
    dot_general x1, matrix products, on_device(): gate_up = jnp.dot(piece_cols, main_flat, preferred_element_type=jnp.float32)  10.8 us
    psum x1, blocking collectives, on_device(): square_sum = lax.psum(jnp.sum(gated * gated, axis=1), 'head')  10.5 us
  transfers between devices with their start and end apart: 5, of which 4 were waited for; matrix products, arithmetic and copies ran while one was open for 7% of the time, Pallas kernels for 0%

commit v1 on v0

v1 whole, which is shorter than its diff:
```python
import jax
import jax.numpy as jnp
from jax import lax
from jax.experimental import pallas as pl
from jax.experimental.pallas import tpu as pltpu
from jax.sharding import PartitionSpec as P

BF = jnp.bfloat16
F32 = jnp.float32
STRETCH = 256
TAIL = 16
TILE = 256
LOG2E = 1.4426950408889634
RING = 4
VMEM = 50 * 1024 * 1024


def dot(a, b):
    return jnp.dot(a, b, preferred_element_type=F32)


def turned(value, steps):
    return lax.ppermute(value, "head", [(i, (i + steps) % RING) for i in range(RING)])


def shifted(value, steps):
    count = lax.axis_size("ctx")
    return lax.ppermute(value, "ctx", [(i, i + steps) for i in range(count - steps)])


def silu(v):
    return v * (1.0 / (1.0 + jnp.exp(-v)))


def split3(x):
    high = x.astype(BF).astype(F32)
    rest = x - high
    mid = rest.astype(BF).astype(F32)
    low = (rest - mid).astype(BF).astype(F32)
    return high, mid, low


def pack3(x):
    high, mid, low = split3(x)
    return (high + pltpu.roll(mid, 32, 1) + pltpu.roll(low, 64, 1)).astype(BF)


def spread(tile, width):
    lane = lax.broadcasted_iota(jnp.int32, (128, width), 0)
    col = lax.broadcasted_iota(jnp.int32, (128, width), 1)
    hit = ((lane & 31) == tile * (width // 64) + (col >> 6)) & (lane < 96)
    return jnp.where(hit, 1.0, 0.0).astype(BF)


def params(n=1):
    return pltpu.CompilerParams(
        dimension_semantics=("arbitrary",) * n, vmem_limit_bytes=VMEM
    )


def cost(flops, bytes_accessed, exps=0):
    return pl.CostEstimate(
        flops=int(flops), bytes_accessed=int(bytes_accessed), transcendentals=int(exps)
    )


def whole(shape):
    return pl.BlockSpec(shape, lambda i, ids: (0,) * len(shape))


def tile_of(i):
    return jnp.maximum(i - 1, 0)


def own_body(ids, x, wsd, wv, osd, ov):
    i = pl.program_id(0)

    @pl.when(i == 0)
    def _():
        osd[...] = dot(x[...], wsd[...])

    @pl.when(i > 0)
    def _():
        ov[...] = dot(x[...], wv[...])


def own_part(ids, x, wsd, wv):
    rows, k = x.shape
    nsd, nv = wsd.shape[1], wv.shape[1] // 2
    past = nv // TILE
    return pl.pallas_call(
        own_body,
        grid_spec=pltpu.PrefetchScalarGridSpec(
            num_scalar_prefetch=1,
            grid=(1 + nv // TILE,),
            in_specs=[
                whole((rows, k)),
                pl.BlockSpec((k, nsd), lambda i, ids: (ids[0], 0)),
                pl.BlockSpec((k, TILE), lambda i, ids: (ids[0], past + tile_of(i))),
            ],
            out_specs=[
                whole((rows, nsd)),
                pl.BlockSpec((rows, TILE), lambda i, ids: (0, tile_of(i))),
            ],
        ),
        out_shape=[
            jax.ShapeDtypeStruct((rows, nsd), F32),
            jax.ShapeDtypeStruct((rows, nv), F32),
        ],
        compiler_params=params(),
        cost_estimate=cost(2 * rows * k * (nsd + nv), 2 * k * (nsd + nv) + 4 * rows * (nsd + nv)),
        name="own_part",
    )(ids, x, wsd, wv)


def next_body(ids, x1, x2, wsd1, wsd2, wv1, wv2, asd, av, osd, ov):
    i = pl.program_id(0)

    @pl.when(i == 0)
    def _():
        osd[...] = asd[...] + dot(x1[...], wsd1[...]) + dot(x2[...], wsd2[...])

    @pl.when(i > 0)
    def _():
        ov[...] = av[...] + dot(x1[...], wv1[...]) + dot(x2[...], wv2[...])


def next_part(ids, x1, x2, wsd, wv, asd, av):
    rows, k = x1.shape
    nsd, nv = wsd.shape[1], wv.shape[1] // 2
    past = nv // TILE
    acc = pl.BlockSpec((rows, TILE), lambda i, ids: (0, tile_of(i)))
    return pl.pallas_call(
        next_body,
        grid_spec=pltpu.PrefetchScalarGridSpec(
            num_scalar_prefetch=1,
            grid=(1 + nv // TILE,),
            in_specs=[
                whole((rows, k)),
                whole((rows, k)),
                pl.BlockSpec((k, nsd), lambda i, ids: (ids[1], 0)),
                pl.BlockSpec((k, nsd), lambda i, ids: (ids[2], 0)),
                pl.BlockSpec((k, TILE), lambda i, ids: (ids[1], past + tile_of(i))),
                pl.BlockSpec((k, TILE), lambda i, ids: (ids[2], past + tile_of(i))),
                whole((rows, nsd)),
                acc,
            ],
            out_specs=[whole((rows, nsd)), acc],
        ),
        out_shape=[
            jax.ShapeDtypeStruct((rows, nsd), F32),
            jax.ShapeDtypeStruct((rows, nv), F32),
        ],
        compiler_params=params(),
        cost_estimate=cost(4 * rows * k * (nsd + nv), 4 * k * (nsd + nv) + 8 * rows * (nsd + nv)),
        name="next_part",
    )(ids, x1, x2, wsd, wsd, wv, wv, asd, av)


def conv_block(xs, taps, block, width):
    low = TAIL + block * STRETCH
    total = None
    for k in range(4):
        start = low - 3 + k
        term = xs[start : start + STRETCH, :width] * taps[k : k + 1, :]
        total = term if total is None else total + term
    return silu(total).astype(BF)


def convolved(ids, xs, taps, width, put):
    @pl.when(ids[4] == 0)
    def _():
        xs[TAIL - 8 : TAIL, :] = jnp.zeros((8, xs.shape[1]), F32)

    put(0, conv_block(xs, taps, 0, width))

    @pl.when(ids[5] == 0)
    def _():
        xs[TAIL + STRETCH - 8 : TAIL + STRETCH, :] = jnp.zeros((8, xs.shape[1]), F32)

    put(1, conv_block(xs, taps, 1, width))


def state_body(
    ids, x1, x2, wsd, wv, asd, av, taps_s, taps_v, heads,
    act, bc, cum3, cum_t, step_t, ecum3, state0, state_dev, rows_out, payload,
    xs, bt, w3, last3,
):
    i = pl.program_id(0)
    n1 = x1.shape[0]

    @pl.when(i == 0)
    def _():
        first = asd[:n1, :] + dot(x1[...], wsd[...])
        second = asd[n1:, :] + dot(x2[...], wsd[...])
        xs[:n1, :] = first[:, :256].astype(BF).astype(F32)
        xs[n1:, :] = second[:, :256].astype(BF).astype(F32)

        def put(block, value):
            bc[block * STRETCH : (block + 1) * STRETCH, :] = value
            bt[block] = jnp.transpose(value[:, :128].astype(F32)).astype(BF)

        convolved(ids, xs, taps_s, 256, put)
        raws = (first[TAIL:, 256:], second[:, 256:])
        lane = lax.broadcasted_iota(jnp.int32, (STRETCH, 128), 1)
        row_id = lax.broadcasted_iota(jnp.int32, (STRETCH, STRETCH), 0)
        col_id = lax.broadcasted_iota(jnp.int32, (STRETCH, STRETCH), 1)
        below = jnp.where(row_id >= col_id, 1.0, 0.0).astype(BF)
        lasts = []
        for block in range(2):
            rows = slice(block * STRETCH, (block + 1) * STRETCH)
            raw = raws[block] + heads[0:1, :]
            small = jnp.exp(-jnp.abs(raw))
            one = 1.0 + small
            log_one = jnp.where(one == 1.0, small, jnp.log(one) * (small / (one - 1.0 + 1e-30)))
            step = jnp.where(lane < 32, jnp.maximum(raw, 0.0) + log_one, 0.0)
            decay = pack3(step * (heads[1:2, :] * (-LOG2E)))
            sums = dot(below, decay)
            sums = sums + pltpu.roll(sums, 96, 1) + pltpu.roll(sums, 64, 1)
            sums = jnp.where(lane < 32, sums, 0.0)
            final = sums[STRETCH - 1 : STRETCH, :]
            cum3[rows, :] = pack3(sums)
            cum_t[block] = jnp.transpose(sums)[:32]
            step_t[block] = jnp.transpose(step)[:32]
            keep = jnp.where(lane < 32, jnp.exp2(sums), 0.0)
            ecum3[rows, :] = pack3(keep)
            w3[rows, :] = pack3(jnp.exp2(final - sums) * step)
            lasts.append(jnp.where(lane[:1] < 32, jnp.exp2(final), 0.0))
        pad_row = lax.broadcasted_iota(jnp.int32, (16, 128), 0)
        last3[...] = pack3(
            jnp.where(pad_row == 0, lasts[0], jnp.where(pad_row == 1, lasts[1], 0.0))
        )

    @pl.when(i > 0)
    def _():
        xs[:n1, :] = (av[:n1, :] + dot(x1[...], wv[...])).astype(BF).astype(F32)
        xs[n1:, :] = (av[n1:, :] + dot(x2[...], wv[...])).astype(BF).astype(F32)
        select = spread(i - 1, TILE)
        states = []

        def put(block, value):
            rows = slice(block * STRETCH, (block + 1) * STRETCH)
            act[rows, :] = value
            weighted = (value.astype(F32) * dot(w3[rows, :], select)).astype(BF)
            states.append(dot(bt[block], weighted))

        convolved(ids, xs, taps_v, TILE, put)
        ends = dot(last3[...], select)
        carry0 = jnp.where(ids[4] > 0, 1.0, 0.0)
        carry1 = jnp.where(ids[5] > 0, 1.0, 0.0)
        end0, end1 = ends[0:1, :], ends[1:2, :] * carry1
        whole_decay = end0 * carry0 * end1
        device = states[1] + end1 * states[0]
        state0[...] = states[0]
        state_dev[...] = device
        row = lax.broadcasted_iota(jnp.int32, (16, TILE), 0)
        rows_out[...] = jnp.where(row[:8] == 0, end0, jnp.where(row[:8] == 1, whole_decay, 0.0))
        high, mid, low = split3(whole_decay)
        payload[:128, :] = device.astype(BF)
        payload[128:, :] = jnp.where(
            row == 0, high, jnp.where(row == 1, mid, jnp.where(row == 2, low, 0.0))
        ).astype(BF)


def state_part(ids, x1, x2, wsd, wv, asd, av, taps_s, taps_v, heads):
    k = x1.shape[1]
    n1, n2 = x1.shape[0], x2.shape[0]
    rows = n1 + n2
    tok = rows - TAIL
    nsd, nv = wsd.shape[1], wv.shape[1] // 2
    past = nv // TILE

    def tiled(height):
        return pl.BlockSpec((height, TILE), lambda i, ids: (0, tile_of(i)))

    return pl.pallas_call(
        state_body,
        grid_spec=pltpu.PrefetchScalarGridSpec(
            num_scalar_prefetch=1,
            grid=(1 + nv // TILE,),
            in_specs=[
                whole((n1, k)),
                whole((n2, k)),
                pl.BlockSpec((k, nsd), lambda i, ids: (ids[3], 0)),
                pl.BlockSpec((k, TILE), lambda i, ids: (ids[3], past + tile_of(i))),
                whole((rows, nsd)),
                tiled(rows),
                whole((4, 256)),
                tiled(4),
                whole((8, 128)),
            ],
            out_specs=[
                tiled(tok),
                whole((tok, 256)),
                whole((tok, 128)),
                whole((2, 32, STRETCH)),
                whole((2, 32, STRETCH)),
                whole((tok, 128)),
                tiled(128),
                tiled(128),
                tiled(8),
                tiled(144),
            ],
            scratch_shapes=[
                pltpu.VMEM((rows, TILE), F32),
                pltpu.VMEM((2, 128, STRETCH), BF),
                pltpu.VMEM((tok, 128), BF),
                pltpu.VMEM((16, 128), BF),
            ],
        ),
        out_shape=[
            jax.ShapeDtypeStruct((tok, nv), BF),
            jax.ShapeDtypeStruct((tok, 256), BF),
            jax.ShapeDtypeStruct((tok, 128), BF),
            jax.ShapeDtypeStruct((2, 32, STRETCH), F32),
            jax.ShapeDtypeStruct((2, 32, STRETCH), F32),
            jax.ShapeDtypeStruct((tok, 128), BF),
            jax.ShapeDtypeStruct((128, nv), F32),
            jax.ShapeDtypeStruct((128, nv), F32),
            jax.ShapeDtypeStruct((8, nv), F32),
            jax.ShapeDtypeStruct((144, nv), BF),
        ],
        compiler_params=params(),
        cost_estimate=cost(2 * rows * k * (nsd + nv), 2 * k * (nsd + nv) + 8 * rows * (nsd + nv)),
        name="state_part",
    )(ids, x1, x2, wsd, wv, asd, av, taps_s, taps_v, heads)


def join_body(state, row, got, out):
    out[...] = (state[...] + row[1:2, :] * got[:128, :].astype(F32)).astype(BF)


def join_part(state, row, got):
    return pl.pallas_call(
        join_body,
        out_shape=jax.ShapeDtypeStruct(state.shape, BF),
        compiler_params=pltpu.CompilerParams(vmem_limit_bytes=VMEM),
        cost_estimate=cost(2 * state.size, 8 * state.size),
        name="join_part",
    )(state, row, got)


def mix_body(ids, x, r, l, o1, o2, wg, act, bc, cum3, cum_t, step_t, ecum3, skip, p_out, q_out, sc):
    i = pl.program_id(0)
    k = x.shape[1]

    @pl.when(i == 0)
    def _():
        row_id = lax.broadcasted_iota(jnp.int32, (STRETCH, STRETCH), 0)
        col_id = lax.broadcasted_iota(jnp.int32, (STRETCH, STRETCH), 1)
        for block in range(2):
            rows = slice(block * STRETCH, (block + 1) * STRETCH)
            scores = lax.dot_general(
                bc[rows, 128:], bc[rows, :128], (((1,), (1,)), ((), ())), preferred_element_type=F32
            )
            sc[block] = jnp.where(row_id >= col_id, scores, 0.0)

    def weights(at):
        return wg[pl.ds(pl.multiple_of(ids[at] * k, 128), k), :]

    select = spread(i, TILE)
    lane = lax.broadcasted_iota(jnp.int32, (128, STRETCH), 0)
    group = lax.broadcasted_iota(jnp.int32, (STRETCH, TILE), 1) >> 6
    half = STRETCH // 2
    for block in range(2):
        rows = slice(block * STRETCH, (block + 1) * STRETCH)
        here = slice(TAIL + block * STRETCH, TAIL + (block + 1) * STRETCH)
        other = o1[TAIL:, :] if block == 0 else o2[...]
        gate = (
            dot(x[here, :], weights(0))
            + dot(r[here, :], weights(1))
            + dot(l[here, :], weights(2))
            + dot(other, weights(3))
        )
        gate = silu(gate.astype(BF).astype(F32))
        values = act[rows, :]
        top = jnp.zeros((half, TILE), F32)
        bottom = jnp.zeros((half, TILE), F32)
        for j in range(TILE // 64):
            h = i * (TILE // 64) + j
            pick = jnp.where(((lane & 31) == h) & (lane < 96), 1.0, 0.0).astype(BF)
            cum = dot(cum3[rows, :], pick)
            cum_s = cum_t[block, pl.ds(h, 1), :]
            step_s = step_t[block, pl.ds(h, 1), :]
            mine = jnp.where(group == j, values, jnp.zeros_like(values))
            m_top = (
                sc[block, :half, :half]
                * jnp.exp2(jnp.minimum(cum[:half, :half] - cum_s[:, :half], 0.0))
                * step_s[:, :half]
            ).astype(BF)
            m_bottom = (
                sc[block, half:, :]
                * jnp.exp2(jnp.minimum(cum[half:, :] - cum_s, 0.0))
                * step_s
            ).astype(BF)
            top = top + dot(m_top, mine[:half, :])
            bottom = bottom + dot(m_bottom, mine)
        within = jnp.concatenate([top, bottom], axis=0)
        p_out[rows, :] = (within + skip[0:1, :] * values.astype(F32)) * gate
        q_out[rows, :] = dot(ecum3[rows, :], select) * gate


def mix_part(ids, x, r, l, o1, o2, wg, act, bc, cum3, cum_t, step_t, ecum3, skip):
    tok, nv = act.shape

    def tiled(height):
        return pl.BlockSpec((height, TILE), lambda i, ids: (0, i))

    return pl.pallas_call(
        mix_body,
        grid_spec=pltpu.PrefetchScalarGridSpec(
            num_scalar_prefetch=1,
            grid=(nv // TILE,),
            in_specs=[
                whole(x.shape),
                whole(r.shape),
                whole(l.shape),
                whole(o1.shape),
                whole(o2.shape),
                tiled(wg.shape[0]),
                tiled(tok),
                whole(bc.shape),
                whole(cum3.shape),
                whole(cum_t.shape),
                whole(step_t.shape),
                whole(ecum3.shape),
                tiled(8),
            ],
            out_specs=[tiled(tok), tiled(tok)],
            scratch_shapes=[pltpu.VMEM((2, STRETCH, STRETCH), F32)],
        ),
        out_shape=[jax.ShapeDtypeStruct((tok, nv), F32)] * 2,
        compiler_params=params(),
        cost_estimate=cost(tok * wg.size, wg.size + 10 * tok * nv, 20 * tok * 256),
        name="mix_part",
    )(ids, x, r, l, o1, o2, wg, act, bc, cum3, cum_t, step_t, ecum3, skip)


def gated_body(ids, p, q, bc, got1, got2, state0, rows_in, gain, wo, z, far, squares, acc, sq):
    i = pl.program_id(0)
    carry0 = jnp.where(ids[4] > 0, 1.0, 0.0)
    carry1 = jnp.where(ids[5] > 0, 1.0, 0.0)
    tail = got1[128:, :].astype(F32)
    decay = tail[0:1, :] + tail[1:2, :] + tail[2:3, :]
    entering = got1[:128, :].astype(F32) + decay * got2[...].astype(F32)
    start0 = entering * carry0
    start1 = (rows_in[0:1, :] * start0 + state0[...]) * carry1
    sums = []
    for block, start in ((0, start0), (1, start1)):
        rows = slice(block * STRETCH, (block + 1) * STRETCH)
        from_start = dot(bc[rows, 128:], start.astype(BF))
        gated = p[rows, :] + q[rows, :] * from_start
        square = gated * gated
        sums.append(square[:, :128] + square[:, 128:])
        z[rows, :] = (gated * gain[0:1, :]).astype(BF)
    part = dot(z[...], wo[...])
    square = jnp.concatenate(sums, axis=0)

    @pl.when(i == 0)
    def _():
        acc[...] = part
        sq[...] = square

    @pl.when(i > 0)
    def _():
        acc[...] += part
        sq[...] += square

    @pl.when(i == pl.num_programs(0) - 1)
    def _():
        far[...] = acc[...].astype(BF)
        flat = jnp.sum(jnp.transpose(sq[...]), axis=0, keepdims=True)
        squares[...] = jnp.broadcast_to(flat, squares.shape)


def gated_part(ids, p, q, bc, got1, got2, state0, rows_in, gain, wo):
    tok, nv = p.shape
    ncol = wo.shape[1] // RING

    def tiled(height):
        return pl.BlockSpec((height, TILE), lambda i, ids: (0, i))

    return pl.pallas_call(
        gated_body,
        grid_spec=pltpu.PrefetchScalarGridSpec(
            num_scalar_prefetch=1,
            grid=(nv // TILE,),
            in_specs=[
                tiled(tok),
                tiled(tok),
                whole(bc.shape),
                tiled(144),
                tiled(128),
                tiled(128),
                tiled(8),
                tiled(8),
                pl.BlockSpec((TILE, ncol), lambda i, ids: (i, ids[3])),
            ],
            out_specs=[tiled(tok), whole((tok, ncol)), whole((8, tok))],
            scratch_shapes=[pltpu.VMEM((tok, ncol), F32), pltpu.VMEM((tok, 128), F32)],
        ),
        out_shape=[
            jax.ShapeDtypeStruct((tok, nv), BF),
            jax.ShapeDtypeStruct((tok, ncol), BF),
            jax.ShapeDtypeStruct((8, tok), F32),
        ],
        compiler_params=params(),
        cost_estimate=cost(2 * tok * nv * (ncol + 128), 10 * tok * nv + 2 * nv * ncol),
        name="gated_part",
    )(ids, p, q, bc, got1, got2, state0, rows_in, gain, wo)


def near_body(ids, z, wo, out):
    out[0] = dot(z[...], wo[...]).astype(BF)


def near_part(ids, z, wo, ats, name):
    tok, nv = z.shape
    ncol = wo.shape[1] // RING
    first = ats[0]
    step = ats[1] - ats[0] if len(ats) > 1 else 0
    return pl.pallas_call(
        near_body,
        grid_spec=pltpu.PrefetchScalarGridSpec(
            num_scalar_prefetch=1,
            grid=(len(ats),),
            in_specs=[
                whole((tok, nv)),
                pl.BlockSpec((nv, ncol), lambda i, ids: (0, ids[first + step * i])),
            ],
            out_specs=pl.BlockSpec((1, tok, ncol), lambda i, ids: (i, 0, 0)),
        ),
        out_shape=jax.ShapeDtypeStruct((len(ats), tok, ncol), BF),
        compiler_params=params(),
        cost_estimate=cost(2 * tok * nv * ncol * len(ats), 2 * nv * ncol * len(ats) + 4 * tok * nv),
        name=name,
    )(ids, z, wo)


def add_body(a1, b1, a2, b2, o1, o2):
    o1[...] = (a1[...].astype(F32) + b1[...].astype(F32)).astype(BF)
    o2[...] = (a2[...].astype(F32) + b2[...].astype(F32)).astype(BF)


def add_part(a1, b1, a2, b2):
    shape = jax.ShapeDtypeStruct(a1.shape, BF)
    return pl.pallas_call(
        add_body,
        out_shape=[shape, shape],
        compiler_params=pltpu.CompilerParams(vmem_limit_bytes=VMEM),
        cost_estimate=cost(2 * a1.size, 12 * a1.size),
        name="add_part",
    )(a1, b1, a2, b2)


def final_body(own, top_r, low_r, top_l, low_l, s0, s1, s2, s3, out):
    total = s0[...] + s1[...] + s2[...] + s3[...]
    inv = lax.rsqrt(total * (1.0 / 5120.0) + 1e-05)
    inv = jnp.transpose(jnp.broadcast_to(inv[0:1, :], (128, inv.shape[1])))
    half = STRETCH
    for low, r, l in ((0, top_r, top_l), (half, low_r, low_l)):
        value = (
            own[0, low : low + half, :].astype(F32) + r[...].astype(F32) + l[...].astype(F32)
        )
        scale = inv[low : low + half, :]
        for c in range(0, value.shape[1], 128):
            out[low : low + half, c : c + 128] = (value[:, c : c + 128] * scale).astype(BF)


def final_part(own, top_r, low_r, top_l, low_l, squares):
    shape = own.shape[1:]
    return pl.pallas_call(
        final_body,
        out_shape=jax.ShapeDtypeStruct(shape, BF),
        compiler_params=pltpu.CompilerParams(vmem_limit_bytes=VMEM),
        cost_estimate=cost(4 * own.size, 8 * own.size),
        name="final_part",
    )(own, top_r, low_r, top_l, low_l, *squares)


def on_device(
    tokens,
    send_rows,
    send_counts,
    stretch_segments,
    main_proj,
    state_proj,
    step_proj,
    conv_main,
    conv_state,
    step_bias,
    decay_log,
    skip_gain,
    norm_gain,
    out_proj,
):
    ctx = lax.axis_index("ctx").astype(jnp.int32)
    head = lax.axis_index("head").astype(jnp.int32)
    tok, width = tokens.shape
    sources, slots = send_rows.shape[1:]
    heads = step_bias.shape[0]
    inner = main_proj.shape[2]
    head_dim = inner // heads

    send_list = send_rows.reshape(sources * slots)
    pick = (send_list[:, None] == jnp.arange(tok, dtype=jnp.int32)[None, :]).astype(BF)
    outgoing = dot(pick, tokens).astype(BF).reshape(sources, slots, width)
    arrived = lax.all_to_all(outgoing, "ctx", split_axis=0, concat_axis=0, tiled=True)

    blocks = tok // STRETCH
    block_ids = ctx * blocks + jnp.arange(blocks, dtype=jnp.int32)
    segment = jnp.take(stretch_segments, block_ids)
    before = jnp.take(stretch_segments, jnp.maximum(block_ids - 1, 0))
    carry = ((segment == before) & (block_ids > 0)).astype(jnp.int32)
    ring = jnp.stack([head, head + 3, head + 1, head + 2]) % RING
    ids = jnp.concatenate([ring, carry]).astype(jnp.int32)
    wm = main_proj.reshape(main_proj.shape[0], 2 * inner)
    wsd = jnp.concatenate(
        [state_proj, jnp.pad(step_proj, ((0, 0), (0, 128 - heads)))], axis=1
    )
    head_rows = jnp.zeros((8, 128), F32)
    head_rows = head_rows.at[0, :heads].set(step_bias).at[1, :heads].set(jnp.exp(decay_log))
    skip = jnp.broadcast_to(jnp.repeat(skip_gain, head_dim)[None, :], (8, inner))
    gain = jnp.broadcast_to(norm_gain[None, :], (8, inner))

    column = jnp.take(send_counts, ctx, axis=1)
    ends = jnp.cumsum(column)
    begins = ends - column
    position = jnp.arange(tok, dtype=jnp.int32)
    slot = position[:, None] - begins[None, :]
    inside = (slot >= 0) & (slot < column[None, :])
    flat = jnp.sum(
        jnp.where(inside, slot + jnp.arange(sources, dtype=jnp.int32)[None, :] * slots, 0), axis=1
    )
    place = (flat[:, None] == jnp.arange(sources * slots, dtype=jnp.int32)[None, :]).astype(BF)
    arrived, wm, wsd, place = lax.optimization_barrier((arrived, wm, wsd, place))
    packed = dot(place, arrived.reshape(sources * slots, width)).astype(BF)
    tail = shifted(packed[tok - TAIL :], 1)
    x = jnp.concatenate([tail, packed], axis=0)

    cut = TAIL + STRETCH
    r = turned(x, 1)
    l = turned(x, -1)
    acc_sd, acc_v = own_part(ids, x, wsd, wm)
    r, l, acc_sd, acc_v = lax.optimization_barrier((r, l, acc_sd, acc_v))
    o1 = turned(r[:cut], 1)
    o2 = turned(l[cut:], -1)
    acc_sd, acc_v = next_part(ids, r, l, wsd, wm, acc_sd, acc_v)
    o1, o2, acc_sd, acc_v = lax.optimization_barrier((o1, o2, acc_sd, acc_v))
    act, bc, cum3, cum_t, step_t, ecum3, state0, state_dev, rows_out, payload = state_part(
        ids, o1, o2, wsd, wm, acc_sd, acc_v, conv_state, conv_main, head_rows
    )

    got1 = shifted(payload, 1)
    joined = join_part(state_dev, rows_out, got1)
    got2 = shifted(joined, 2)
    p, q = mix_part(ids, x, r, l, o1, o2, wm, act, bc, cum3, cum_t, step_t, ecum3, skip)

    z, far, squares = gated_part(
        ids, p, q, bc, got1, got2, state0, rows_out, gain, out_proj
    )
    half = STRETCH
    far_r = turned(far[:half], 1)
    far_l = turned(far[half:], -1)
    near = near_part(ids, z, out_proj, (1, 2), "near_part")
    low_r = turned(near[1, half:], 1)
    top_l = turned(near[0, :half], -1)
    sq_r = turned(squares, 1)
    sq_l = turned(squares, -1)
    sq_o = turned(squares, 2)
    own = near_part(ids, z, out_proj, (0,), "mine_part")
    sum_r, sum_l = add_part(near[1, :half], far_r, near[0, half:], far_l)
    top_r = turned(sum_r, 1)
    low_l = turned(sum_l, -1)
    return final_part(own, top_r, low_r, top_l, low_l, (squares, sq_r, sq_l, sq_o))


def solution(mesh):
    return jax.shard_map(
        on_device,
        mesh=mesh,
        in_specs=(
            P("ctx", "head"),
            P("ctx", None, None),
            P(),
            P(),
            P(None, None, "head"),
            P(),
            P(None, "head"),
            P(None, "head"),
            P(),
            P("head"),
            P("head"),
            P("head"),
            P("head"),
            P("head", None),
        ),
        out_specs=P("ctx", "head"),
        check_vma=False,
    )
```

time: 304 us -> 161 us (0.53)
  waiting for transfers between devices: 151 us -> 28.4 us
  Pallas kernels: 0 us -> 59.8 us
  blocking collectives: 34.4 us -> 0 us
  matrix products: 36.6 us -> 4.79 us
  starting transfers between devices: 10.2 us -> 37.7 us
  between operations: 13.8 us -> 0.29 us
  other arithmetic: 16.8 us -> 3.48 us
  local copies, waits for them, and re-layouts: 37.5 us -> 25.2 us
    unnamed x4 -> x0, waiting for transfers between devices: 81.3 us -> none
    pallas_call x0 -> x10, Pallas kernels: none -> 59.8 us  [the longest x1 15.6 us: mix_part(): pl.pallas_call(mix_body, grid_spec=pltpu.PrefetchScalarGridSpec(num_scala...]
    all_gather x2 -> x0, waiting for transfers between devices: 50.5 us -> none  [the longest x1 32.2 us: carried_in(): lax.all_gather(a.astype(kind), axis)]
    dot_general x10 -> x2, matrix products: 34.2 us -> 4.79 us  [dot(): return jnp.dot(a, b, preferred_element_type=F32)]
    ppermute x1 -> x16, starting transfers between devices: 1.74 us -> 29.2 us  [the longest x13 15.9 us: turned(): lax.ppermute(value, 'head', [(i, (i + steps) % RING) for i in range(RING)])]
    ppermute x1 -> x16, waiting for transfers between devices: 0.01 us -> 24.6 us  [the longest x13 22.5 us: turned(): lax.ppermute(value, 'head', [(i, (i + steps) % RING) for i in range(RING)])]
    all_gather x1 -> x0, blocking collectives: 24 us -> none  [carried_in(): lax.all_gather(a.astype(kind), axis)]
    all_to_all x1, waiting for transfers between devices: 19.3 us -> 3.8 us  [on_device(): lax.all_to_all(outgoing, 'ctx', split_axis=0, concat_axis=0, tiled=True)]
  transfers between devices with their start and end apart: 5 -> 17, of which waited for: 4 -> 8; matrix products, arithmetic and copies ran while one was open for 7% -> 14% of each run, Pallas kernels for 0% -> 24%
where the time goes in v1:
time: 161 us; the launch traced here: 160 us
  Pallas kernels  59.8 us (37%)
  starting transfers between devices  37.7 us (23%)
  waiting for transfers between devices  28.4 us (18%)
  local copies, waits for them, and re-layouts  25.2 us (16%)
  matrix products  4.79 us (3%)
  other arithmetic  3.48 us (2%)
    ppermute x13, waiting for transfers between devices, turned(): lax.ppermute(value, 'head', [(i, (i + steps) % RING) for i in range(RING)])  22.5 us
    unnamed x46, local copies, waits for them, and re-layouts  18.3 us
    ppermute x13, starting transfers between devices, turned(): lax.ppermute(value, 'head', [(i, (i + steps) % RING) for i in range(RING)])  15.9 us
    pallas_call x1, Pallas kernels, mix_part(): pl.pallas_call(mix_body, grid_spec=pltpu.PrefetchScalarGridSpec(num_scala...  15.6 us
    ppermute x3, starting transfers between devices, shifted(): lax.ppermute(value, 'ctx', [(i, i + steps) for i in range(count - steps)])  13.3 us
    pallas_call x1, Pallas kernels, state_part(): pl.pallas_call(state_body, grid_spec=pltpu.PrefetchScalarGridSpec(num_sca...  12 us
    pallas_call x1, Pallas kernels, next_part(): pl.pallas_call(next_body, grid_spec=pltpu.PrefetchScalarGridSpec(num_scal...  9.14 us
    all_to_all x1, starting transfers between devices, on_device(): lax.all_to_all(outgoing, 'ctx', split_axis=0, concat_axis=0, tiled=True)  8.49 us
  transfers between devices with their start and end apart: 17, of which 8 were waited for; matrix products, arithmetic and copies ran while one was open for 14% of the time, Pallas kernels for 24%

profile of v1, /device:TPU:0, one launch (start us, length us, event | category | flops | bytes accessed | tf_op | source)
XLA Modules:
  0.0 159.7 jit_solution(17737382414021078079)
XLA Ops:
  0.0 0.9 eq.34
  1.1 2.2 %fusion.4 = bf16[1024,640]{1,0:T(8,128)(2,1)} fusion(bf16[512,640]{1,0:T(8,128)(2,1)S(1)} %copy-done, s32[1024]{0:T(1024)S(1)} %eq.34), kind=kOutput, calls=%fused_computation.9 | convolution fusion | flops 672268288 | bytes 1970176 | tf_op jit(solution)/shard_map/dot_general | solution.py:19
  3.3 8.5 %all-to-all-start = ((bf16[32,32,640]{2,1,0:T(8,128)(2,1)}), bf16[32,32,640]{2,1,0:T(8,128)(2,1)}, u32[]{:S(2)}, u32[]{:S(2)}) async-start(bf16[32,32,640]{2,1,0:T(8,128)(2,1)} %bitcast.4), calls=%async_computation | async-start | bytes 2621440 | tf_op jit(solution)/shard_map/all_to_all | solution.py:608
  12.2 12.5 %copy.18 = bf16[320,8,2,1280]{3,1,2,0:T(8,128)(2,1)} copy(bf16[320,8,2,1280]{3,2,1,0:T(2,128)(2,1)} %bitcast.27) | data formatting | bytes 26214400
  24.6 0.4 copy.17
  25.1 1.2 fusion.2
  26.3 1.6 fusion.3.wsd.wsd1.wsd2
  27.9 3.8 %all-to-all-done = bf16[32,32,640]{2,1,0:T(8,128)(2,1)} async-done(((bf16[32,32,640]{2,1,0:T(8,128)(2,1)}), bf16[32,32,640]{2,1,0:T(8,128)(2,1)}, u32[]{:S(2)}, u32[]{:S(2)}) %all-to-all-start) | async-done | bytes 1310752 | tf_op jit(solution)/shard_map/all_to_all | solution.py:608
  31.7 2.6 %convolution_convert_fusion = bf16[512,640]{1,0:T(8,128)(2,1)S(1)} fusion(bf16[512,1024]{1,0:T(8,128)(2,1)} %fusion.2, bf16[1024,640]{1,0:T(8,128)(2,1)} %bitcast.5), kind=kOutput, calls=%fused_computation.10 | convolution fusion | flops 671416320 | bytes 3014656 | tf_op jit(solution)/shard_map/dot_general | solution.py:19
  34.4 2.0 %collective-permute-start = (bf16[16,640]{1,0:T(8,128)(2,1)S(1)}, bf16[16,640]{1,0:T(8,128)(2,1)S(1)}, u32[]{:S(2)}, u32[]{:S(2)}) collective-permute-start(bf16[16,640]{1,0:T(8,128)(2,1)S(1)} %slice.82), channel_id=1, source_target_pairs={{0,4},{4,8},{8,12},{12,16},{16,20},{20,24},{24,28},{28,32},{32,36}... | collective-permute-start | bytes 61448 | tf_op jit(solution)/shard_map/ppermute | solution.py:28
  36.4 0.8 collective-permute-done
  37.3 1.6 %collective-permute-start.1 = (bf16[528,640]{1,0:T(8,128)(2,1)S(1)}, bf16[528,640]{1,0:T(8,128)(2,1)S(1)}, u32[]{:S(2)}, u32[]{:S(2)}) collective-permute-start(bf16[528,640]{1,0:T(8,128)(2,1)S(1)} %pad_maximum_fusion.x), channel_id=1, source_target_pairs={{0,1},{1,2},{2,3},{3,0},{4,5},{5,6},{6,7},{7,4},{8,9},{9,10},{10,1... | collective-permute-start | bytes 2027528 | tf_op jit(solution)/shard_map/ppermute | solution.py:23
  38.9 1.7 %collective-permute-start.2 = (bf16[528,640]{1,0:T(8,128)(2,1)S(1)}, bf16[528,640]{1,0:T(8,128)(2,1)}, u32[]{:S(2)}, u32[]{:S(2)}) collective-permute-start(bf16[528,640]{1,0:T(8,128)(2,1)S(1)} %pad_maximum_fusion.x), channel_id=1, source_target_pairs={{0,3},{1,0},{2,1},{3,2},{4,7},{5,4},{6,5},{7,6},{8,11},{9,8},{10,9... | collective-permute-start | bytes 2027528 | tf_op jit(solution)/shard_map/ppermute | solution.py:23
  40.6 0.6 gather_fusion
  41.2 0.6 gather_fusion.1
  42.1 6.6 %own_part.1 = (f32[528,384]{1,0:T(8,128)S(1)}, f32[528,1280]{1,0:T(8,128)}) custom-call(s32[6]{0:T(128)S(1)} %pad_add_fusion.ids, bf16[528,640]{1,0:T(8,128)(2,1)S(1)} %pad_maximum_fusion.x, bf16[2560,384]{1,0:T(8,128)(2,1)S(1)} %fusion.3.wsd.wsd1.wsd2, bf16[2560,2560]{1,0:T(8,128)(2,1)} %bitcast.22), custom_call_target="tpu_custom_call" | custom-call | flops 1124597760 | bytes 5644288 | tf_op jit(solution)/shard_map/own_part/pallas_call | solution.py:91
  48.6 0.9 copy-done.3
  49.6 6.5 %collective-permute-done.1.x1.r = bf16[528,640]{1,0:T(8,128)(2,1)S(1)} collective-permute-done((bf16[528,640]{1,0:T(8,128)(2,1)S(1)}, bf16[528,640]{1,0:T(8,128)(2,1)S(1)}, u32[]{:S(2)}, u32[]{:S(2)}) %collective-permute-start.1) | collective-permute-done | bytes 675872 | tf_op jit(solution)/shard_map/ppermute | solution.py:23
  56.2 1.6 %collective-permute-start.3 = (bf16[272,640]{1,0:T(8,128)(2,1)S(1)}, bf16[272,640]{1,0:T(8,128)(2,1)S(1)}, u32[]{:S(2)}, u32[]{:S(2)}) collective-permute-start(bf16[272,640]{1,0:T(8,128)(2,1)S(1)} %slice.63), channel_id=1, source_target_pairs={{0,1},{1,2},{2,3},{3,0},{4,5},{5,6},{6,7},{7,4},{8,9},{9,10},{10,1... | collective-permute-start | bytes 1044488 | tf_op jit(solution)/shard_map/ppermute | solution.py:23
  57.9 1.7 %slice.64 = bf16[256,640]{1,0:T(8,128)(2,1)} slice(bf16[528,640]{1,0:T(8,128)(2,1)} %collective-permute-done.2.x2.l), slice={[272:528], [0:640]} | slice | bytes 655360 | tf_op jit(solution)/shard_map/slice | solution.py:647
  59.6 1.7 %collective-permute-start.4 = (bf16[256,640]{1,0:T(8,128)(2,1)}, bf16[256,640]{1,0:T(8,128)(2,1)S(1)}, u32[]{:S(2)}, u32[]{:S(2)}) collective-permute-start(bf16[256,640]{1,0:T(8,128)(2,1)} %slice.64), channel_id=1, source_target_pairs={{0,3},{1,0},{2,1},{3,2},{4,7},{5,4},{6,5},{7,6},{8,11},{9,8},{10,9... | collective-permute-start | bytes 983048 | tf_op jit(solution)/shard_map/ppermute | solution.py:23
  61.4 1.1 copy-done.4
  62.5 9.1 %next_part.1 = (f32[528,384]{1,0:T(8,128)S(1)}, f32[528,1280]{1,0:T(8,128)}) custom-call(s32[6]{0:T(128)S(1)} %pad_add_fusion.ids, bf16[528,640]{1,0:T(8,128)(2,1)S(1)} %collective-permute-done.1.x1.r, bf16[528,640]{1,0:T(8,128)(2,1)} %collective-permute-done.2.x2.l, bf16[2560,384]{1,0:T(8,128)(2,1)} %copy-done.2, bf16[2560,384]{1,0:T(8,128)(2,1)} %copy-done.2, ...), custom_call_target="tpu_custom_call" | custom-call | flops 2249195520 | bytes 11288576 | tf_op jit(solution)/shard_map/next_part/pallas_call | solution.py:133
  71.7 0.7 copy-done.10
  72.4 0.7 copy-done.13
  73.1 12.0 %state_part.1 = (bf16[512,1280]{1,0:T(8,128)(2,1)}, bf16[512,256]{1,0:T(8,128)(2,1)S(1)}, bf16[512,128]{1,0:T(8,128)(2,1)S(1)}, f32[2,32,256]{2,1,0:T(8,128)S(1)...) custom-call(s32[6]{0:T(128)S(1)} %copy-done.10, ...), custom_call_target="tpu_custom_call" | custom-call | flops 1124597760 | bytes 9158656 | tf_op jit(solution)/shard_map/state_part/pallas_call | solution.py:276
  85.1 1.3 collective-permute-start.5
  86.4 1.3 collective-permute-done.5.got.got1
  87.7 0.8 join_part.1
  88.5 10.0 %collective-permute-start.6 = (bf16[128,1280]{1,0:T(8,128)(2,1)}, bf16[128,1280]{1,0:T(8,128)(2,1)}, u32[]{:S(2)}, u32[]{:S(2)}) collective-permute-start(bf16[128,1280]{1,0:T(8,128)(2,1)} %join_part.1), channel_id=1, source_target_pairs={{0,8},{4,12},{8,16},{12,20},{16,24},{20,28},{24,32},{28,36},{32,40... | collective-permute-start | bytes 983048 | tf_op jit(solution)/shard_map/ppermute | solution.py:28
  98.5 0.7 broadcast_in_dim.44
  99.2 1.4 broadcast_in_dim.45
  100.5 0.7 broadcast_in_dim.46.skip
  101.2 0.9 copy-done.6
  102.1 0.8 copy-done.8
  103.0 15.6 %mix_part.1 = (f32[512,1280]{1,0:T(8,128)}, f32[512,1280]{1,0:T(8,128)}) custom-call(s32[6]{0:T(128)S(1)} %copy-done.10, bf16[528,640]{1,0:T(8,128)(2,1)S(1)} %pad_maximum_fusion.x, bf16[528,640]{1,0:T(8,128)(2,1)S(1)} %collective-permute-done.1.x1.r, bf16[528,640]{1,0:T(8,128)(2,1)} %collective-permute-done.2.x2.l, ...), custom_call_target="tpu_custom_call" | custom-call | flops 3355443200 | bytes 13107200 | tf_op jit(solution)/shard_map/mix_part/pallas_call | solution.py:409
  118.6 6.8 %gated_part.1 = (bf16[512,1280]{1,0:T(8,128)(2,1)S(1)}, bf16[512,640]{1,0:T(8,128)(2,1)S(1)}, f32[8,512]{1,0:T(8,128)S(1)}) custom-call(s32[6]{0:T(128)S(1)} %copy-done.10, f32[512,1280]{1,0:T(8,128)} %get-tuple-element.85.p, f32[512,1280]{1,0:T(8,128)} %get-tuple-element.86.q, bf16[512,256]{1,0:T(8,128)(2,1)S(1)} %get-tuple-element.80.bc, ...), custom_call_target="tpu_custom_call" | custom-call | flops 1006632960 | bytes 8192000 | tf_op jit(solution)/shard_map/gated_part/pallas_call | solution.py:483
  125.5 0.4 collective-permute-start.7
  125.9 2.9 %collective-permute-start.8 = (bf16[256,640]{1,0:T(8,128)(2,1)S(1)}, bf16[256,640]{1,0:T(8,128)(2,1)S(1)}, u32[]{:S(2)}, u32[]{:S(2)}) collective-permute-start(bf16[256,640]{1,0:T(8,128)(2,1)S(1)} %get-tuple-element.113), channel_id=1, source_target_pairs={{0,3},{1,0},{2,1},{3,2},{4,7},{5,4},{6,5},{7,6},{8,11},{9,8},{10,9... | collective-permute-start | bytes 983048 | tf_op jit(solution)/shard_map/ppermute | solution.py:23
  128.8 4.4 %near_part.1 = bf16[2,512,640]{2,1,0:T(8,128)(2,1)S(1)} custom-call(s32[6]{0:T(128)S(1)} %copy-done.10, bf16[512,1280]{1,0:T(8,128)(2,1)S(1)} %get-tuple-element.91.z, bf16[1280,2560]{1,0:T(8,128)(2,1)} %wo.5), custom_call_target="tpu_custom_call" | custom-call | flops 1677721600 | bytes 5898240 | tf_op jit(solution)/shard_map/near_part/pallas_call | solution.py:522
  133.4 3.2 %collective-permute-start.11 = (bf16[256,640]{1,0:T(8,128)(2,1)S(1)}, bf16[256,640]{1,0:T(8,128)(2,1)S(1)}, u32[]{:S(2)}, u32[]{:S(2)}) collective-permute-start(bf16[256,640]{1,0:T(8,128)(2,1)S(1)} %get-tuple-element.109), channel_id=1, source_target_pairs={{0,3},{1,0},{2,1},{3,2},{4,7},{5,4},{6,5},{7,6},{8,11},{9,8},{10,9... | collective-permute-start | bytes 983048 | tf_op jit(solution)/shard_map/ppermute | solution.py:23
  136.8 1.3 collective-permute-start.12
  138.1 0.8 collective-permute-start.9
  138.9 10.6 %collective-permute-done.13.s1 = f32[8,512]{1,0:T(8,128)S(1)} collective-permute-done((f32[8,512]{1,0:T(8,128)S(1)}, f32[8,512]{1,0:T(8,128)S(1)}, u32[]{:S(2)}, u32[]{:S(2)}) %collective-permute-start.13) | collective-permute-done | bytes 16416 | tf_op jit(solution)/shard_map/ppermute | solution.py:23
  149.9 3.4 %collective-permute-done.14.s2 = f32[8,512]{1,0:T(8,128)S(1)} collective-permute-done((f32[8,512]{1,0:T(8,128)S(1)}, f32[8,512]{1,0:T(8,128)S(1)}, u32[]{:S(2)}, u32[]{:S(2)}) %collective-permute-start.14) | collective-permute-done | bytes 16416 | tf_op jit(solution)/shard_map/ppermute | solution.py:23
  153.5 3.2 %mine_part.1.own = bf16[1,512,640]{2,1,0:T(8,128)(2,1)S(1)} custom-call(s32[6]{0:T(128)S(1)} %copy-done.10, bf16[512,1280]{1,0:T(8,128)(2,1)S(1)} %get-tuple-element.91.z, bf16[1280,2560]{1,0:T(8,128)(2,1)} %wo.5), custom_call_target="tpu_custom_call" | custom-call | flops 838860800 | bytes 4259840 | tf_op jit(solution)/shard_map/mine_part/pallas_call | solution.py:522
  156.7 1.8 %collective-permute-done.15.s3 = f32[8,512]{1,0:T(8,128)S(1)} collective-permute-done((f32[8,512]{1,0:T(8,128)S(1)}, f32[8,512]{1,0:T(8,128)S(1)}, u32[]{:S(2)}, u32[]{:S(2)}) %collective-permute-start.15) | collective-permute-done | bytes 16416 | tf_op jit(solution)/shard_map/ppermute | solution.py:23
  158.6 1.2 final_part.1
  (74 shorter events, 2.4 us)
Async XLA Ops:
  0.0 1.1 copy-start
  3.3 8.5 %copy-start.17 = (s32[32,32]{1,0:T(8,128)S(1)}, s32[32,32]{1,0:T(8,128)}, u32[]{:S(2)}) copy-start(s32[32,32]{1,0:T(8,128)} %param.22) | copy-start | bytes 12292
  3.3 28.4 %all-to-all-start = ((bf16[32,32,640]{2,1,0:T(8,128)(2,1)}), bf16[32,32,640]{2,1,0:T(8,128)(2,1)}, u32[]{:S(2)}, u32[]{:S(2)}) async-start(bf16[32,32,640]{2,1,0:T(8,128)(2,1)} %bitcast.4), calls=%async_computation | async-start | bytes 2621440 | tf_op jit(solution)/shard_map/all_to_all | solution.py:608
  12.1 12.5 %copy-start.16 = (bf16[2560,20]{0,1:T(8,128)(2,1)S(1)}, bf16[2560,20]{0,1:T(8,128)(2,1)}, u32[]{:S(2)}) copy-start(bf16[2560,20]{0,1:T(8,128)(2,1)} %param.26) | copy-start | bytes 307204
  27.9 14.2 %copy-start.2 = (bf16[2560,384]{1,0:T(8,128)(2,1)}, bf16[2560,384]{1,0:T(8,128)(2,1)S(1)}, u32[]{:S(2)}) copy-start(bf16[2560,384]{1,0:T(8,128)(2,1)S(1)} %fusion.3.wsd.wsd1.wsd2) | copy-start | bytes 5898244
  31.7 8.9 %copy-start.15 = (s32[64]{0:T(128)S(1)}, s32[64]{0:T(128)}, u32[]{:S(2)}) copy-start(s32[64]{0:T(128)} %param.23) | copy-start | bytes 772
  34.3 7.5 %copy-start.19 = (f32[20]{0:T(128)S(1)}, f32[20]{0:T(128)}, u32[]{:S(2)}) copy-start(f32[20]{0:T(128)} %param.29) | copy-start | bytes 244
  34.4 2.9 %collective-permute-start = (bf16[16,640]{1,0:T(8,128)(2,1)S(1)}, bf16[16,640]{1,0:T(8,128)(2,1)S(1)}, u32[]{:S(2)}, u32[]{:S(2)}) collective-permute-start(bf16[16,640]{1,0:T(8,128)(2,1)S(1)} %slice.82), channel_id=1, source_target_pairs={{0,4},{4,8},{8,12},{12,16},{16,20},{20,24},{24,28},{28,32},{32,36}... | collective-permute-start | bytes 61448 | tf_op jit(solution)/shard_map/ppermute | solution.py:28
  37.3 18.8 %collective-permute-start.1 = (bf16[528,640]{1,0:T(8,128)(2,1)S(1)}, bf16[528,640]{1,0:T(8,128)(2,1)S(1)}, u32[]{:S(2)}, u32[]{:S(2)}) collective-permute-start(bf16[528,640]{1,0:T(8,128)(2,1)S(1)} %pad_maximum_fusion.x), channel_id=1, source_target_pairs={{0,1},{1,2},{2,3},{3,0},{4,5},{5,6},{6,7},{7,4},{8,9},{9,10},{10,1... | collective-permute-start | bytes 2027528 | tf_op jit(solution)/shard_map/ppermute | solution.py:23
  38.9 17.2 %collective-permute-start.2 = (bf16[528,640]{1,0:T(8,128)(2,1)S(1)}, bf16[528,640]{1,0:T(8,128)(2,1)}, u32[]{:S(2)}, u32[]{:S(2)}) collective-permute-start(bf16[528,640]{1,0:T(8,128)(2,1)S(1)} %pad_maximum_fusion.x), channel_id=1, source_target_pairs={{0,3},{1,0},{2,1},{3,2},{4,7},{5,4},{6,5},{7,6},{8,11},{9,8},{10,9... | collective-permute-start | bytes 2027528 | tf_op jit(solution)/shard_map/ppermute | solution.py:23
  42.1 19.3 %copy-start.9 = (s32[6]{0:T(128)}, s32[6]{0:T(128)S(1)}, u32[]{:S(2)}) copy-start(s32[6]{0:T(128)S(1)} %pad_add_fusion.ids) | copy-start | bytes 76
  42.1 19.2 %copy-start.21 = (f32[20]{0:T(128)S(1)}, f32[20]{0:T(128)}, u32[]{:S(2)}) copy-start(f32[20]{0:T(128)} %param.30) | copy-start | bytes 244
  48.6 0.9 copy-start.3
  56.2 15.5 %collective-permute-start.3 = (bf16[272,640]{1,0:T(8,128)(2,1)S(1)}, bf16[272,640]{1,0:T(8,128)(2,1)S(1)}, u32[]{:S(2)}, u32[]{:S(2)}) collective-permute-start(bf16[272,640]{1,0:T(8,128)(2,1)S(1)} %slice.63), channel_id=1, source_target_pairs={{0,1},{1,2},{2,3},{3,0},{4,5},{5,6},{6,7},{7,4},{8,9},{9,10},{10,1... | collective-permute-start | bytes 1044488 | tf_op jit(solution)/shard_map/ppermute | solution.py:23
  59.6 12.1 %collective-permute-start.4 = (bf16[256,640]{1,0:T(8,128)(2,1)}, bf16[256,640]{1,0:T(8,128)(2,1)S(1)}, u32[]{:S(2)}, u32[]{:S(2)}) collective-permute-start(bf16[256,640]{1,0:T(8,128)(2,1)} %slice.64), channel_id=1, source_target_pairs={{0,3},{1,0},{2,1},{3,2},{4,7},{5,4},{6,5},{7,6},{8,11},{9,8},{10,9... | collective-permute-start | bytes 983048 | tf_op jit(solution)/shard_map/ppermute | solution.py:23
  61.4 1.1 copy-start.4
  62.5 9.1 %copy-start.12 = (f32[8,128]{1,0:T(8,128)}, f32[8,128]{1,0:T(8,128)S(1)}, u32[]{:S(2)}) copy-start(f32[8,128]{1,0:T(8,128)S(1)} %scatter.9.heads) | copy-start | bytes 12292
  62.5 9.2 %copy-start.11 = (f32[4,1280]{1,0:T(4,128)S(1)}, f32[4,1280]{1,0:T(4,128)}, u32[]{:S(2)}) copy-start(f32[4,1280]{1,0:T(4,128)} %taps_v.1) | copy-start | bytes 61444
  62.5 9.2 %copy-start.14 = (f32[4,256]{1,0:T(4,128)S(1)}, f32[4,256]{1,0:T(4,128)}, u32[]{:S(2)}) copy-start(f32[4,256]{1,0:T(4,128)} %taps_s.1) | copy-start | bytes 12292
  71.7 0.7 copy-start.10
  72.4 0.7 copy-start.13
  73.1 25.4 %copy-start.20 = (f32[20]{0:T(128)S(1)}, f32[20]{0:T(128)}, u32[]{:S(2)}) copy-start(f32[20]{0:T(128)} %param.31) | copy-start | bytes 244
  85.1 3.4 %copy-start.5 = (bf16[512,128]{1,0:T(8,128)(2,1)}, bf16[512,128]{1,0:T(8,128)(2,1)S(1)}, u32[]{:S(2)}) copy-start(bf16[512,128]{1,0:T(8,128)(2,1)S(1)} %get-tuple-element.84.ecum3) | copy-start | bytes 393220
  85.1 13.4 %copy-start.7 = (f32[2,32,256]{2,1,0:T(8,128)}, f32[2,32,256]{2,1,0:T(8,128)S(1)}, u32[]{:S(2)}) copy-start(f32[2,32,256]{2,1,0:T(8,128)S(1)} %get-tuple-element.83.step_t) | copy-start | bytes 196612
  85.1 2.6 %collective-permute-start.5 = (bf16[144,1280]{1,0:T(8,128)(2,1)S(1)}, bf16[144,1280]{1,0:T(8,128)(2,1)S(1)}, u32[]{:S(2)}, u32[]{:S(2)}) collective-permute-start(bf16[144,1280]{1,0:T(8,128)(2,1)S(1)} %get-tuple-element.87), channel_id=1, source_target_pairs={{0,4},{4,8},{8,12},{12,16},{16,20},{20,24},{24,28},{28,32},{32,36}... | collective-permute-start | bytes 1105928 | tf_op jit(solution)/shard_map/ppermute | solution.py:28
  88.5 30.1 %collective-permute-start.6 = (bf16[128,1280]{1,0:T(8,128)(2,1)}, bf16[128,1280]{1,0:T(8,128)(2,1)}, u32[]{:S(2)}, u32[]{:S(2)}) collective-permute-start(bf16[128,1280]{1,0:T(8,128)(2,1)} %join_part.1), channel_id=1, source_target_pairs={{0,8},{4,12},{8,16},{12,20},{16,24},{20,28},{24,32},{28,36},{32,40... | collective-permute-start | bytes 983048 | tf_op jit(solution)/shard_map/ppermute | solution.py:28
  101.2 0.9 copy-start.6
  102.1 0.8 copy-start.8
  103.0 15.6 %copy-start.18 = (f32[1280]{0:T(1024)S(1)}, f32[1280]{0:T(1024)}, u32[]{:S(2)}) copy-start(f32[1280]{0:T(1024)} %param.32) | copy-start | bytes 15364
  125.5 11.1 %collective-permute-start.7 = (bf16[256,640]{1,0:T(8,128)(2,1)S(1)}, bf16[256,640]{1,0:T(8,128)(2,1)S(1)}, u32[]{:S(2)}, u32[]{:S(2)}) collective-permute-start(bf16[256,640]{1,0:T(8,128)(2,1)S(1)} %get-tuple-element.114), channel_id=1, source_target_pairs={{0,1},{1,2},{2,3},{3,0},{4,5},{5,6},{6,7},{7,4},{8,9},{9,10},{10,1... | collective-permute-start | bytes 983048 | tf_op jit(solution)/shard_map/ppermute | solution.py:23
  125.9 10.7 %collective-permute-start.8 = (bf16[256,640]{1,0:T(8,128)(2,1)S(1)}, bf16[256,640]{1,0:T(8,128)(2,1)S(1)}, u32[]{:S(2)}, u32[]{:S(2)}) collective-permute-start(bf16[256,640]{1,0:T(8,128)(2,1)S(1)} %get-tuple-element.113), channel_id=1, source_target_pairs={{0,3},{1,0},{2,1},{3,2},{4,7},{5,4},{6,5},{7,6},{8,11},{9,8},{10,9... | collective-permute-start | bytes 983048 | tf_op jit(solution)/shard_map/ppermute | solution.py:23
  133.3 25.2 %collective-permute-start.10 = (bf16[256,640]{1,0:T(8,128)(2,1)S(1)}, bf16[256,640]{1,0:T(8,128)(2,1)S(1)}, u32[]{:S(2)}, u32[]{:S(2)}) collective-permute-start(bf16[256,640]{1,0:T(8,128)(2,1)S(1)} %get-tuple-element.110), channel_id=1, source_target_pairs={{0,1},{1,2},{2,3},{3,0},{4,5},{5,6},{6,7},{7,4},{8,9},{9,10},{10,1... | collective-permute-start | bytes 983048 | tf_op jit(solution)/shard_map/ppermute | solution.py:23
  133.4 25.1 %collective-permute-start.11 = (bf16[256,640]{1,0:T(8,128)(2,1)S(1)}, bf16[256,640]{1,0:T(8,128)(2,1)S(1)}, u32[]{:S(2)}, u32[]{:S(2)}) collective-permute-start(bf16[256,640]{1,0:T(8,128)(2,1)S(1)} %get-tuple-element.109), channel_id=1, source_target_pairs={{0,3},{1,0},{2,1},{3,2},{4,7},{5,4},{6,5},{7,6},{8,11},{9,8},{10,9... | collective-permute-start | bytes 983048 | tf_op jit(solution)/shard_map/ppermute | solution.py:23
  136.8 21.7 %collective-permute-start.12 = (bf16[256,640]{1,0:T(8,128)(2,1)S(1)}, bf16[256,640]{1,0:T(8,128)(2,1)S(1)}, u32[]{:S(2)}, u32[]{:S(2)}) collective-permute-start(bf16[256,640]{1,0:T(8,128)(2,1)S(1)} %get-tuple-element.94), channel_id=1, source_target_pairs={{0,3},{1,0},{2,1},{3,2},{4,7},{5,4},{6,5},{7,6},{8,11},{9,8},{10,9... | collective-permute-start | bytes 983048 | tf_op jit(solution)/shard_map/ppermute | solution.py:23
  138.1 20.4 %collective-permute-start.9 = (bf16[256,640]{1,0:T(8,128)(2,1)S(1)}, bf16[256,640]{1,0:T(8,128)(2,1)S(1)}, u32[]{:S(2)}, u32[]{:S(2)}) collective-permute-start(bf16[256,640]{1,0:T(8,128)(2,1)S(1)} %get-tuple-element.93), channel_id=1, source_target_pairs={{0,1},{1,2},{2,3},{3,0},{4,5},{5,6},{6,7},{7,4},{8,9},{9,10},{10,1... | collective-permute-start | bytes 983048 | tf_op jit(solution)/shard_map/ppermute | solution.py:23
  138.9 10.7 %collective-permute-start.13 = (f32[8,512]{1,0:T(8,128)S(1)}, f32[8,512]{1,0:T(8,128)S(1)}, u32[]{:S(2)}, u32[]{:S(2)}) collective-permute-start(f32[8,512]{1,0:T(8,128)S(1)} %get-tuple-element.95.s0), channel_id=1, source_target_pairs={{0,1},{1,2},{2,3},{3,0},{4,5},{5,6},{6,7},{7,4},{8,9},{9,10},{10,1... | collective-permute-start | bytes 49160 | tf_op jit(solution)/shard_map/ppermute | solution.py:23
  149.6 3.7 %collective-permute-start.14 = (f32[8,512]{1,0:T(8,128)S(1)}, f32[8,512]{1,0:T(8,128)S(1)}, u32[]{:S(2)}, u32[]{:S(2)}) collective-permute-start(f32[8,512]{1,0:T(8,128)S(1)} %get-tuple-element.95.s0), channel_id=1, source_target_pairs={{0,3},{1,0},{2,1},{3,2},{4,7},{5,4},{6,5},{7,6},{8,11},{9,8},{10,9... | collective-permute-start | bytes 49160 | tf_op jit(solution)/shard_map/ppermute | solution.py:23
  153.3 5.2 %collective-permute-start.15 = (f32[8,512]{1,0:T(8,128)S(1)}, f32[8,512]{1,0:T(8,128)S(1)}, u32[]{:S(2)}, u32[]{:S(2)}) collective-permute-start(f32[8,512]{1,0:T(8,128)S(1)} %get-tuple-element.95.s0), channel_id=1, source_target_pairs={{0,2},{1,3},{2,0},{3,1},{4,6},{5,7},{6,4},{7,5},{8,10},{9,11},{10,... | collective-permute-start | bytes 49160 | tf_op jit(solution)/shard_map/ppermute | solution.py:23
  153.5 6.2 %copy-start.1 = (bf16[512,640]{1,0:T(8,128)(2,1)S(1)}, bf16[512,640]{1,0:T(8,128)(2,1)}, u32[]{:S(2)}) copy-start(bf16[512,640]{1,0:T(8,128)(2,1)} %param.20) | copy-start | bytes 1966084

commit v2 on v0

v2 whole, which is shorter than its diff:
```python
import jax
import jax.numpy as jnp
from jax import lax
from jax.experimental import pallas as pl
from jax.experimental.pallas import tpu as pltpu
from jax.sharding import PartitionSpec as P

BF = jnp.bfloat16
F32 = jnp.float32
STRETCH = 256
TAIL = 16
TILE = 256
LOG2E = 1.4426950408889634
RING = 4
VMEM = 16 * 1024 * 1024


def dot(a, b):
    return jnp.dot(a, b, preferred_element_type=F32)


def turned(value, steps):
    return lax.ppermute(value, "head", [(i, (i + steps) % RING) for i in range(RING)])


def shifted(value, steps):
    count = lax.axis_size("ctx")
    return lax.ppermute(value, "ctx", [(i, i + steps) for i in range(count - steps)])


def silu(v):
    return v * (1.0 / (1.0 + jnp.exp(-v)))


def split3(x):
    high = x.astype(BF).astype(F32)
    rest = x - high
    mid = rest.astype(BF).astype(F32)
    low = (rest - mid).astype(BF).astype(F32)
    return high, mid, low


def pack3(x):
    high, mid, low = split3(x)
    return (high + pltpu.roll(mid, 32, 1) + pltpu.roll(low, 64, 1)).astype(BF)


def spread(tile, width):
    lane = lax.broadcasted_iota(jnp.int32, (128, width), 0)
    col = lax.broadcasted_iota(jnp.int32, (128, width), 1)
    hit = ((lane & 31) == tile * (width // 64) + (col >> 6)) & (lane < 96)
    return jnp.where(hit, 1.0, 0.0).astype(BF)


def call(body, outs, args, name, flops, exps=0, scratch=()):
    size = sum(a.size * a.dtype.itemsize for a in args[1:]) + sum(
        o.size * o.dtype.itemsize for o in outs
    )
    return pl.pallas_call(
        body,
        in_specs=[pl.BlockSpec(memory_space=pltpu.SMEM)]
        + [pl.BlockSpec(memory_space=pltpu.VMEM)] * (len(args) - 1),
        out_specs=[pl.BlockSpec(memory_space=pltpu.VMEM)] * len(outs),
        out_shape=outs,
        scratch_shapes=scratch,
        compiler_params=pltpu.CompilerParams(vmem_limit_bytes=VMEM),
        cost_estimate=pl.CostEstimate(
            flops=int(flops), bytes_accessed=int(size), transcendentals=int(exps)
        ),
        name=name,
    )(*args)


def shape(dims, dtype=F32):
    return jax.ShapeDtypeStruct(dims, dtype)


def chunk_of(ids, at, k):
    return pl.ds(pl.multiple_of(ids[at] * k, 128), k)


def wide(j):
    return slice(j * TILE, (j + 1) * TILE)


def block_rows(block):
    return slice(block * STRETCH, (block + 1) * STRETCH)


def own_body(ids, x, wsd, wm, acc):
    at = chunk_of(ids, 0, x.shape[1])
    acc[:, 2560:] = dot(x[...], wsd[at, :])
    for j in range(10):
        acc[:, wide(j)] = dot(x[...], wm[at, wide(j)])


def own_part(ids, x, wsd, wm):
    rows, k = x.shape
    n = wsd.shape[1] + wm.shape[1]
    return call(own_body, [shape((rows, n))], (ids, x, wsd, wm), "own_part", 2 * rows * k * n)[0]


def next_body(ids, r, l, wsd, wm, before, acc):
    k = r.shape[1]
    at_r, at_l = chunk_of(ids, 1, k), chunk_of(ids, 2, k)
    acc[:, 2560:] = before[:, 2560:] + dot(r[...], wsd[at_r, :]) + dot(l[...], wsd[at_l, :])
    for j in range(10):
        c = wide(j)
        acc[:, c] = before[:, c] + dot(r[...], wm[at_r, c]) + dot(l[...], wm[at_l, c])


def next_part(ids, r, l, wsd, wm, acc):
    rows, k = r.shape
    n = acc.shape[1]
    return call(
        next_body, [shape((rows, n))], (ids, r, l, wsd, wm, acc), "next_part", 4 * rows * k * n
    )[0]


def tail_body(ids, t, t_r, t_l, t_o, wsd, wm, out):
    k = t.shape[1]
    total_s = jnp.zeros((TAIL, 256), F32)
    totals = [jnp.zeros((TAIL, TILE), F32)] * 5
    for at, piece in enumerate((t, t_r, t_l, t_o)):
        place = chunk_of(ids, at, k)
        total_s = total_s + dot(piece[...], wsd[place, :256])
        for j in range(5):
            totals[j] = totals[j] + dot(piece[...], wm[place, wide(5 + j)])
    keep = ids[4] > 0
    for j in range(5):
        out[:, wide(j)] = jnp.where(keep, totals[j].astype(BF).astype(F32), 0.0)
    out[:, 1280:] = jnp.where(keep, total_s.astype(BF).astype(F32), 0.0)


def tail_part(ids, t, t_r, t_l, t_o, wsd, wm):
    return call(
        tail_body,
        [shape((TAIL, 1536))],
        (ids, t, t_r, t_l, t_o, wsd, wm),
        "tail_part",
        2 * 256 * 2560 * 1536,
    )[0]


SEG = STRETCH + 8


def convolved(ids, xs, first, second, before, taps):
    xs[:8, :] = before
    xs[8:SEG, :] = first
    xs[SEG : SEG + 8, :] = jnp.where(ids[5] > 0, first[STRETCH - 8 :, :], 0.0)
    xs[SEG + 8 :, :] = second
    result = []
    for block in range(2):
        total = None
        for k in range(4):
            low = block * SEG + 5 + k
            term = xs[low : low + STRETCH, :] * taps[k : k + 1, :]
            total = term if total is None else total + term
        result.append(silu(total).astype(BF))
    return result


def rounded(x):
    return x.astype(BF).astype(F32)


def state_body(
    ids, o1, o2, wsd, wm, acc, tail, taps_s, taps_v, heads,
    act, bc, cum3, cum_t, step_t, ecum3, state0, state_dev, rows_out, payload,
    xs, bt, w3, last3,
):
    k = o1.shape[1]
    at = chunk_of(ids, 3, k)
    first = acc[:STRETCH, 2560:] + dot(o1[...], wsd[at, :])
    second = acc[STRETCH:, 2560:] + dot(o2[...], wsd[at, :])
    pair = convolved(
        ids, xs.at[0], rounded(first[:, :256]), rounded(second[:, :256]), tail[8:, 1280:], taps_s
    )
    lane = lax.broadcasted_iota(jnp.int32, (STRETCH, 128), 1)
    row_id = lax.broadcasted_iota(jnp.int32, (STRETCH, STRETCH), 0)
    col_id = lax.broadcasted_iota(jnp.int32, (STRETCH, STRETCH), 1)
    below = jnp.where(row_id >= col_id, 1.0, 0.0).astype(BF)
    lasts = []
    for block, raw in ((0, first[:, 256:]), (1, second[:, 256:])):
        rows = block_rows(block)
        bc[rows, :] = pair[block]
        bt[block] = jnp.transpose(pair[block][:, :128].astype(F32)).astype(BF)
        raw = raw + heads[0:1, :]
        small = jnp.exp(-jnp.abs(raw))
        one = 1.0 + small
        log_one = jnp.where(one == 1.0, small, jnp.log(one) * (small / (one - 1.0 + 1e-30)))
        step = jnp.where(lane < 32, jnp.maximum(raw, 0.0) + log_one, 0.0)
        decay = pack3(step * (heads[1:2, :] * (-LOG2E)))
        sums = dot(below, decay)
        sums = sums + pltpu.roll(sums, 96, 1) + pltpu.roll(sums, 64, 1)
        sums = jnp.where(lane < 32, sums, 0.0)
        final = sums[STRETCH - 1 : STRETCH, :]
        cum3[rows, :] = pack3(sums)
        cum_t[block] = jnp.transpose(sums)[:32]
        step_t[block] = jnp.transpose(step)[:32]
        ecum3[rows, :] = pack3(jnp.where(lane < 32, jnp.exp2(sums), 0.0))
        w3[rows, :] = pack3(jnp.exp2(final - sums) * step)
        lasts.append(jnp.where(lane[:1] < 32, jnp.exp2(final), 0.0))
    pad_row = lax.broadcasted_iota(jnp.int32, (16, 128), 0)
    last3[...] = pack3(jnp.where(pad_row == 0, lasts[0], jnp.where(pad_row == 1, lasts[1], 0.0)))
    carry0 = jnp.where(ids[4] > 0, 1.0, 0.0)
    carry1 = jnp.where(ids[5] > 0, 1.0, 0.0)
    row = lax.broadcasted_iota(jnp.int32, (16, TILE), 0)
    for j in range(5):
        c = wide(j)
        a = wide(5 + j)
        first = rounded(acc[:STRETCH, a] + dot(o1[...], wm[at, a]))
        second = rounded(acc[STRETCH:, a] + dot(o2[...], wm[at, a]))
        pair = convolved(ids, xs.at[1 + j % 2], first, second, tail[8:, c], taps_v[:, c])
        select = spread(j, TILE)
        states = []
        for block in range(2):
            rows = block_rows(block)
            act[rows, c] = pair[block]
            weighted = (pair[block].astype(F32) * dot(w3[rows, :], select)).astype(BF)
            states.append(dot(bt[block], weighted))
        ends = dot(last3[...], select)
        end0, end1 = ends[0:1, :], ends[1:2, :] * carry1
        whole_decay = end0 * carry0 * end1
        device = states[1] + end1 * states[0]
        state0[:, c] = states[0]
        state_dev[:, c] = device
        rows_out[:, c] = jnp.where(row[:8] == 0, end0, jnp.where(row[:8] == 1, whole_decay, 0.0))
        high, mid, low = split3(whole_decay)
        payload[:128, c] = device.astype(BF)
        payload[128:, c] = jnp.where(
            row == 0, high, jnp.where(row == 1, mid, jnp.where(row == 2, low, 0.0))
        ).astype(BF)


def state_part(ids, o1, o2, wsd, wm, acc, tail, taps_s, taps_v, heads):
    tok = acc.shape[0]
    return call(
        state_body,
        [
            shape((tok, 1280), BF),
            shape((tok, 256), BF),
            shape((tok, 128), BF),
            shape((2, 32, STRETCH)),
            shape((2, 32, STRETCH)),
            shape((tok, 128), BF),
            shape((128, 1280)),
            shape((128, 1280)),
            shape((8, 1280)),
            shape((144, 1280), BF),
        ],
        (ids, o1, o2, wsd, wm, acc, tail, taps_s, taps_v, heads),
        "state_part",
        2 * tok * 640 * 1664 * 2,
        scratch=[
            pltpu.VMEM((3, 2 * SEG, TILE), F32),
            pltpu.VMEM((2, 128, STRETCH), BF),
            pltpu.VMEM((tok, 128), BF),
            pltpu.VMEM((16, 128), BF),
        ],
    )


def join_body(ids, state, row, got, out):
    out[...] = (state[...] + row[1:2, :] * got[:128, :].astype(F32)).astype(BF)


def join_part(ids, state, row, got):
    return call(
        join_body, [shape(state.shape, BF)], (ids, state, row, got), "join_part", 2 * state.size
    )[0]


def mix_body(ids, o1, o2, wm, acc, act, bc, cum3, cum_t, step_t, ecum3, skip, p_out, q_out, sc):
    k = o1.shape[1]
    at = chunk_of(ids, 3, k)
    row_id = lax.broadcasted_iota(jnp.int32, (STRETCH, STRETCH), 0)
    col_id = lax.broadcasted_iota(jnp.int32, (STRETCH, STRETCH), 1)
    for block in range(2):
        rows = block_rows(block)
        scores = lax.dot_general(
            bc[rows, 128:], bc[rows, :128], (((1,), (1,)), ((), ())), preferred_element_type=F32
        )
        sc[block] = jnp.where(row_id >= col_id, scores, 0.0)
    half = STRETCH // 2

    def one(i, _):
        c = pl.ds(pl.multiple_of(i * TILE, TILE), TILE)
        select = spread(i, TILE)
        lane = lax.broadcasted_iota(jnp.int32, (128, STRETCH), 0)
        group = lax.broadcasted_iota(jnp.int32, (STRETCH, TILE), 1) >> 6
        for block, other in ((0, o1), (1, o2)):
            rows = block_rows(block)
            gate = silu(rounded(acc[rows, c] + dot(other[...], wm[at, c])))
            values = act[rows, c]
            top = jnp.zeros((half, TILE), F32)
            bottom = jnp.zeros((half, TILE), F32)
            for j in range(TILE // 64):
                h = i * (TILE // 64) + j
                pick = jnp.where(((lane & 31) == h) & (lane < 96), 1.0, 0.0).astype(BF)
                cum = dot(cum3[rows, :], pick)
                cum_s = cum_t[block, pl.ds(h, 1), :]
                step_s = step_t[block, pl.ds(h, 1), :]
                mine = jnp.where(group == j, values, jnp.zeros_like(values))
                m_top = (
                    sc[block, :half, :half]
                    * jnp.exp2(jnp.minimum(cum[:half, :half] - cum_s[:, :half], 0.0))
                    * step_s[:, :half]
                ).astype(BF)
                m_bottom = (
                    sc[block, half:, :]
                    * jnp.exp2(jnp.minimum(cum[half:, :] - cum_s, 0.0))
                    * step_s
                ).astype(BF)
                top = top + dot(m_top, mine[:half, :])
                bottom = bottom + dot(m_bottom, mine)
            within = jnp.concatenate([top, bottom], axis=0)
            p_out[rows, c] = (within + skip[0:1, c] * values.astype(F32)) * gate
            q_out[rows, c] = dot(ecum3[rows, :], select) * gate
        return 0

    lax.fori_loop(0, act.shape[1] // TILE, one, 0)


def mix_part(ids, o1, o2, wm, acc, act, bc, cum3, cum_t, step_t, ecum3, skip):
    return call(
        mix_body,
        [shape(act.shape)] * 2,
        (ids, o1, o2, wm, acc, act, bc, cum3, cum_t, step_t, ecum3, skip),
        "mix_part",
        8e9,
        exps=20 * 512 * 256,
        scratch=[pltpu.VMEM((2, STRETCH, STRETCH), F32)],
    )


def gated_body(
    ids, p, q, bc, got1, got2, state0, rows_in, gain, wo, z, far_r, far_l, squares
):
    carry0 = jnp.where(ids[4] > 0, 1.0, 0.0)
    carry1 = jnp.where(ids[5] > 0, 1.0, 0.0)
    sums = [None, None]
    for j in range(5):
        c = wide(j)
        more = got1[128:, c].astype(F32)
        decay = more[0:1, :] + more[1:2, :] + more[2:3, :]
        entering = got1[:128, c].astype(F32) + decay * got2[:, c].astype(F32)
        start0 = entering * carry0
        start1 = (rows_in[0:1, c] * start0 + state0[:, c]) * carry1
        for block, start in ((0, start0), (1, start1)):
            rows = block_rows(block)
            from_start = dot(bc[rows, 128:], start.astype(BF))
            gated = p[rows, c] + q[rows, c] * from_start
            square = gated * gated
            square = square[:, :128] + square[:, 128:]
            sums[block] = square if sums[block] is None else sums[block] + square
            z[rows, c] = (gated * gain[0:1, c]).astype(BF)
    ncol = wo.shape[1] // RING
    at = pl.ds(pl.multiple_of(ids[3] * ncol, 128), ncol)
    far_r[:STRETCH, :] = dot(z[:STRETCH, :], wo[:, at]).astype(BF)
    far_l[:STRETCH, :] = dot(z[STRETCH:, :], wo[:, at]).astype(BF)
    flats = [jnp.sum(jnp.transpose(s), axis=0, keepdims=True) for s in sums]
    row = lax.broadcasted_iota(jnp.int32, (16, STRETCH), 0)
    for block in range(2):
        squares[:, block_rows(block)] = jnp.broadcast_to(flats[block], (8, STRETCH))
        high, mid, low = split3(flats[block])
        packed = jnp.where(
            row == 0, high, jnp.where(row == 1, mid, jnp.where(row == 2, low, 0.0))
        ).astype(BF)
        far_r[STRETCH:, block_rows(block)] = packed
        far_l[STRETCH:, block_rows(block)] = packed
    far_r[STRETCH:, 512:] = jnp.zeros((16, ncol - 512), BF)
    far_l[STRETCH:, 512:] = jnp.zeros((16, ncol - 512), BF)


def gated_part(ids, p, q, bc, got1, got2, state0, rows_in, gain, wo):
    tok, nv = p.shape
    ncol = wo.shape[1] // RING
    return call(
        gated_body,
        [
            shape((tok, nv), BF),
            shape((STRETCH + 16, ncol), BF),
            shape((STRETCH + 16, ncol), BF),
            shape((8, tok)),
        ],
        (ids, p, q, bc, got1, got2, state0, rows_in, gain, wo),
        "gated_part",
        2 * tok * nv * (ncol + 128),
    )


def near_body(ids, z, wo, low_r, top_l, top_r, low_l):
    ncol = wo.shape[1] // RING
    at_l = pl.ds(pl.multiple_of(ids[1] * ncol, 128), ncol)
    at_r = pl.ds(pl.multiple_of(ids[2] * ncol, 128), ncol)
    low_r[...] = dot(z[STRETCH:, :], wo[:, at_r]).astype(BF)
    top_l[...] = dot(z[:STRETCH, :], wo[:, at_l]).astype(BF)
    top_r[...] = dot(z[:STRETCH, :], wo[:, at_r])
    low_l[...] = dot(z[STRETCH:, :], wo[:, at_l])


def near_part(ids, z, wo):
    tok, nv = z.shape
    ncol = wo.shape[1] // RING
    return call(
        near_body,
        [shape((STRETCH, ncol), BF)] * 2 + [shape((STRETCH, ncol))] * 2,
        (ids, z, wo),
        "near_part",
        4 * tok * nv * ncol,
    )


def mine_body(ids, z, wo, out):
    ncol = wo.shape[1] // RING
    at = pl.ds(pl.multiple_of(ids[0] * ncol, 128), ncol)
    out[...] = dot(z[...], wo[:, at])


def mine_part(ids, z, wo):
    tok, nv = z.shape
    ncol = wo.shape[1] // RING
    return call(mine_body, [shape((tok, ncol))], (ids, z, wo), "mine_part", 2 * tok * nv * ncol)[0]


def add_body(ids, a1, b1, a2, b2, o1, o2):
    o1[:STRETCH, :] = (a1[...] + b1[:STRETCH, :].astype(F32)).astype(BF)
    o1[STRETCH:, :] = b1[STRETCH:, :]
    o2[...] = (a2[...] + b2[:STRETCH, :].astype(F32)).astype(BF)


def add_part(ids, a1, b1, a2, b2):
    return call(
        add_body,
        [shape(b1.shape, BF), shape(a2.shape, BF)],
        (ids, a1, b1, a2, b2),
        "add_part",
        2 * a1.size,
    )


def final_body(ids, own, top_r, low_r, top_l, low_l, mine, sq_r, sq_l, out):
    total = mine[0:1, :]
    for other in (sq_r, sq_l, top_r):
        more = other[STRETCH:, :512].astype(F32)
        total = total + (more[0:1, :] + more[1:2, :] + more[2:3, :])
    inv = lax.rsqrt(total * (1.0 / 5120.0) + 1e-05)
    inv = jnp.transpose(jnp.broadcast_to(inv, (128, inv.shape[1])))
    for block, r, l in ((0, top_r, top_l), (1, low_r, low_l)):
        rows = block_rows(block)
        scale = inv[rows, :]
        for low in range(0, out.shape[1], 128):
            c = slice(low, low + 128)
            value = own[rows, c] + r[:STRETCH, c].astype(F32) + l[:STRETCH, c].astype(F32)
            out[rows, c] = (value * scale).astype(BF)


def final_part(ids, own, top_r, low_r, top_l, low_l, mine, sq_r, sq_l):
    return call(
        final_body,
        [shape(own.shape, BF)],
        (ids, own, top_r, low_r, top_l, low_l, mine, sq_r, sq_l),
        "final_part",
        4 * own.size,
    )[0]


def on_device(
    tokens,
    send_rows,
    send_counts,
    stretch_segments,
    main_proj,
    state_proj,
    step_proj,
    conv_main,
    conv_state,
    step_bias,
    decay_log,
    skip_gain,
    norm_gain,
    out_proj,
):
    ctx = lax.axis_index("ctx").astype(jnp.int32)
    head = lax.axis_index("head").astype(jnp.int32)
    tok, width = tokens.shape
    sources, slots = send_rows.shape[1:]
    heads = step_bias.shape[0]
    inner = main_proj.shape[2]
    head_dim = inner // heads

    send_list = send_rows.reshape(sources * slots)
    pick = (send_list[:, None] == jnp.arange(tok, dtype=jnp.int32)[None, :]).astype(BF)
    outgoing = dot(pick, tokens).astype(BF).reshape(sources, slots, width)
    arrived = lax.all_to_all(outgoing, "ctx", split_axis=0, concat_axis=0, tiled=True)

    blocks = tok // STRETCH
    block_ids = ctx * blocks + jnp.arange(blocks, dtype=jnp.int32)
    segment = jnp.take(stretch_segments, block_ids)
    before = jnp.take(stretch_segments, jnp.maximum(block_ids - 1, 0))
    carry = ((segment == before) & (block_ids > 0)).astype(jnp.int32)
    ring = jnp.stack([head, head + 3, head + 1, head + 2]) % RING
    ids = jnp.concatenate([ring, carry]).astype(jnp.int32)
    wm = main_proj.reshape(main_proj.shape[0], 2 * inner)
    wsd = jnp.concatenate(
        [state_proj, jnp.pad(step_proj, ((0, 0), (0, 128 - heads)))], axis=1
    )
    head_rows = jnp.zeros((8, 128), F32)
    head_rows = head_rows.at[0, :heads].set(step_bias).at[1, :heads].set(jnp.exp(decay_log))
    skip = jnp.broadcast_to(jnp.repeat(skip_gain, head_dim)[None, :], (8, inner))
    gain = jnp.broadcast_to(norm_gain[None, :], (8, inner))

    column = jnp.take(send_counts, ctx, axis=1)
    ends = jnp.cumsum(column)
    begins = ends - column
    position = jnp.arange(tok, dtype=jnp.int32)
    slot = position[:, None] - begins[None, :]
    inside = (slot >= 0) & (slot < column[None, :])
    flat = jnp.sum(
        jnp.where(inside, slot + jnp.arange(sources, dtype=jnp.int32)[None, :] * slots, 0), axis=1
    )
    place = (flat[:, None] == jnp.arange(sources * slots, dtype=jnp.int32)[None, :]).astype(BF)
    arrived, wm, wsd, place = lax.optimization_barrier((arrived, wm, wsd, place))
    packed = dot(place, arrived.reshape(sources * slots, width)).astype(BF)

    r = turned(packed, 1)
    l = turned(packed, -1)
    t = shifted(packed[tok - TAIL :], 1)
    t_r = turned(t, 1)
    t_l = turned(t, -1)
    t_o = turned(t, 2)
    acc = own_part(ids, packed, wsd, wm)
    r, l, acc = lax.optimization_barrier((r, l, acc))
    o1 = turned(r[:STRETCH], 1)
    o2 = turned(l[STRETCH:], -1)
    acc = next_part(ids, r, l, wsd, wm, acc)
    tail = tail_part(ids, t, t_r, t_l, t_o, wsd, wm)
    o1, o2, acc, tail, skip, gain = lax.optimization_barrier((o1, o2, acc, tail, skip, gain))
    act, bc, cum3, cum_t, step_t, ecum3, state0, state_dev, rows_out, payload = state_part(
        ids, o1, o2, wsd, wm, acc, tail, conv_state, conv_main, head_rows
    )

    got1 = shifted(payload, 1)
    joined = join_part(ids, state_dev, rows_out, got1)
    got2 = shifted(joined, 2)
    p, q = mix_part(ids, o1, o2, wm, acc, act, bc, cum3, cum_t, step_t, ecum3, skip)

    z, far_r, far_l, squares = gated_part(
        ids, p, q, bc, got1, got2, state0, rows_out, gain, out_proj
    )
    got_r = turned(far_r, 1)
    got_l = turned(far_l, -1)
    low_r, top_l, top_r, low_l = near_part(ids, z, out_proj)
    low_r = turned(low_r, 1)
    top_l = turned(top_l, -1)
    sum_r, sum_l = add_part(ids, top_r, got_r, low_l, got_l)
    top_r = turned(sum_r, 1)
    low_l = turned(sum_l, -1)
    own = mine_part(ids, z, out_proj)
    return final_part(ids, own, top_r, low_r, top_l, low_l, squares, got_r, got_l)


def solution(mesh):
    return jax.shard_map(
        on_device,
        mesh=mesh,
        in_specs=(
            P("ctx", "head"),
            P("ctx", None, None),
            P(),
            P(),
            P(None, None, "head"),
            P(),
            P(None, "head"),
            P(None, "head"),
            P(),
            P("head"),
            P("head"),
            P("head"),
            P("head"),
            P("head", None),
        ),
        out_specs=P("ctx", "head"),
        check_vma=False,
    )
```

time: 304 us -> 128 us (0.42)
  waiting for transfers between devices: 151 us -> 20 us
  Pallas kernels: 0 us -> 34.5 us
  blocking collectives: 34.4 us -> 0 us
  matrix products: 36.6 us -> 5.69 us
  starting transfers between devices: 10.2 us -> 40.6 us
  local copies, waits for them, and re-layouts: 37.5 us -> 21.2 us
  between operations: 13.8 us -> 0.32 us
  other arithmetic: 16.8 us -> 3.44 us
    unnamed x4 -> x0, waiting for transfers between devices: 81.3 us -> none
    all_gather x2 -> x0, waiting for transfers between devices: 50.5 us -> none  [the longest x1 32.2 us: carried_in(): lax.all_gather(a.astype(kind), axis)]
    pallas_call x0 -> x11, Pallas kernels: none -> 34.5 us  [call(): pl.pallas_call(body, in_specs=[pl.BlockSpec(memory_space=pltpu.SMEM)] + [...]
    ppermute x1 -> x16, starting transfers between devices: 1.74 us -> 32.1 us  [the longest x13 19.5 us: turned(): lax.ppermute(value, 'head', [(i, (i + steps) % RING) for i in range(RING)])]
    dot_general x10 -> x2, matrix products: 34.2 us -> 5.69 us  [dot(): return jnp.dot(a, b, preferred_element_type=F32)]
    all_gather x1 -> x0, blocking collectives: 24 us -> none  [carried_in(): lax.all_gather(a.astype(kind), axis)]
    ppermute x1 -> x16, waiting for transfers between devices: 0.01 us -> 17.6 us  [the longest x13 16 us: turned(): lax.ppermute(value, 'head', [(i, (i + steps) % RING) for i in range(RING)])]
    all_to_all x1, waiting for transfers between devices: 19.3 us -> 2.35 us  [on_device(): lax.all_to_all(outgoing, 'ctx', split_axis=0, concat_axis=0, tiled=True)]
  transfers between devices with their start and end apart: 5 -> 17, of which waited for: 4 -> 8; matrix products, arithmetic and copies ran while one was open for 7% -> 15% of each run, Pallas kernels for 0% -> 18%
where the time goes in v2:
time: 128 us; the launch traced here: 126 us
  starting transfers between devices  40.6 us (32%)
  Pallas kernels  34.5 us (27%)
  local copies, waits for them, and re-layouts  21.2 us (17%)
  waiting for transfers between devices  20 us (16%)
  matrix products  5.69 us (4%)
  other arithmetic  3.44 us (3%)
    pallas_call x11, Pallas kernels, call(): pl.pallas_call(body, in_specs=[pl.BlockSpec(memory_space=pltpu.SMEM)] + [...  34.5 us
    ppermute x13, starting transfers between devices, turned(): lax.ppermute(value, 'head', [(i, (i + steps) % RING) for i in range(RING)])  19.5 us
    unnamed x32, local copies, waits for them, and re-layouts  17.9 us
    ppermute x13, waiting for transfers between devices, turned(): lax.ppermute(value, 'head', [(i, (i + steps) % RING) for i in range(RING)])  16 us
    ppermute x3, starting transfers between devices, shifted(): lax.ppermute(value, 'ctx', [(i, i + steps) for i in range(count - steps)])  12.6 us
    all_to_all x1, starting transfers between devices, on_device(): lax.all_to_all(outgoing, 'ctx', split_axis=0, concat_axis=0, tiled=True)  8.49 us
    dot_general x2, matrix products, dot(): return jnp.dot(a, b, preferred_element_type=F32)  5.69 us
  transfers between devices with their start and end apart: 17, of which 8 were waited for; matrix products, arithmetic and copies ran while one was open for 15% of the time, Pallas kernels for 18%

profile of v2, /device:TPU:0, one launch (start us, length us, event | category | flops | bytes accessed | tf_op | source)
XLA Modules:
  0.0 125.7 jit_solution(987596374483735938)
XLA Ops:
  0.0 0.9 eq.34
  0.9 0.2 copy-done
  1.1 2.2 %fusion.4 = bf16[1024,640]{1,0:T(8,128)(2,1)} fusion(bf16[512,640]{1,0:T(8,128)(2,1)S(1)} %copy-done, s32[1024]{0:T(1024)S(1)} %eq.34), kind=kOutput, calls=%fused_computation.9 | convolution fusion | flops 672268288 | bytes 1970176 | tf_op jit(solution)/shard_map/dot_general | solution.py:19
  3.3 8.5 %all-to-all-start = ((bf16[32,32,640]{2,1,0:T(8,128)(2,1)}), bf16[32,32,640]{2,1,0:T(8,128)(2,1)}, u32[]{:S(2)}, u32[]{:S(2)}) async-start(bf16[32,32,640]{2,1,0:T(8,128)(2,1)} %bitcast.4), calls=%async_computation | async-start | bytes 2621440 | tf_op jit(solution)/shard_map/all_to_all | solution.py:497
  12.2 12.5 %copy.18 = bf16[320,8,2,1280]{3,1,2,0:T(8,128)(2,1)} copy(bf16[320,8,2,1280]{3,2,1,0:T(2,128)(2,1)} %bitcast.21) | data formatting | bytes 26214400
  24.7 0.4 copy.17
  25.1 0.6 gather_fusion
  25.8 0.6 gather_fusion.1
  26.6 1.2 fusion.2
  27.8 1.6 %fusion.3.wsd = bf16[2560,384]{1,0:T(8,128)(2,1)S(1)} fusion(bf16[2560,20]{1,0:T(8,128)(2,1)S(1)} %copy.17, bf16[2560,256]{1,0:T(8,128)(2,1)} %param.25), kind=kLoop, calls=%fused_computation.8 | loop fusion | flops 5898240 | bytes 3379200 | tf_op jit(solution)/shard_map/concatenate | solution.py:507
  29.4 2.3 %all-to-all-done = bf16[32,32,640]{2,1,0:T(8,128)(2,1)} async-done(((bf16[32,32,640]{2,1,0:T(8,128)(2,1)}), bf16[32,32,640]{2,1,0:T(8,128)(2,1)}, u32[]{:S(2)}, u32[]{:S(2)}) %all-to-all-start) | async-done | bytes 1310752 | tf_op jit(solution)/shard_map/all_to_all | solution.py:497
  31.8 3.5 %convolution_convert_fusion.x = bf16[512,640]{1,0:T(8,128)(2,1)} fusion(bf16[512,1024]{1,0:T(8,128)(2,1)} %fusion.2, bf16[1024,640]{1,0:T(8,128)(2,1)} %bitcast.5), kind=kOutput, calls=%fused_computation.10 | convolution fusion | flops 671416320 | bytes 3014656 | tf_op jit(solution)/shard_map/dot_general | solution.py:19
  35.2 1.6 %collective-permute-start = (bf16[512,640]{1,0:T(8,128)(2,1)}, bf16[512,640]{1,0:T(8,128)(2,1)S(1)}, u32[]{:S(2)}, u32[]{:S(2)}) collective-permute-start(bf16[512,640]{1,0:T(8,128)(2,1)} %convolution_convert_fusion.x), channel_id=1, source_target_pairs={{0,1},{1,2},{2,3},{3,0},{4,5},{5,6},{6,7},{7,4},{8,9},{9,10},{10,1... | collective-permute-start | bytes 1966088 | tf_op jit(solution)/shard_map/ppermute | solution.py:23
  36.8 1.7 %collective-permute-start.1 = (bf16[512,640]{1,0:T(8,128)(2,1)}, bf16[512,640]{1,0:T(8,128)(2,1)S(1)}, u32[]{:S(2)}, u32[]{:S(2)}) collective-permute-start(bf16[512,640]{1,0:T(8,128)(2,1)} %convolution_convert_fusion.x), channel_id=1, source_target_pairs={{0,3},{1,0},{2,1},{3,2},{4,7},{5,4},{6,5},{7,6},{8,11},{9,8},{10,9... | collective-permute-start | bytes 1966088 | tf_op jit(solution)/shard_map/ppermute | solution.py:23
  38.5 0.8 slice.58
  39.2 1.5 %collective-permute-start.4 = (bf16[16,640]{1,0:T(8,128)(2,1)S(1)}, bf16[16,640]{1,0:T(8,128)(2,1)S(1)}, u32[]{:S(2)}, u32[]{:S(2)}) collective-permute-start(bf16[16,640]{1,0:T(8,128)(2,1)S(1)} %slice.58), channel_id=1, source_target_pairs={{0,4},{4,8},{8,12},{12,16},{16,20},{20,24},{24,28},{28,32},{32,36}... | collective-permute-start | bytes 61448 | tf_op jit(solution)/shard_map/ppermute | solution.py:28
  41.2 0.4 collective-permute-done.4.t
  41.6 0.3 collective-permute-start.5
  41.9 2.9 %collective-permute-start.6 = (bf16[16,640]{1,0:T(8,128)(2,1)S(1)}, bf16[16,640]{1,0:T(8,128)(2,1)S(1)}, u32[]{:S(2)}, u32[]{:S(2)}) collective-permute-start(bf16[16,640]{1,0:T(8,128)(2,1)S(1)} %collective-permute-done.4.t), channel_id=1, source_target_pairs={{0,3},{1,0},{2,1},{3,2},{4,7},{5,4},{6,5},{7,6},{8,11},{9,8},{10,9... | collective-permute-start | bytes 61448 | tf_op jit(solution)/shard_map/ppermute | solution.py:23
  44.8 0.7 collective-permute-start.7
  45.6 4.7 %copy-done.2 = bf16[320,8,2,1280]{3,1,2,0:T(8,128)(2,1)S(1)} copy-done((bf16[320,8,2,1280]{3,1,2,0:T(8,128)(2,1)S(1)}, bf16[320,8,2,1280]{3,1,2,0:T(8,128)(2,1)}, u32[]{:S(2)}) %copy-start.2) | copy-done | bytes 13107224
  50.3 3.8 %own_part.1.before = f32[512,2944]{1,0:T(8,128)S(1)} custom-call(s32[6]{0:T(128)S(1)} %pad_add_fusion.ids, bf16[512,640]{1,0:T(8,128)(2,1)} %convolution_convert_fusion.x, bf16[2560,384]{1,0:T(8,128)(2,1)S(1)} %fusion.3.wsd, bf16[2560,2560]{1,0:T(8,128)(2,1)S(1)} %bitcast.14), custom_call_target="tpu_custom_call" | custom-call | flops 1929379840 | bytes 21757952 | tf_op jit(solution)/shard_map/own_part/pallas_call | solution.py:59
  54.2 1.4 %collective-permute-done.7.t_o = bf16[16,640]{1,0:T(8,128)(2,1)S(1)} collective-permute-done((bf16[16,640]{1,0:T(8,128)(2,1)S(1)}, bf16[16,640]{1,0:T(8,128)(2,1)S(1)}, u32[]{:S(2)}, u32[]{:S(2)}) %collective-permute-start.7) | collective-permute-done | bytes 20512 | tf_op jit(solution)/shard_map/ppermute | solution.py:23
  55.5 1.7 %tail_part.1.tail = f32[16,1536]{1,0:T(8,128)S(1)} custom-call(s32[6]{0:T(128)S(1)} %pad_add_fusion.ids, bf16[16,640]{1,0:T(8,128)(2,1)S(1)} %collective-permute-done.4.t, bf16[16,640]{1,0:T(8,128)(2,1)S(1)} %collective-permute-done.5.t_r, bf16[16,640]{1,0:T(8,128)(2,1)S(1)} %collective-permute-done.6.t_l, bf16[16,640]{1,0:T(8,128)(2,1)S(1)} %collective-permute-done.7.t_o, ...), custom_call_target="tpu_custom_call" | custom-call | flops 2013265920 | bytes 15253504 | tf_op jit(solution)/shard_map/tail_part/pallas_call | solution.py:59
  57.3 1.2 collective-permute-start.2
  58.6 2.3 %collective-permute-start.3 = (bf16[256,640]{1,0:T(8,128)(2,1)S(1)}, bf16[256,640]{1,0:T(8,128)(2,1)S(1)}, u32[]{:S(2)}, u32[]{:S(2)}) collective-permute-start(bf16[256,640]{1,0:T(8,128)(2,1)S(1)} %slice.45), channel_id=1, source_target_pairs={{0,3},{1,0},{2,1},{3,2},{4,7},{5,4},{6,5},{7,6},{8,11},{9,8},{10,9... | collective-permute-start | bytes 983048 | tf_op jit(solution)/shard_map/ppermute | solution.py:23
  60.9 5.5 %next_part.1.acc = f32[512,2944]{1,0:T(8,128)S(1)} custom-call(s32[6]{0:T(128)S(1)} %pad_add_fusion.ids, bf16[512,640]{1,0:T(8,128)(2,1)S(1)} %collective-permute-done.r, bf16[512,640]{1,0:T(8,128)(2,1)S(1)} %collective-permute-done.1.l, bf16[2560,384]{1,0:T(8,128)(2,1)S(1)} %fusion.3.wsd, bf16[2560,2560]{1,0:T(8,128)(2,1)S(1)} %bitcast.16, ...), custom_call_target="tpu_custom_call" | custom-call | flops 3858759680 | bytes 28442624 | tf_op jit(solution)/shard_map/next_part/pallas_call | solution.py:59
  66.5 1.2 collective-permute-done.2.o1
  67.7 6.2 %state_part.1 = (bf16[512,1280]{1,0:T(8,128)(2,1)S(1)}, bf16[512,256]{1,0:T(8,128)(2,1)S(1)}, bf16[512,128]{1,0:T(8,128)(2,1)S(1)}, f32[2,32,256]{2,1,0:T(8,128)...) custom-call(s32[6]{0:T(128)S(1)} %pad_add_fusion.ids, ...), custom_call_target="tpu_custom_call" | custom-call | flops 2181038080 | bytes 25571328 | tf_op jit(solution)/shard_map/state_part/pallas_call | solution.py:59
  73.9 1.3 %collective-permute-start.8 = (bf16[144,1280]{1,0:T(8,128)(2,1)S(1)}, bf16[144,1280]{1,0:T(8,128)(2,1)S(1)}, u32[]{:S(2)}, u32[]{:S(2)}) collective-permute-start(bf16[144,1280]{1,0:T(8,128)(2,1)S(1)} %get-tuple-element.85), channel_id=1, source_target_pairs={{0,4},{4,8},{8,12},{12,16},{16,20},{20,24},{24,28},{28,32},{32,36}... | collective-permute-start | bytes 1105928 | tf_op jit(solution)/shard_map/ppermute | solution.py:28
  75.2 1.3 %collective-permute-done.8.got.got1 = bf16[144,1280]{1,0:T(8,128)(2,1)S(1)} collective-permute-done((bf16[144,1280]{1,0:T(8,128)(2,1)S(1)}, bf16[144,1280]{1,0:T(8,128)(2,1)S(1)}, u32[]{:S(2)}, u32[]{:S(2)}) %collective-permute-start.8) | collective-permute-done | bytes 368672 | tf_op jit(solution)/shard_map/ppermute | solution.py:28
  76.5 0.6 join_part.1
  77.2 9.8 %collective-permute-start.9 = (bf16[128,1280]{1,0:T(8,128)(2,1)S(1)}, bf16[128,1280]{1,0:T(8,128)(2,1)S(1)}, u32[]{:S(2)}, u32[]{:S(2)}) collective-permute-start(bf16[128,1280]{1,0:T(8,128)(2,1)S(1)} %join_part.1), channel_id=1, source_target_pairs={{0,8},{4,12},{8,16},{12,20},{16,24},{20,28},{24,32},{28,36},{32,40... | collective-permute-start | bytes 983048 | tf_op jit(solution)/shard_map/ppermute | solution.py:28
  87.0 7.2 %mix_part.1 = (f32[512,1280]{1,0:T(8,128)S(1)}, f32[512,1280]{1,0:T(8,128)S(1)}) custom-call(s32[6]{0:T(128)S(1)} %pad_add_fusion.ids, bf16[256,640]{1,0:T(8,128)(2,1)S(1)} %collective-permute-done.2.o1, bf16[256,640]{1,0:T(8,128)(2,1)S(1)} %collective-permute-done.3.o2, bf16[2560,2560]{1,0:T(8,128)(2,1)S(1)} %bitcast.18, f32[512,2944]{1,0:T(8,128)S(1)} %next_part.1.acc, ...), custom_call_target="tpu_custom_call" | custom-call | flops 8000000000 | bytes 27041792 | tf_op jit(solution)/shard_map/mix_part/pallas_call | solution.py:59
  94.2 2.4 %gated_part.1 = (bf16[512,1280]{1,0:T(8,128)(2,1)S(1)}, bf16[272,640]{1,0:T(8,128)(2,1)S(1)}, bf16[272,640]{1,0:T(8,128)(2,1)S(1)}, f32[8,512]{1,0:T(8,128)S(1)}) custom-call(s32[6]{0:T(128)S(1)} %pad_add_fusion.ids, f32[512,1280]{1,0:T(8,128)S(1)} %get-tuple-element.83.p, f32[512,1280]{1,0:T(8,128)S(1)} %get-tuple-element.84.q, ...), custom_call_target="tpu_custom_call" | custom-call | flops 1006632960 | bytes 15515648 | tf_op jit(solution)/shard_map/gated_part/pallas_call | solution.py:59
  96.7 1.6 %collective-permute-start.10 = (bf16[272,640]{1,0:T(8,128)(2,1)S(1)}, bf16[272,640]{1,0:T(8,128)(2,1)S(1)}, u32[]{:S(2)}, u32[]{:S(2)}) collective-permute-start(bf16[272,640]{1,0:T(8,128)(2,1)S(1)} %get-tuple-element.92), channel_id=1, source_target_pairs={{0,1},{1,2},{2,3},{3,0},{4,5},{5,6},{6,7},{7,4},{8,9},{9,10},{10,1... | collective-permute-start | bytes 1044488 | tf_op jit(solution)/shard_map/ppermute | solution.py:23
  98.3 1.8 %collective-permute-start.11 = (bf16[272,640]{1,0:T(8,128)(2,1)S(1)}, bf16[272,640]{1,0:T(8,128)(2,1)S(1)}, u32[]{:S(2)}, u32[]{:S(2)}) collective-permute-start(bf16[272,640]{1,0:T(8,128)(2,1)S(1)} %get-tuple-element.94), channel_id=1, source_target_pairs={{0,3},{1,0},{2,1},{3,2},{4,7},{5,4},{6,5},{7,6},{8,11},{9,8},{10,9... | collective-permute-start | bytes 1044488 | tf_op jit(solution)/shard_map/ppermute | solution.py:23
  100.1 2.8 %near_part.1 = (bf16[256,640]{1,0:T(8,128)(2,1)S(1)}, bf16[256,640]{1,0:T(8,128)(2,1)S(1)}, f32[256,640]{1,0:T(8,128)S(1)}, f32[256,640]{1,0:T(8,128)S(1)}) custom-call(s32[6]{0:T(128)S(1)} %pad_add_fusion.ids, bf16[512,1280]{1,0:T(8,128)(2,1)S(1)} %get-tuple-element.90.z, bf16[1280,2560]{1,0:T(8,128)(2,1)S(1)} %bitcast.20), custom_call_target="tpu_custom_call" | custom-call | flops 1677721600 | bytes 9830400 | tf_op jit(solution)/shard_map/near_part/pallas_call | solution.py:59
  102.9 3.9 %collective-permute-done.10.b1.sq_r = bf16[272,640]{1,0:T(8,128)(2,1)S(1)} collective-permute-done((bf16[272,640]{1,0:T(8,128)(2,1)S(1)}, bf16[272,640]{1,0:T(8,128)(2,1)S(1)}, u32[]{:S(2)}, u32[]{:S(2)}) %collective-permute-start.10) | collective-permute-done | bytes 348192 | tf_op jit(solution)/shard_map/ppermute | solution.py:23
  106.9 0.7 add_part.1
  107.6 1.2 collective-permute-start.12
  108.8 1.7 %collective-permute-start.13 = (bf16[256,640]{1,0:T(8,128)(2,1)S(1)}, bf16[256,640]{1,0:T(8,128)(2,1)S(1)}, u32[]{:S(2)}, u32[]{:S(2)}) collective-permute-start(bf16[256,640]{1,0:T(8,128)(2,1)S(1)} %get-tuple-element.96), channel_id=1, source_target_pairs={{0,1},{1,2},{2,3},{3,0},{4,5},{5,6},{6,7},{7,4},{8,9},{9,10},{10,1... | collective-permute-start | bytes 983048 | tf_op jit(solution)/shard_map/ppermute | solution.py:23
  110.5 1.5 %collective-permute-start.14 = (bf16[256,640]{1,0:T(8,128)(2,1)S(1)}, bf16[256,640]{1,0:T(8,128)(2,1)S(1)}, u32[]{:S(2)}, u32[]{:S(2)}) collective-permute-start(bf16[256,640]{1,0:T(8,128)(2,1)S(1)} %get-tuple-element.97), channel_id=1, source_target_pairs={{0,3},{1,0},{2,1},{3,2},{4,7},{5,4},{6,5},{7,6},{8,11},{9,8},{10,9... | collective-permute-start | bytes 983048 | tf_op jit(solution)/shard_map/ppermute | solution.py:23
  112.0 0.9 collective-permute-start.15
  112.9 1.7 %mine_part.1.own = f32[512,640]{1,0:T(8,128)S(1)} custom-call(s32[6]{0:T(128)S(1)} %pad_add_fusion.ids, bf16[512,1280]{1,0:T(8,128)(2,1)S(1)} %get-tuple-element.90.z, bf16[1280,2560]{1,0:T(8,128)(2,1)S(1)} %bitcast.20), custom_call_target="tpu_custom_call" | custom-call | flops 838860800 | bytes 9175040 | tf_op jit(solution)/shard_map/mine_part/pallas_call | solution.py:59
  114.6 9.2 %collective-permute-done.13.low_r = bf16[256,640]{1,0:T(8,128)(2,1)S(1)} collective-permute-done((bf16[256,640]{1,0:T(8,128)(2,1)S(1)}, bf16[256,640]{1,0:T(8,128)(2,1)S(1)}, u32[]{:S(2)}, u32[]{:S(2)}) %collective-permute-start.13) | collective-permute-done | bytes 327712 | tf_op jit(solution)/shard_map/ppermute | solution.py:23
  123.8 0.2 collective-permute-done.15.low_l
  124.0 1.7 %final_part.1 = bf16[512,640]{1,0:T(8,128)(2,1)} custom-call(s32[6]{0:T(128)S(1)} %pad_add_fusion.ids, f32[512,640]{1,0:T(8,128)S(1)} %mine_part.1.own, bf16[272,640]{1,0:T(8,128)(2,1)S(1)} %collective-permute-done.12.top_r, bf16[256,640]{1,0:T(8,128)(2,1)S(1)} %collective-permute-done.13.low_r, bf16[256,640]{1,0:T(8,128)(2,1)S(1)} %collective-permute-done.14.top_l, ...), custom_call_target="tpu_custom_call" | custom-call | flops 1310720 | bytes 4009984 | tf_op jit(solution)/shard_map/final_part/pallas_call | solution.py:59
  (59 shorter events, 1.2 us)
Async XLA Ops:
  0.0 1.1 copy-start
  3.3 8.5 %copy-start.8 = (s32[32,32]{1,0:T(8,128)S(1)}, s32[32,32]{1,0:T(8,128)}, u32[]{:S(2)}) copy-start(s32[32,32]{1,0:T(8,128)} %param.22) | copy-start | bytes 12292
  3.3 28.4 %all-to-all-start = ((bf16[32,32,640]{2,1,0:T(8,128)(2,1)}), bf16[32,32,640]{2,1,0:T(8,128)(2,1)}, u32[]{:S(2)}, u32[]{:S(2)}) async-start(bf16[32,32,640]{2,1,0:T(8,128)(2,1)} %bitcast.4), calls=%async_computation | async-start | bytes 2621440 | tf_op jit(solution)/shard_map/all_to_all | solution.py:497
  12.2 12.5 %copy-start.7 = (bf16[2560,20]{0,1:T(8,128)(2,1)S(1)}, bf16[2560,20]{0,1:T(8,128)(2,1)}, u32[]{:S(2)}) copy-start(bf16[2560,20]{0,1:T(8,128)(2,1)} %param.26) | copy-start | bytes 307204
  12.2 12.9 %copy-start.6 = (s32[64]{0:T(128)S(1)}, s32[64]{0:T(128)}, u32[]{:S(2)}) copy-start(s32[64]{0:T(128)} %param.23) | copy-start | bytes 772
  31.7 6.7 %copy-start.12 = (f32[20]{0:T(128)S(1)}, f32[20]{0:T(128)}, u32[]{:S(2)}) copy-start(f32[20]{0:T(128)} %param.30) | copy-start | bytes 244
  31.7 9.1 %copy-start.10 = (f32[20]{0:T(128)S(1)}, f32[20]{0:T(128)}, u32[]{:S(2)}) copy-start(f32[20]{0:T(128)} %param.31) | copy-start | bytes 244
  31.7 9.2 %copy-start.11 = (f32[20]{0:T(128)S(1)}, f32[20]{0:T(128)}, u32[]{:S(2)}) copy-start(f32[20]{0:T(128)} %param.29) | copy-start | bytes 244
  35.2 22.0 %collective-permute-start = (bf16[512,640]{1,0:T(8,128)(2,1)}, bf16[512,640]{1,0:T(8,128)(2,1)S(1)}, u32[]{:S(2)}, u32[]{:S(2)}) collective-permute-start(bf16[512,640]{1,0:T(8,128)(2,1)} %convolution_convert_fusion.x), channel_id=1, source_target_pairs={{0,1},{1,2},{2,3},{3,0},{4,5},{5,6},{6,7},{7,4},{8,9},{9,10},{10,1... | collective-permute-start | bytes 1966088 | tf_op jit(solution)/shard_map/ppermute | solution.py:23
  36.8 20.4 %collective-permute-start.1 = (bf16[512,640]{1,0:T(8,128)(2,1)}, bf16[512,640]{1,0:T(8,128)(2,1)S(1)}, u32[]{:S(2)}, u32[]{:S(2)}) collective-permute-start(bf16[512,640]{1,0:T(8,128)(2,1)} %convolution_convert_fusion.x), channel_id=1, source_target_pairs={{0,3},{1,0},{2,1},{3,2},{4,7},{5,4},{6,5},{7,6},{8,11},{9,8},{10,9... | collective-permute-start | bytes 1966088 | tf_op jit(solution)/shard_map/ppermute | solution.py:23
  39.2 2.3 %collective-permute-start.4 = (bf16[16,640]{1,0:T(8,128)(2,1)S(1)}, bf16[16,640]{1,0:T(8,128)(2,1)S(1)}, u32[]{:S(2)}, u32[]{:S(2)}) collective-permute-start(bf16[16,640]{1,0:T(8,128)(2,1)S(1)} %slice.58), channel_id=1, source_target_pairs={{0,4},{4,8},{8,12},{12,16},{16,20},{20,24},{24,28},{28,32},{32,36}... | collective-permute-start | bytes 61448 | tf_op jit(solution)/shard_map/ppermute | solution.py:28
  41.6 12.5 %collective-permute-start.5 = (bf16[16,640]{1,0:T(8,128)(2,1)S(1)}, bf16[16,640]{1,0:T(8,128)(2,1)S(1)}, u32[]{:S(2)}, u32[]{:S(2)}) collective-permute-start(bf16[16,640]{1,0:T(8,128)(2,1)S(1)} %collective-permute-done.4.t), channel_id=1, source_target_pairs={{0,1},{1,2},{2,3},{3,0},{4,5},{5,6},{6,7},{7,4},{8,9},{9,10},{10,1... | collective-permute-start | bytes 61448 | tf_op jit(solution)/shard_map/ppermute | solution.py:23
  41.9 12.3 %collective-permute-start.6 = (bf16[16,640]{1,0:T(8,128)(2,1)S(1)}, bf16[16,640]{1,0:T(8,128)(2,1)S(1)}, u32[]{:S(2)}, u32[]{:S(2)}) collective-permute-start(bf16[16,640]{1,0:T(8,128)(2,1)S(1)} %collective-permute-done.4.t), channel_id=1, source_target_pairs={{0,3},{1,0},{2,1},{3,2},{4,7},{5,4},{6,5},{7,6},{8,11},{9,8},{10,9... | collective-permute-start | bytes 61448 | tf_op jit(solution)/shard_map/ppermute | solution.py:23
  44.8 10.7 %collective-permute-start.7 = (bf16[16,640]{1,0:T(8,128)(2,1)S(1)}, bf16[16,640]{1,0:T(8,128)(2,1)S(1)}, u32[]{:S(2)}, u32[]{:S(2)}) collective-permute-start(bf16[16,640]{1,0:T(8,128)(2,1)S(1)} %collective-permute-done.4.t), channel_id=1, source_target_pairs={{0,2},{1,3},{2,0},{3,1},{4,6},{5,7},{6,4},{7,5},{8,10},{9,11},{10,... | collective-permute-start | bytes 61448 | tf_op jit(solution)/shard_map/ppermute | solution.py:23
  45.5 4.7 %copy-start.2 = (bf16[320,8,2,1280]{3,1,2,0:T(8,128)(2,1)S(1)}, bf16[320,8,2,1280]{3,1,2,0:T(8,128)(2,1)}, u32[]{:S(2)}) copy-start(bf16[320,8,2,1280]{3,1,2,0:T(8,128)(2,1)} %copy.18) | copy-start | bytes 39321604
  50.3 5.3 %copy-start.3 = (bf16[320,8,2,1280]{3,1,2,0:T(8,128)(2,1)S(1)}, bf16[320,8,2,1280]{3,1,2,0:T(8,128)(2,1)}, u32[]{:S(2)}) copy-start(bf16[320,8,2,1280]{3,1,2,0:T(8,128)(2,1)} %copy.18) | copy-start | bytes 39321604
  57.3 10.4 %collective-permute-start.2 = (bf16[256,640]{1,0:T(8,128)(2,1)S(1)}, bf16[256,640]{1,0:T(8,128)(2,1)S(1)}, u32[]{:S(2)}, u32[]{:S(2)}) collective-permute-start(bf16[256,640]{1,0:T(8,128)(2,1)S(1)} %slice.44), channel_id=1, source_target_pairs={{0,1},{1,2},{2,3},{3,0},{4,5},{5,6},{6,7},{7,4},{8,9},{9,10},{10,1... | collective-permute-start | bytes 983048 | tf_op jit(solution)/shard_map/ppermute | solution.py:23
  58.5 9.1 %copy-start.9 = (f32[1280]{0:T(1024)S(1)}, f32[1280]{0:T(1024)}, u32[]{:S(2)}) copy-start(f32[1280]{0:T(1024)} %param.32) | copy-start | bytes 15364
  58.5 9.1 %copy-start.4 = (f32[4,1280]{1,0:T(4,128)S(1)}, f32[4,1280]{1,0:T(4,128)}, u32[]{:S(2)}) copy-start(f32[4,1280]{1,0:T(4,128)} %taps_v.1) | copy-start | bytes 61444
  58.6 9.1 %copy-start.5 = (f32[4,256]{1,0:T(4,128)S(1)}, f32[4,256]{1,0:T(4,128)}, u32[]{:S(2)}) copy-start(f32[4,256]{1,0:T(4,128)} %taps_s.1) | copy-start | bytes 12292
  58.6 9.1 %collective-permute-start.3 = (bf16[256,640]{1,0:T(8,128)(2,1)S(1)}, bf16[256,640]{1,0:T(8,128)(2,1)S(1)}, u32[]{:S(2)}, u32[]{:S(2)}) collective-permute-start(bf16[256,640]{1,0:T(8,128)(2,1)S(1)} %slice.45), channel_id=1, source_target_pairs={{0,3},{1,0},{2,1},{3,2},{4,7},{5,4},{6,5},{7,6},{8,11},{9,8},{10,9... | collective-permute-start | bytes 983048 | tf_op jit(solution)/shard_map/ppermute | solution.py:23
  73.9 2.6 %collective-permute-start.8 = (bf16[144,1280]{1,0:T(8,128)(2,1)S(1)}, bf16[144,1280]{1,0:T(8,128)(2,1)S(1)}, u32[]{:S(2)}, u32[]{:S(2)}) collective-permute-start(bf16[144,1280]{1,0:T(8,128)(2,1)S(1)} %get-tuple-element.85), channel_id=1, source_target_pairs={{0,4},{4,8},{8,12},{12,16},{16,20},{20,24},{24,28},{28,32},{32,36}... | collective-permute-start | bytes 1105928 | tf_op jit(solution)/shard_map/ppermute | solution.py:28
  77.2 17.0 %collective-permute-start.9 = (bf16[128,1280]{1,0:T(8,128)(2,1)S(1)}, bf16[128,1280]{1,0:T(8,128)(2,1)S(1)}, u32[]{:S(2)}, u32[]{:S(2)}) collective-permute-start(bf16[128,1280]{1,0:T(8,128)(2,1)S(1)} %join_part.1), channel_id=1, source_target_pairs={{0,8},{4,12},{8,16},{12,20},{16,24},{20,28},{24,32},{28,36},{32,40... | collective-permute-start | bytes 983048 | tf_op jit(solution)/shard_map/ppermute | solution.py:28
  86.9 7.3 %slice-start = ((s8[6553600]{0:T(1024)(128)(4,1)}), s8[4194304]{0:T(1024)(128)(4,1)S(1)}, s32[]{:S(2)}) async-start(s8[6553600]{0:T(1024)(128)(4,1)} %bitcast.19), calls=%async_computation.1 | async-start | bytes 8388608
  86.9 7.3 %slice-start.1 = ((s8[6553600]{0:T(1024)(128)(4,1)}), s8[2359296]{0:T(1024)(128)(4,1)S(1)}, s32[]{:S(2)}) async-start(s8[6553600]{0:T(1024)(128)(4,1)} %bitcast.19), calls=%async_computation.2 | async-start | bytes 4718592
  96.7 10.2 %collective-permute-start.10 = (bf16[272,640]{1,0:T(8,128)(2,1)S(1)}, bf16[272,640]{1,0:T(8,128)(2,1)S(1)}, u32[]{:S(2)}, u32[]{:S(2)}) collective-permute-start(bf16[272,640]{1,0:T(8,128)(2,1)S(1)} %get-tuple-element.92), channel_id=1, source_target_pairs={{0,1},{1,2},{2,3},{3,0},{4,5},{5,6},{6,7},{7,4},{8,9},{9,10},{10,1... | collective-permute-start | bytes 1044488 | tf_op jit(solution)/shard_map/ppermute | solution.py:23
  98.3 8.6 %collective-permute-start.11 = (bf16[272,640]{1,0:T(8,128)(2,1)S(1)}, bf16[272,640]{1,0:T(8,128)(2,1)S(1)}, u32[]{:S(2)}, u32[]{:S(2)}) collective-permute-start(bf16[272,640]{1,0:T(8,128)(2,1)S(1)} %get-tuple-element.94), channel_id=1, source_target_pairs={{0,3},{1,0},{2,1},{3,2},{4,7},{5,4},{6,5},{7,6},{8,11},{9,8},{10,9... | collective-permute-start | bytes 1044488 | tf_op jit(solution)/shard_map/ppermute | solution.py:23
  107.6 16.5 %collective-permute-start.12 = (bf16[272,640]{1,0:T(8,128)(2,1)S(1)}, bf16[272,640]{1,0:T(8,128)(2,1)S(1)}, u32[]{:S(2)}, u32[]{:S(2)}) collective-permute-start(bf16[272,640]{1,0:T(8,128)(2,1)S(1)} %get-tuple-element.95), channel_id=1, source_target_pairs={{0,1},{1,2},{2,3},{3,0},{4,5},{5,6},{6,7},{7,4},{8,9},{9,10},{10,1... | collective-permute-start | bytes 1044488 | tf_op jit(solution)/shard_map/ppermute | solution.py:23
  108.8 15.0 %collective-permute-start.13 = (bf16[256,640]{1,0:T(8,128)(2,1)S(1)}, bf16[256,640]{1,0:T(8,128)(2,1)S(1)}, u32[]{:S(2)}, u32[]{:S(2)}) collective-permute-start(bf16[256,640]{1,0:T(8,128)(2,1)S(1)} %get-tuple-element.96), channel_id=1, source_target_pairs={{0,1},{1,2},{2,3},{3,0},{4,5},{5,6},{6,7},{7,4},{8,9},{9,10},{10,1... | collective-permute-start | bytes 983048 | tf_op jit(solution)/shard_map/ppermute | solution.py:23
  110.5 13.3 %collective-permute-start.14 = (bf16[256,640]{1,0:T(8,128)(2,1)S(1)}, bf16[256,640]{1,0:T(8,128)(2,1)S(1)}, u32[]{:S(2)}, u32[]{:S(2)}) collective-permute-start(bf16[256,640]{1,0:T(8,128)(2,1)S(1)} %get-tuple-element.97), channel_id=1, source_target_pairs={{0,3},{1,0},{2,1},{3,2},{4,7},{5,4},{6,5},{7,6},{8,11},{9,8},{10,9... | collective-permute-start | bytes 983048 | tf_op jit(solution)/shard_map/ppermute | solution.py:23
  112.0 12.0 %collective-permute-start.15 = (bf16[256,640]{1,0:T(8,128)(2,1)S(1)}, bf16[256,640]{1,0:T(8,128)(2,1)S(1)}, u32[]{:S(2)}, u32[]{:S(2)}) collective-permute-start(bf16[256,640]{1,0:T(8,128)(2,1)S(1)} %get-tuple-element.98), channel_id=1, source_target_pairs={{0,3},{1,0},{2,1},{3,2},{4,7},{5,4},{6,5},{7,6},{8,11},{9,8},{10,9... | collective-permute-start | bytes 983048 | tf_op jit(solution)/shard_map/ppermute | solution.py:23
  124.0 1.7 %copy-start.1 = (bf16[512,640]{1,0:T(8,128)(2,1)S(1)}, bf16[512,640]{1,0:T(8,128)(2,1)}, u32[]{:S(2)}) copy-start(bf16[512,640]{1,0:T(8,128)(2,1)} %param.20) | copy-start | bytes 1966084

commit v3 on v2

v3 whole, which is shorter than its diff:
```python
import jax
import jax.numpy as jnp
from jax import lax
from jax.experimental import pallas as pl
from jax.experimental.pallas import tpu as pltpu
from jax.sharding import PartitionSpec as P

BF = jnp.bfloat16
F32 = jnp.float32
STRETCH = 256
TAIL = 16
TILE = 256
LOG2E = 1.4426950408889634
RING = 4
VMEM = 16 * 1024 * 1024


def dot(a, b):
    return jnp.dot(a, b, preferred_element_type=F32)


def turned(value, steps):
    return lax.ppermute(value, "head", [(i, (i + steps) % RING) for i in range(RING)])


def shifted(value, steps):
    count = lax.axis_size("ctx")
    return lax.ppermute(value, "ctx", [(i, i + steps) for i in range(count - steps)])


def silu(v):
    return v * (1.0 / (1.0 + jnp.exp(-v)))


def split3(x):
    high = x.astype(BF).astype(F32)
    rest = x - high
    mid = rest.astype(BF).astype(F32)
    low = (rest - mid).astype(BF).astype(F32)
    return high, mid, low


def pack3(x):
    high, mid, low = split3(x)
    return (high + pltpu.roll(mid, 32, 1) + pltpu.roll(low, 64, 1)).astype(BF)


def spread(tile, width):
    lane = lax.broadcasted_iota(jnp.int32, (128, width), 0)
    col = lax.broadcasted_iota(jnp.int32, (128, width), 1)
    hit = ((lane & 31) == tile * (width // 64) + (col >> 6)) & (lane < 96)
    return jnp.where(hit, 1.0, 0.0).astype(BF)


def call(body, outs, args, name, flops, exps=0, scratch=()):
    size = sum(a.size * a.dtype.itemsize for a in args[1:]) + sum(
        o.size * o.dtype.itemsize for o in outs
    )
    return pl.pallas_call(
        body,
        in_specs=[pl.BlockSpec(memory_space=pltpu.SMEM)]
        + [pl.BlockSpec(memory_space=pltpu.VMEM)] * (len(args) - 1),
        out_specs=[pl.BlockSpec(memory_space=pltpu.VMEM)] * len(outs),
        out_shape=outs,
        scratch_shapes=scratch,
        compiler_params=pltpu.CompilerParams(vmem_limit_bytes=VMEM),
        cost_estimate=pl.CostEstimate(
            flops=int(flops), bytes_accessed=int(size), transcendentals=int(exps)
        ),
        name=name,
    )(*args)


def shape(dims, dtype=F32):
    return jax.ShapeDtypeStruct(dims, dtype)


def chunk_of(ids, at, k):
    return pl.ds(pl.multiple_of(ids[at] * k, 128), k)


def wide(j):
    return slice(j * TILE, (j + 1) * TILE)


def block_rows(block):
    return slice(block * STRETCH, (block + 1) * STRETCH)


def flat_body(ids, w, out):
    k = w.shape[0]
    for low in range(0, k, STRETCH):
        rows = slice(low, low + STRETCH)
        out[rows, :] = w[rows].reshape(STRETCH, out.shape[1])


def flat_part(ids, w):
    out = shape((w.shape[0], 2 * w.shape[2]), BF)
    return call(flat_body, [out], (ids, w), "flat_part", 1e9)[0]


CUT = STRETCH - TAIL


def arrange_body(ids, target, arrived, second, first, last):
    slots = arrived.shape[0]
    for low, high in ((CUT, 2 * STRETCH), (0, CUT)):
        row = lax.broadcasted_iota(jnp.int32, (high - low, slots), 0) + low
        pick = jnp.where(row == target[...], 1.0, 0.0).astype(BF)
        rows = dot(pick, arrived[...]).astype(BF)
        if low:
            second[...] = rows
            last[...] = rows[high - low - TAIL :, :]
        else:
            first[...] = rows


def arrange_part(ids, target, arrived):
    slots, k = arrived.shape
    return call(
        arrange_body,
        [shape((STRETCH + TAIL, k), BF), shape((CUT, k), BF), shape((TAIL, k), BF)],
        (ids, target, arrived),
        "arrange_part",
        2 * 512 * slots * k,
    )


def own_body(ids, x, sp, tp, wm, acc):
    at = chunk_of(ids, 0, x.shape[1])
    acc[:, 2560:2816] = dot(x[...], sp[at, :])
    acc[:, 2816 : 2816 + tp.shape[1]] = dot(x[...], tp[at, :])
    for j in range(10):
        acc[:, wide(j)] = dot(x[...], wm[at, wide(j)])


def own_part(ids, x, sp, tp, wm):
    rows, k = x.shape
    n = 2944
    return call(own_body, [shape((rows, n))], (ids, x, sp, tp, wm), "own_part", 2 * rows * k * n)[0]


def next_body(ids, r, l, sp, tp, wm, before, acc):
    k = r.shape[1]
    at_r, at_l = chunk_of(ids, 1, k), chunk_of(ids, 2, k)
    c = slice(2560, 2816)
    acc[:, c] = before[:, c] + dot(r[...], sp[at_r, :]) + dot(l[...], sp[at_l, :])
    c = slice(2816, 2816 + tp.shape[1])
    acc[:, c] = before[:, c] + dot(r[...], tp[at_r, :]) + dot(l[...], tp[at_l, :])
    for j in range(10):
        c = wide(j)
        acc[:, c] = before[:, c] + dot(r[...], wm[at_r, c]) + dot(l[...], wm[at_l, c])


def next_part(ids, r, l, sp, tp, wm, acc):
    rows, k = r.shape
    n = acc.shape[1]
    return call(
        next_body, [shape((rows, n))], (ids, r, l, sp, tp, wm, acc), "next_part", 4 * rows * k * n
    )[0]


def rounded(x):
    return x.astype(BF).astype(F32)


def conv_silu(xs, taps):
    total = None
    for k in range(4):
        term = xs[5 + k : 5 + k + STRETCH, :] * taps[k : k + 1, :]
        total = term if total is None else total + term
    return silu(total).astype(BF)


def step_rows(row, value):
    high, mid, low = split3(value)
    return jnp.where(row == 0, high, jnp.where(row == 1, mid, jnp.where(row == 2, low, 0.0)))


def decays(raw, heads, cum3, cum_t, step_t, ecum3):
    lane = lax.broadcasted_iota(jnp.int32, (STRETCH, 128), 1)
    row_id = lax.broadcasted_iota(jnp.int32, (STRETCH, STRETCH), 0)
    col_id = lax.broadcasted_iota(jnp.int32, (STRETCH, STRETCH), 1)
    below = jnp.where(row_id >= col_id, 1.0, 0.0).astype(BF)
    raw = jnp.where(lane < 20, raw, 0.0) + heads[0:1, :]
    small = jnp.exp(-jnp.abs(raw))
    one = 1.0 + small
    log_one = jnp.where(one == 1.0, small, jnp.log(one) * (small / (one - 1.0 + 1e-30)))
    step = jnp.where(lane < 20, jnp.maximum(raw, 0.0) + log_one, 0.0)
    sums = dot(below, pack3(step * (heads[1:2, :] * (-LOG2E))))
    sums = sums + pltpu.roll(sums, 96, 1) + pltpu.roll(sums, 64, 1)
    sums = jnp.where(lane < 32, sums, 0.0)
    final = sums[STRETCH - 1 : STRETCH, :]
    cum3[...] = pack3(sums)
    cum_t[...] = jnp.transpose(sums)[:32]
    step_t[...] = jnp.transpose(step)[:32]
    ecum3[...] = pack3(jnp.where(lane < 32, jnp.exp2(sums), 0.0))
    weights = pack3(jnp.exp2(final - sums) * step)
    ends = pack3(jnp.broadcast_to(jnp.where(lane[:1] < 32, jnp.exp2(final), 0.0), (16, 128)))
    return weights, ends


def second_body(
    ids, o1, o2, sp, tp, wm, acc, taps_s, taps_v, heads,
    act, bc, cum3, cum_t, step_t, ecum3, payload, mid, mid_step, xs,
):
    k = o1.shape[1]
    n1 = o1.shape[0]
    at = chunk_of(ids, 3, k)

    def channels(slot, c, w):
        buf = xs.at[slot]
        first = rounded(acc[:n1, c] + dot(o1[...], w))
        buf[8 : n1 - 8, :] = first[TAIL:, :]
        buf[:8, :] = jnp.where(ids[5] > 0, first[8:TAIL, :], 0.0)
        buf[n1 - 8 : STRETCH + 8, :] = rounded(acc[n1:, c] + dot(o2[...], w))
        return buf, first[:TAIL, :]

    buf, edge = channels(0, slice(2560, 2816), sp[at, :])
    mid[:, 1280:] = edge
    bc[...] = conv_silu(buf, taps_s)
    bt = jnp.transpose(bc[:, :128].astype(F32)).astype(BF)
    n = tp.shape[1]
    buf = xs.at[3]
    buf[:n1, :n] = acc[:n1, 2816 : 2816 + n] + dot(o1[...], tp[at, :])
    buf[n1:, :n] = acc[n1:, 2816 : 2816 + n] + dot(o2[...], tp[at, :])
    mid_step[...] = buf[:TAIL, :128]
    weights, ends = decays(buf[TAIL : TAIL + STRETCH, :128], heads, cum3, cum_t, step_t, ecum3)
    carry = jnp.where(ids[5] > 0, 1.0, 0.0)
    row = lax.broadcasted_iota(jnp.int32, (16, TILE), 0)
    for j in range(5):
        c = wide(j)
        buf, edge = channels(1 + j % 2, wide(5 + j), wm[at, wide(5 + j)])
        mid[:, c] = edge
        value = conv_silu(buf, taps_v[:, c])
        act[:, c] = value
        select = spread(j, TILE)
        weighted = (value.astype(F32) * dot(weights, select)).astype(BF)
        payload[:128, c] = dot(bt, weighted).astype(BF)
        payload[128:, c] = step_rows(row, dot(ends, select) * carry).astype(BF)


def block_outs():
    return [
        shape((STRETCH, 1280), BF),
        shape((STRETCH, 256), BF),
        shape((STRETCH, 128), BF),
        shape((32, STRETCH)),
        shape((32, STRETCH)),
        shape((STRETCH, 128), BF),
    ]


def second_part(ids, o1, o2, sp, tp, wm, acc, taps_s, taps_v, heads):
    return call(
        second_body,
        block_outs() + [shape((144, 1280), BF), shape((TAIL, 1536)), shape((TAIL, 128))],
        (ids, o1, o2, sp, tp, wm, acc, taps_s, taps_v, heads),
        "second_part",
        4 * STRETCH * 640 * 1664,
        scratch=[pltpu.VMEM((4, STRETCH + TAIL, TILE), F32)],
    )


def first_body(
    ids, o1, o2, sp, tp, wm, acc, taps_s, taps_v, heads, mid, mid_step, got,
    act, bc, cum3, cum_t, step_t, ecum3, joined, joined_low, state0, end_row, xs,
):
    k = o1.shape[1]
    n1 = o1.shape[0]
    at = chunk_of(ids, 3, k)

    def channels(slot, c, w, edge):
        buf = xs.at[slot]
        first = rounded(acc[:n1, c] + dot(o1[...], w))
        buf[8 : n1 - 8, :] = first[TAIL:, :]
        buf[:8, :] = jnp.where(ids[4] > 0, first[8:TAIL, :], 0.0)
        buf[n1 - 8 : STRETCH - 8, :] = rounded(acc[n1:, c] + dot(o2[...], w))
        buf[STRETCH - 8 : STRETCH + 8, :] = edge
        return buf

    buf = channels(0, slice(2560, 2816), sp[at, :], mid[:, 1280:])
    bc[...] = conv_silu(buf, taps_s)
    bt = jnp.transpose(bc[:, :128].astype(F32)).astype(BF)
    n = tp.shape[1]
    buf = xs.at[3]
    buf[:n1, :n] = acc[:n1, 2816 : 2816 + n] + dot(o1[...], tp[at, :])
    buf[n1:STRETCH, :n] = acc[n1:, 2816 : 2816 + n] + dot(o2[...], tp[at, :])
    buf[STRETCH:, :128] = mid_step[...]
    weights, ends = decays(buf[TAIL : TAIL + STRETCH, :128], heads, cum3, cum_t, step_t, ecum3)
    carry = jnp.where(ids[4] > 0, 1.0, 0.0)
    row = lax.broadcasted_iota(jnp.int32, (16, TILE), 0)
    for j in range(5):
        c = wide(j)
        buf = channels(1 + j % 2, wide(5 + j), wm[at, wide(5 + j)], mid[:, c])
        value = conv_silu(buf, taps_v[:, c])
        act[:, c] = value
        select = spread(j, TILE)
        weighted = (value.astype(F32) * dot(weights, select)).astype(BF)
        state = dot(bt, weighted)
        end = dot(ends, select)
        state0[:, c] = state
        end_row[:, c] = end[:8, :]
        decay = end[0:1, :] * carry
        more = got[128:, c].astype(F32)
        before = more[0:1, :] + more[1:2, :] + more[2:3, :]
        low = (state + decay * got[:128, c].astype(F32)).astype(BF)
        joined[:128, c] = low
        joined_low[:, c] = low
        joined[128:, c] = step_rows(row, decay * before).astype(BF)


def first_part(ids, o1, o2, sp, tp, wm, acc, taps_s, taps_v, heads, mid, mid_step, got):
    return call(
        first_body,
        block_outs()
        + [shape((144, 1280), BF), shape((128, 1280), BF), shape((128, 1280)), shape((8, 1280))],
        (ids, o1, o2, sp, tp, wm, acc, taps_s, taps_v, heads, mid, mid_step, got),
        "first_part",
        4 * STRETCH * 640 * 1664,
        scratch=[pltpu.VMEM((4, STRETCH + TAIL, TILE), F32)],
    )


def mix_body(
    ids, a1, a2, b1, b2, wm, acc0, acc1, heads,
    act0, bc0, cum30, cum_t0, step_t0, ecum30,
    act1, bc1, cum31, cum_t1, step_t1, ecum31,
    p_out, q_out, sc, xo,
):
    k = a1.shape[1]
    at = chunk_of(ids, 3, k)
    low = 0
    for piece in (a1[TAIL:, :], a2[...], b1[...], b2[...]):
        xo[low : low + piece.shape[0], :] = piece
        low += piece.shape[0]
    row_id = lax.broadcasted_iota(jnp.int32, (STRETCH, STRETCH), 0)
    col_id = lax.broadcasted_iota(jnp.int32, (STRETCH, STRETCH), 1)
    for block, bc in ((0, bc0), (1, bc1)):
        scores = lax.dot_general(
            bc[:, 128:], bc[:, :128], (((1,), (1,)), ((), ())), preferred_element_type=F32
        )
        sc[block] = jnp.where(row_id >= col_id, scores, 0.0)
    half = STRETCH // 2
    heads3 = pack3(heads[...])

    def one(i, _):
        c = pl.ds(pl.multiple_of(i * TILE, TILE), TILE)
        select = spread(i, TILE)
        skip = dot(heads3, select)[2:3, :]
        lane = lax.broadcasted_iota(jnp.int32, (128, STRETCH), 0)
        group = lax.broadcasted_iota(jnp.int32, (STRETCH, TILE), 1) >> 6
        for block, act, cum3, cum_t, step_t, ecum3 in (
            (1, act1, cum31, cum_t1, step_t1, ecum31),
            (0, act0, cum30, cum_t0, step_t0, ecum30),
        ):
            rows = block_rows(block)
            if block:
                gate = acc1[TAIL:, c]
            else:
                gate = jnp.concatenate([acc0[TAIL:, c], acc1[:TAIL, c]], axis=0)
            gate = silu(rounded(gate + dot(xo[rows, :], wm[at, c])))
            values = act[:, c]
            top = jnp.zeros((half, TILE), F32)
            bottom = jnp.zeros((half, TILE), F32)
            for j in range(TILE // 64):
                h = i * (TILE // 64) + j
                pick = jnp.where(((lane & 31) == h) & (lane < 96), 1.0, 0.0).astype(BF)
                cum = dot(cum3[...], pick)
                cum_s = cum_t[pl.ds(h, 1), :]
                step_s = step_t[pl.ds(h, 1), :]
                mine = jnp.where(group == j, values, jnp.zeros_like(values))
                m_top = (
                    sc[block, :half, :half]
                    * jnp.exp2(jnp.minimum(cum[:half, :half] - cum_s[:, :half], 0.0))
                    * step_s[:, :half]
                ).astype(BF)
                m_bottom = (
                    sc[block, half:, :]
                    * jnp.exp2(jnp.minimum(cum[half:, :] - cum_s, 0.0))
                    * step_s
                ).astype(BF)
                top = top + dot(m_top, mine[:half, :])
                bottom = bottom + dot(m_bottom, mine)
            within = jnp.concatenate([top, bottom], axis=0)
            p_out[rows, c] = (within + skip * values.astype(F32)) * gate
            q_out[rows, c] = dot(ecum3[...], select) * gate
        return 0

    lax.fori_loop(0, act0.shape[1] // TILE, one, 0)


def mix_part(ids, a1, a2, b1, b2, wm, acc0, acc1, heads, block0, block1):
    tok = 2 * STRETCH
    return call(
        mix_body,
        [shape((tok, 1280))] * 2,
        (ids, a1, a2, b1, b2, wm, acc0, acc1, heads, *block0, *block1),
        "mix_part",
        8e9,
        exps=20 * 512 * 256,
        scratch=[pltpu.VMEM((2, STRETCH, STRETCH), F32), pltpu.VMEM((tok, a1.shape[1]), BF)],
    )


def gated_body(
    ids, p, q, bc0, bc1, got_s, got_v, got_w, state0, end_row, gain, wo,
    z, far_r, far_l, dir_r, dir_l, squares,
):
    carry0 = jnp.where(ids[4] > 0, 1.0, 0.0)
    carry1 = jnp.where(ids[5] > 0, 1.0, 0.0)
    sums = [None, None]
    for j in range(5):
        c = wide(j)
        more = got_s[128:, c].astype(F32)
        decay1 = more[0:1, :] + more[1:2, :] + more[2:3, :]
        more = got_v[128:, c].astype(F32)
        decay2 = more[0:1, :] + more[1:2, :] + more[2:3, :]
        entering = got_s[:128, c].astype(F32) + decay1 * (
            got_v[:128, c].astype(F32) + decay2 * got_w[:, c].astype(F32)
        )
        start0 = entering * carry0
        start1 = (end_row[0:1, c] * start0 + state0[:, c]) * carry1
        for block, start, bc in ((0, start0, bc0), (1, start1, bc1)):
            rows = block_rows(block)
            from_start = dot(bc[:, 128:], start.astype(BF))
            gated = p[rows, c] + q[rows, c] * from_start
            square = gated * gated
            square = square[:, :128] + square[:, 128:]
            sums[block] = square if sums[block] is None else sums[block] + square
            z[rows, c] = (gated * gain[0:1, c]).astype(BF)
    ncol = wo.shape[1] // RING
    top, low = block_rows(0), block_rows(1)
    far_r[:STRETCH, :] = dot(z[top, :], wo[:, chunk_of(ids, 3, ncol)]).astype(BF)
    far_l[:STRETCH, :] = dot(z[low, :], wo[:, chunk_of(ids, 3, ncol)]).astype(BF)
    dir_r[...] = dot(z[low, :], wo[:, chunk_of(ids, 2, ncol)]).astype(BF)
    dir_l[...] = dot(z[top, :], wo[:, chunk_of(ids, 1, ncol)]).astype(BF)
    row = lax.broadcasted_iota(jnp.int32, (16, STRETCH), 0)
    for block in range(2):
        c = block_rows(block)
        flat = jnp.sum(jnp.transpose(sums[block]), axis=0, keepdims=True)
        squares[:, c] = jnp.broadcast_to(flat, (8, STRETCH))
        packed = step_rows(row, flat).astype(BF)
        far_r[STRETCH:, c] = packed
        far_l[STRETCH:, c] = packed
    far_r[STRETCH:, 512:] = jnp.zeros((16, ncol - 512), BF)
    far_l[STRETCH:, 512:] = jnp.zeros((16, ncol - 512), BF)


def gated_part(ids, p, q, bc0, bc1, got_s, got_v, got_w, state0, end_row, gain, wo):
    tok, nv = p.shape
    ncol = wo.shape[1] // RING
    return call(
        gated_body,
        [
            shape((tok, nv), BF),
            shape((STRETCH + 16, ncol), BF),
            shape((STRETCH + 16, ncol), BF),
            shape((STRETCH, ncol), BF),
            shape((STRETCH, ncol), BF),
            shape((8, tok)),
        ],
        (ids, p, q, bc0, bc1, got_s, got_v, got_w, state0, end_row, gain, wo),
        "gated_part",
        2 * tok * nv * (2 * ncol + 128),
    )


def near_body(ids, z, wo, top_r, low_l):
    ncol = wo.shape[1] // RING
    top_r[...] = dot(z[:STRETCH, :], wo[:, chunk_of(ids, 2, ncol)])
    low_l[...] = dot(z[STRETCH:, :], wo[:, chunk_of(ids, 1, ncol)])


def near_part(ids, z, wo):
    tok, nv = z.shape
    ncol = wo.shape[1] // RING
    return call(
        near_body, [shape((STRETCH, ncol))] * 2, (ids, z, wo), "near_part", 2 * tok * nv * ncol
    )


def mine_body(ids, z, wo, low_r, top_l, own):
    ncol = wo.shape[1] // RING
    at = chunk_of(ids, 0, ncol)
    own[:STRETCH, :] = dot(z[:STRETCH, :], wo[:, at]) + top_l[...].astype(F32)
    own[STRETCH:, :] = dot(z[STRETCH:, :], wo[:, at]) + low_r[...].astype(F32)


def mine_part(ids, z, wo, low_r, top_l):
    tok, nv = z.shape
    ncol = wo.shape[1] // RING
    return call(
        mine_body,
        [shape((tok, ncol))],
        (ids, z, wo, low_r, top_l),
        "mine_part",
        4 * tok * nv * ncol,
    )[0]


def add_body(ids, a1, b1, a2, b2, o1, o2):
    o1[:STRETCH, :] = (a1[...] + b1[:STRETCH, :].astype(F32)).astype(BF)
    o1[STRETCH:, :] = b1[STRETCH:, :]
    o2[...] = (a2[...] + b2[:STRETCH, :].astype(F32)).astype(BF)


def add_part(ids, a1, b1, a2, b2):
    return call(
        add_body,
        [shape(b1.shape, BF), shape(a2.shape, BF)],
        (ids, a1, b1, a2, b2),
        "add_part",
        2 * a1.size,
    )


def final_body(ids, own, top_r, low_l, mine, sq_r, sq_l, out):
    total = mine[0:1, :]
    for other in (sq_r, sq_l, top_r):
        more = other[STRETCH:, :512].astype(F32)
        total = total + (more[0:1, :] + more[1:2, :] + more[2:3, :])
    inv = lax.rsqrt(total * (1.0 / 5120.0) + 1e-05)
    inv = jnp.transpose(jnp.broadcast_to(inv, (128, inv.shape[1])))
    for block, got in ((0, top_r), (1, low_l)):
        rows = block_rows(block)
        scale = inv[rows, :]
        for low in range(0, out.shape[1], 128):
            c = slice(low, low + 128)
            out[rows, c] = ((own[rows, c] + got[:STRETCH, c].astype(F32)) * scale).astype(BF)


def final_part(ids, own, top_r, low_l, mine, sq_r, sq_l):
    return call(
        final_body,
        [shape(own.shape, BF)],
        (ids, own, top_r, low_l, mine, sq_r, sq_l),
        "final_part",
        4 * own.size,
    )[0]


def on_device(
    tokens,
    send_rows,
    send_counts,
    stretch_segments,
    main_proj,
    state_proj,
    step_proj,
    conv_main,
    conv_state,
    step_bias,
    decay_log,
    skip_gain,
    norm_gain,
    out_proj,
):
    ctx = lax.axis_index("ctx").astype(jnp.int32)
    head = lax.axis_index("head").astype(jnp.int32)
    tok, width = tokens.shape
    sources, slots = send_rows.shape[1:]
    heads = step_bias.shape[0]
    inner = main_proj.shape[2]
    head_dim = inner // heads

    send_list = send_rows.reshape(sources * slots)
    pick = (send_list[:, None] == jnp.arange(tok, dtype=jnp.int32)[None, :]).astype(BF)
    outgoing = dot(pick, tokens).astype(BF).reshape(sources, slots, width)
    arrived = lax.all_to_all(outgoing, "ctx", split_axis=0, concat_axis=0, tiled=True)

    blocks = tok // STRETCH
    block_ids = ctx * blocks + jnp.arange(blocks, dtype=jnp.int32)
    segment = jnp.take(stretch_segments, block_ids)
    before = jnp.take(stretch_segments, jnp.maximum(block_ids - 1, 0))
    carry = ((segment == before) & (block_ids > 0)).astype(jnp.int32)
    ring = jnp.stack([head, head + 3, head + 1, head + 2]) % RING
    ids = jnp.concatenate([ring, carry]).astype(jnp.int32)
    wm = flat_part(ids, main_proj)
    pad = ((0, 128 - heads),)
    head_rows = jnp.stack(
        [jnp.pad(step_bias, pad), jnp.pad(jnp.exp(decay_log), pad), jnp.pad(skip_gain, pad)]
    )
    head_rows = jnp.pad(head_rows, ((0, 5), (0, 0)))
    gain = norm_gain[None, :]

    column = jnp.take(send_counts, ctx, axis=1)
    begins = jnp.cumsum(column) - column
    slot = jnp.arange(slots, dtype=jnp.int32)[None, :]
    target = jnp.where(slot < column[:, None], begins[:, None] + slot, -1)
    target = target.reshape(1, sources * slots)
    arrived, wm, target, head_rows, gain, ids = lax.optimization_barrier(
        (arrived, wm, target, head_rows, gain, ids)
    )
    second, first, last = arrange_part(ids, target, arrived.reshape(sources * slots, width))
    weights = (state_proj, step_proj, wm)
    taps = (conv_state, conv_main, head_rows)

    r1 = turned(second, 1)
    l1 = turned(second, -1)
    t = shifted(last, 1)
    acc1 = own_part(ids, second, *weights)
    first = jnp.concatenate([t, first], axis=0)
    r1, l1, acc1, first = lax.optimization_barrier((r1, l1, acc1, first))
    cut = STRETCH // 2 + TAIL
    b1 = turned(r1[:cut], 1)
    b2 = turned(l1[cut:], -1)
    acc1 = next_part(ids, r1, l1, *weights, acc1)
    first, acc1 = lax.optimization_barrier((first, acc1))
    r0 = turned(first, 1)
    l0 = turned(first, -1)
    acc0 = own_part(ids, first, *weights)
    b1, b2, acc1, acc0 = lax.optimization_barrier((b1, b2, acc1, acc0))
    *block1, payload, mid, mid_step = second_part(ids, b1, b2, *weights, acc1, *taps)
    got_s = shifted(payload, 1)
    r0, l0, acc0, payload = lax.optimization_barrier((r0, l0, acc0, payload))
    cut = STRETCH // 2
    a1 = turned(r0[:cut], 1)
    a2 = turned(l0[cut:], -1)
    acc0 = next_part(ids, r0, l0, *weights, acc0)
    *block0, joined, joined_low, state0, end_row = first_part(
        ids, a1, a2, *weights, acc0, *taps, mid, mid_step, got_s
    )

    got_v = shifted(joined, 1)
    got_w = shifted(joined_low, 2)
    p, q = mix_part(ids, a1, a2, b1, b2, wm, acc0, acc1, head_rows, block0, block1)

    z, far_r, far_l, dir_r, dir_l, squares = gated_part(
        ids, p, q, block0[1], block1[1], got_s, got_v, got_w, state0, end_row, gain, out_proj
    )
    got_r = turned(far_r, 1)
    got_l = turned(far_l, -1)
    low_r = turned(dir_r, 1)
    top_l = turned(dir_l, -1)
    top_r, low_l = near_part(ids, z, out_proj)
    sum_r, sum_l = add_part(ids, top_r, got_r, low_l, got_l)
    top_r = turned(sum_r, 1)
    low_l = turned(sum_l, -1)
    own = mine_part(ids, z, out_proj, low_r, top_l)
    return final_part(ids, own, top_r, low_l, squares, got_r, got_l)


def solution(mesh):
    return jax.shard_map(
        on_device,
        mesh=mesh,
        in_specs=(
            P("ctx", "head"),
            P("ctx", None, None),
            P(),
            P(),
            P(None, None, "head"),
            P(),
            P(None, "head"),
            P(None, "head"),
            P(),
            P("head"),
            P("head"),
            P("head"),
            P("head"),
            P("head", None),
        ),
        out_specs=P("ctx", "head"),
        check_vma=False,
    )
```

time: 128 us -> 123 us (0.961)
  Pallas kernels: 34.5 us -> 41.5 us
  matrix products: 5.69 us -> 2.15 us
  other arithmetic: 3.44 us -> 0.66 us
  starting transfers between devices: 40.6 us -> 37.9 us
  waiting for transfers between devices: 20 us -> 17.9 us
    pallas_call x11 -> x14, Pallas kernels: 34.5 us -> 41.5 us  [call(): pl.pallas_call(body, in_specs=[pl.BlockSpec(memory_space=pltpu.SMEM)] + [...]
    ppermute x3 -> x4, starting transfers between devices: 12.6 us -> 8.82 us  [shifted(): lax.ppermute(value, 'ctx', [(i, i + steps) for i in range(count - steps)])]
    dot_general x2 -> x1, matrix products: 5.69 us -> 2.15 us  [dot(): return jnp.dot(a, b, preferred_element_type=F32)]
    ppermute x13 -> x14, waiting for transfers between devices: 16 us -> 13.8 us  [turned(): lax.ppermute(value, 'head', [(i, (i + steps) % RING) for i in range(RING)])]
    ppermute x3 -> x4, waiting for transfers between devices: 1.68 us -> 0.01 us  [shifted(): lax.ppermute(value, 'ctx', [(i, i + steps) for i in range(count - steps)])]
    all_to_all x1, waiting for transfers between devices: 2.35 us -> 4 us  [on_device(): lax.all_to_all(outgoing, 'ctx', split_axis=0, concat_axis=0, tiled=True)]
    concatenate x1, other arithmetic: 1.56 us -> 0.03 us  [on_device(): first = jnp.concatenate([t, first], axis=0)]
    ppermute x13 -> x14, starting transfers between devices: 19.5 us -> 20.7 us  [turned(): lax.ppermute(value, 'head', [(i, (i + steps) % RING) for i in range(RING)])]
  transfers between devices with their start and end apart: 17 -> 19, of which waited for: 8 -> 8; matrix products, arithmetic and copies ran while one was open for 15% -> 2% of each run, Pallas kernels for 18% -> 25%
where the time goes in v3:
time: 123 us; the launch traced here: 121 us
  Pallas kernels  41.5 us (34%)
  starting transfers between devices  37.9 us (31%)
  local copies, waits for them, and re-layouts  20 us (16%)
  waiting for transfers between devices  17.9 us (15%)
  matrix products  2.15 us (2%)
    pallas_call x14, Pallas kernels, call(): pl.pallas_call(body, in_specs=[pl.BlockSpec(memory_space=pltpu.SMEM)] + [...  41.5 us
    ppermute x14, starting transfers between devices, turned(): lax.ppermute(value, 'head', [(i, (i + steps) % RING) for i in range(RING)])  20.7 us
    unnamed x39, local copies, waits for them, and re-layouts  17.7 us
    ppermute x14, waiting for transfers between devices, turned(): lax.ppermute(value, 'head', [(i, (i + steps) % RING) for i in range(RING)])  13.8 us
    ppermute x4, starting transfers between devices, shifted(): lax.ppermute(value, 'ctx', [(i, i + steps) for i in range(count - steps)])  8.82 us
    all_to_all x1, starting transfers between devices, on_device(): lax.all_to_all(outgoing, 'ctx', split_axis=0, concat_axis=0, tiled=True)  8.38 us
    all_to_all x1, waiting for transfers between devices, on_device(): lax.all_to_all(outgoing, 'ctx', split_axis=0, concat_axis=0, tiled=True)  4 us
  transfers between devices with their start and end apart: 19, of which 8 were waited for; matrix products, arithmetic and copies ran while one was open for 2% of the time, Pallas kernels for 25%

profile of v3, /device:TPU:0, one launch (start us, length us, event | category | flops | bytes accessed | tf_op | source)
XLA Modules:
  0.0 120.5 jit_solution(15630297711355141043)
XLA Ops:
  0.0 0.9 eq.20
  0.9 0.2 copy-done
  1.1 2.1 %fusion.1 = bf16[1024,640]{1,0:T(8,128)(2,1)} fusion(bf16[512,640]{1,0:T(8,128)(2,1)S(1)} %copy-done, s32[1024]{0:T(1024)S(1)} %eq.20), kind=kOutput, calls=%fused_computation.4 | convolution fusion | flops 672268288 | bytes 1970176 | tf_op jit(solution)/shard_map/dot_general | solution.py:19
  3.3 8.4 %all-to-all-start = ((bf16[32,32,640]{2,1,0:T(8,128)(2,1)}), bf16[32,32,640]{2,1,0:T(8,128)(2,1)S(1)}, u32[]{:S(2)}, u32[]{:S(2)}) async-start(bf16[32,32,640]{2,1,0:T(8,128)(2,1)} %bitcast.16), calls=%async_computation | async-start | bytes 2621440 | tf_op jit(solution)/shard_map/all_to_all | solution.py:570
  11.7 0.6 gather_fusion
  12.4 0.6 gather_fusion.1
  13.0 0.2 fusion.4
  13.3 0.1 reduce.1
  13.8 4.7 %copy-done.7 = bf16[2560,2,1280]{2,1,0:T(2,128)(2,1)S(1)} copy-done((bf16[2560,2,1280]{2,1,0:T(2,128)(2,1)S(1)}, bf16[2560,2,1280]{2,1,0:T(2,128)(2,1)}, u32[]{:S(2)}) %copy-start.7) | copy-done | bytes 13107224
  18.5 4.3 %flat_part.1.wm = bf16[2560,2560]{1,0:T(8,128)(2,1)S(1)} custom-call(s32[6]{0:T(128)S(1)} %pad_add_fusion.ids, bf16[2560,2,1280]{2,1,0:T(2,128)(2,1)S(1)} %copy-done.7), custom_call_target="tpu_custom_call" | custom-call | flops 1000000000 | bytes 26214400 | tf_op jit(solution)/shard_map/flat_part/pallas_call | solution.py:59
  22.8 4.7 %copy-done.2 = bf16[2560,2560]{1,0:T(8,128)(2,1)} copy-done((bf16[2560,2560]{1,0:T(8,128)(2,1)}, bf16[2560,2560]{1,0:T(8,128)(2,1)S(1)}, u32[]{:S(2)}) %copy-start.2) | copy-done | bytes 13107224
  27.6 4.0 %all-to-all-done = bf16[32,32,640]{2,1,0:T(8,128)(2,1)S(1)} async-done(((bf16[32,32,640]{2,1,0:T(8,128)(2,1)}), bf16[32,32,640]{2,1,0:T(8,128)(2,1)S(1)}, u32[]{:S(2)}, u32[]{:S(2)}) %all-to-all-start) | async-done | bytes 1310752 | tf_op jit(solution)/shard_map/all_to_all | solution.py:570
  31.6 1.5 %arrange_part.1 = (bf16[272,640]{1,0:T(8,128)(2,1)S(1)}, bf16[240,640]{1,0:T(8,128)(2,1)S(1)}, bf16[16,640]{1,0:T(8,128)(2,1)S(1)}) custom-call(s32[6]{0:T(128)S(1)} %pad_add_fusion.ids, s32[1,1024]{1,0:T(1,128)S(1)} %select_n.56.target, bf16[1024,640]{1,0:T(8,128)(2,1)S(1)} %bitcast.15), custom_call_target="tpu_custom_call" | custom-call | flops 671088640 | bytes 1990656 | tf_op jit(solution)/shard_map/arrange_part/pallas_call | solution.py:59
  33.1 3.1 %collective-permute-start.1 = (bf16[272,640]{1,0:T(8,128)(2,1)S(1)}, bf16[272,640]{1,0:T(8,128)(2,1)S(1)}, u32[]{:S(2)}, u32[]{:S(2)}) collective-permute-start(bf16[272,640]{1,0:T(8,128)(2,1)S(1)} %get-tuple-element.62.x), channel_id=1, source_target_pairs={{0,3},{1,0},{2,1},{3,2},{4,7},{5,4},{6,5},{7,6},{8,11},{9,8},{10,9... | collective-permute-start | bytes 1044488 | tf_op jit(solution)/shard_map/ppermute | solution.py:23
  36.2 0.4 copy.21.tp
  36.6 1.7 %collective-permute-start.2 = (bf16[16,640]{1,0:T(8,128)(2,1)S(1)}, bf16[16,640]{1,0:T(8,128)(2,1)S(1)}, u32[]{:S(2)}, u32[]{:S(2)}) collective-permute-start(bf16[16,640]{1,0:T(8,128)(2,1)S(1)} %get-tuple-element.64), channel_id=1, source_target_pairs={{0,4},{4,8},{8,12},{12,16},{16,20},{20,24},{24,28},{28,32},{32,36}... | collective-permute-start | bytes 61448 | tf_op jit(solution)/shard_map/ppermute | solution.py:28
  38.4 4.7 %copy-done.3 = bf16[2560,2560]{1,0:T(8,128)(2,1)S(1)} copy-done((bf16[2560,2560]{1,0:T(8,128)(2,1)S(1)}, bf16[2560,2560]{1,0:T(8,128)(2,1)}, u32[]{:S(2)}) %copy-start.3) | copy-done | bytes 13107224
  43.1 2.0 %own_part.2.before = f32[272,2944]{1,0:T(8,128)S(1)} custom-call(s32[6]{0:T(128)S(1)} %pad_add_fusion.ids, bf16[272,640]{1,0:T(8,128)(2,1)S(1)} %get-tuple-element.62.x, bf16[2560,256]{1,0:T(8,128)(2,1)S(1)} %copy-done.6, bf16[2560,20]{1,0:T(8,128)(2,1)S(1)} %copy.21.tp, bf16[2560,2560]{1,0:T(8,128)(2,1)S(1)} %copy-done.3), custom_call_target="tpu_custom_call" | custom-call | flops 1024983040 | bytes 18071552 | tf_op jit(solution)/shard_map/own_part/pallas_call | solution.py:59
  45.1 2.2 %collective-permute-done.r = bf16[272,640]{1,0:T(8,128)(2,1)S(1)} collective-permute-done((bf16[272,640]{1,0:T(8,128)(2,1)S(1)}, bf16[272,640]{1,0:T(8,128)(2,1)S(1)}, u32[]{:S(2)}, u32[]{:S(2)}) %collective-permute-start) | collective-permute-done | bytes 348192 | tf_op jit(solution)/shard_map/ppermute | solution.py:23
  47.4 0.8 collective-permute-start.6
  48.2 1.2 %collective-permute-start.5 = (bf16[144,640]{1,0:T(8,128)(2,1)S(1)}, bf16[144,640]{1,0:T(8,128)(2,1)S(1)}, u32[]{:S(2)}, u32[]{:S(2)}) collective-permute-start(bf16[144,640]{1,0:T(8,128)(2,1)S(1)} %slice.12), channel_id=1, source_target_pairs={{0,1},{1,2},{2,3},{3,0},{4,5},{5,6},{6,7},{7,4},{8,9},{9,10},{10,1... | collective-permute-start | bytes 552968 | tf_op jit(solution)/shard_map/ppermute | solution.py:23
  49.5 3.4 %next_part.2.acc.acc1 = f32[272,2944]{1,0:T(8,128)S(1)} custom-call(s32[6]{0:T(128)S(1)} %pad_add_fusion.ids, bf16[272,640]{1,0:T(8,128)(2,1)S(1)} %collective-permute-done.r, bf16[272,640]{1,0:T(8,128)(2,1)S(1)} %collective-permute-done.1.l, bf16[2560,256]{1,0:T(8,128)(2,1)S(1)} %copy-done.6, bf16[2560,20]{1,0:T(8,128)(2,1)S(1)} %copy.21.tp, ...), custom_call_target="tpu_custom_call" | custom-call | flops 2049966080 | bytes 21622784 | tf_op jit(solution)/shard_map/next_part/pallas_call | solution.py:59
  52.9 2.1 %collective-permute-start.4 = (bf16[256,640]{1,0:T(8,128)(2,1)S(1)}, bf16[256,640]{1,0:T(8,128)(2,1)S(1)}, u32[]{:S(2)}, u32[]{:S(2)}) collective-permute-start(bf16[256,640]{1,0:T(8,128)(2,1)S(1)} %pad_maximum_fusion.x), channel_id=1, source_target_pairs={{0,3},{1,0},{2,1},{3,2},{4,7},{5,4},{6,5},{7,6},{8,11},{9,8},{10,9... | collective-permute-start | bytes 983048 | tf_op jit(solution)/shard_map/ppermute | solution.py:23
  55.0 1.9 %own_part.3.before = f32[256,2944]{1,0:T(8,128)S(1)} custom-call(s32[6]{0:T(128)S(1)} %pad_add_fusion.ids, bf16[256,640]{1,0:T(8,128)(2,1)S(1)} %pad_maximum_fusion.x, bf16[2560,256]{1,0:T(8,128)(2,1)S(1)} %copy-done.6, bf16[2560,20]{1,0:T(8,128)(2,1)S(1)} %copy.21.tp, bf16[2560,2560]{1,0:T(8,128)(2,1)S(1)} %copy-done.4), custom_call_target="tpu_custom_call" | custom-call | flops 964689920 | bytes 17862656 | tf_op jit(solution)/shard_map/own_part/pallas_call | solution.py:59
  56.9 4.2 %second_part.1 = (bf16[256,1280]{1,0:T(8,128)(2,1)S(1)}, bf16[256,256]{1,0:T(8,128)(2,1)S(1)}, bf16[256,128]{1,0:T(8,128)(2,1)S(1)}, f32[32,256]{1,0:T(8,128)S(1...) custom-call(s32[6]{0:T(128)S(1)} %pad_add_fusion.ids, ...), custom_call_target="tpu_custom_call" | custom-call | flops 1090519040 | bytes 19558400 | tf_op jit(solution)/shard_map/second_part/pallas_call | solution.py:59
  61.2 1.7 %collective-permute-start.9 = (bf16[144,1280]{1,0:T(8,128)(2,1)S(1)}, bf16[144,1280]{1,0:T(8,128)(2,1)S(1)}, u32[]{:S(2)}, u32[]{:S(2)}) collective-permute-start(bf16[144,1280]{1,0:T(8,128)(2,1)S(1)} %get-tuple-element.77), channel_id=1, source_target_pairs={{0,4},{4,8},{8,12},{12,16},{16,20},{20,24},{24,28},{28,32},{32,36}... | collective-permute-start | bytes 1105928 | tf_op jit(solution)/shard_map/ppermute | solution.py:28
  62.8 2.7 %collective-permute-done.3.r = bf16[256,640]{1,0:T(8,128)(2,1)S(1)} collective-permute-done((bf16[256,640]{1,0:T(8,128)(2,1)S(1)}, bf16[256,640]{1,0:T(8,128)(2,1)S(1)}, u32[]{:S(2)}, u32[]{:S(2)}) %collective-permute-start.3) | collective-permute-done | bytes 327712 | tf_op jit(solution)/shard_map/ppermute | solution.py:23
  65.6 3.2 %collective-permute-start.8 = (bf16[128,640]{1,0:T(8,128)(2,1)S(1)}, bf16[128,640]{1,0:T(8,128)(2,1)S(1)}, u32[]{:S(2)}, u32[]{:S(2)}) collective-permute-start(bf16[128,640]{1,0:T(8,128)(2,1)S(1)} %slice.15), channel_id=1, source_target_pairs={{0,3},{1,0},{2,1},{3,2},{4,7},{5,4},{6,5},{7,6},{8,11},{9,8},{10,9... | collective-permute-start | bytes 491528 | tf_op jit(solution)/shard_map/ppermute | solution.py:23
  68.9 3.1 %next_part.3.acc.acc0 = f32[256,2944]{1,0:T(8,128)S(1)} custom-call(s32[6]{0:T(128)S(1)} %pad_add_fusion.ids, bf16[256,640]{1,0:T(8,128)(2,1)S(1)} %collective-permute-done.3.r, bf16[256,640]{1,0:T(8,128)(2,1)S(1)} %collective-permute-done.4.l, bf16[2560,256]{1,0:T(8,128)(2,1)S(1)} %copy-done.6, bf16[2560,20]{1,0:T(8,128)(2,1)S(1)} %copy.21.tp, ...), custom_call_target="tpu_custom_call" | custom-call | flops 1929379840 | bytes 21204992 | tf_op jit(solution)/shard_map/next_part/pallas_call | solution.py:59
  72.0 0.2 collective-permute-done.7.o1.a1
  72.2 4.2 %first_part.1 = (bf16[256,1280]{1,0:T(8,128)(2,1)S(1)}, bf16[256,256]{1,0:T(8,128)(2,1)S(1)}, bf16[256,128]{1,0:T(8,128)(2,1)S(1)}, f32[32,256]{1,0:T(8,128)S(1)...) custom-call(s32[6]{0:T(128)S(1)} %pad_add_fusion.ids, ...), custom_call_target="tpu_custom_call" | custom-call | flops 1090519040 | bytes 20742144 | tf_op jit(solution)/shard_map/first_part/pallas_call | solution.py:59
  76.4 3.9 %collective-permute-start.11 = (bf16[128,1280]{1,0:T(8,128)(2,1)S(1)}, bf16[128,1280]{1,0:T(8,128)(2,1)S(1)}, u32[]{:S(2)}, u32[]{:S(2)}) collective-permute-start(bf16[128,1280]{1,0:T(8,128)(2,1)S(1)} %get-tuple-element.98), channel_id=1, source_target_pairs={{0,8},{4,12},{8,16},{12,20},{16,24},{20,28},{24,32},{28,36},{32,40... | collective-permute-start | bytes 983048 | tf_op jit(solution)/shard_map/ppermute | solution.py:28
  80.3 1.5 %collective-permute-start.10 = (bf16[144,1280]{1,0:T(8,128)(2,1)S(1)}, bf16[144,1280]{1,0:T(8,128)(2,1)S(1)}, u32[]{:S(2)}, u32[]{:S(2)}) collective-permute-start(bf16[144,1280]{1,0:T(8,128)(2,1)S(1)} %get-tuple-element.97), channel_id=1, source_target_pairs={{0,4},{4,8},{8,12},{12,16},{16,20},{20,24},{24,28},{28,32},{32,36}... | collective-permute-start | bytes 1105928 | tf_op jit(solution)/shard_map/ppermute | solution.py:28
  81.8 7.4 %mix_part.1 = (f32[512,1280]{1,0:T(8,128)S(1)}, f32[512,1280]{1,0:T(8,128)S(1)}) custom-call(s32[6]{0:T(128)S(1)} %pad_add_fusion.ids, bf16[128,640]{1,0:T(8,128)(2,1)S(1)} %collective-permute-done.7.o1.a1, bf16[128,640]{1,0:T(8,128)(2,1)S(1)} %collective-permute-done.8.o2.a2, bf16[144,640]{1,0:T(8,128)(2,1)S(1)} %collective-permute-done.5.o1.b1, ...), custom_call_target="tpu_custom_call" | custom-call | flops 8000000000 | bytes 27213824 | tf_op jit(solution)/shard_map/mix_part/pallas_call | solution.py:59
  89.3 3.6 %gated_part.1 = (bf16[512,1280]{1,0:T(8,128)(2,1)S(1)}, bf16[272,640]{1,0:T(8,128)(2,1)S(1)}, bf16[272,640]{1,0:T(8,128)(2,1)S(1)}, bf16[256,640]{1,0:T(8,128)(2...) custom-call(s32[6]{0:T(128)S(1)} %pad_add_fusion.ids, f32[512,1280]{1,0:T(8,128)S(1)} %get-tuple-element.95.p, ...), custom_call_target="tpu_custom_call" | custom-call | flops 1845493760 | bytes 16503808 | tf_op jit(solution)/shard_map/gated_part/pallas_call | solution.py:59
  93.0 3.2 %collective-permute-start.15 = (bf16[272,640]{1,0:T(8,128)(2,1)S(1)}, bf16[272,640]{1,0:T(8,128)(2,1)S(1)}, u32[]{:S(2)}, u32[]{:S(2)}) collective-permute-start(bf16[272,640]{1,0:T(8,128)(2,1)S(1)} %get-tuple-element.108), channel_id=1, source_target_pairs={{0,3},{1,0},{2,1},{3,2},{4,7},{5,4},{6,5},{7,6},{8,11},{9,8},{10,9... | collective-permute-start | bytes 1044488 | tf_op jit(solution)/shard_map/ppermute | solution.py:23
  96.2 3.2 %collective-permute-start.13 = (bf16[256,640]{1,0:T(8,128)(2,1)S(1)}, bf16[256,640]{1,0:T(8,128)(2,1)S(1)}, u32[]{:S(2)}, u32[]{:S(2)}) collective-permute-start(bf16[256,640]{1,0:T(8,128)(2,1)S(1)} %get-tuple-element.104), channel_id=1, source_target_pairs={{0,3},{1,0},{2,1},{3,2},{4,7},{5,4},{6,5},{7,6},{8,11},{9,8},{10,9... | collective-permute-start | bytes 983048 | tf_op jit(solution)/shard_map/ppermute | solution.py:23
  99.5 1.8 %near_part.1 = (f32[256,640]{1,0:T(8,128)S(1)}, f32[256,640]{1,0:T(8,128)S(1)}) custom-call(s32[6]{0:T(128)S(1)} %pad_add_fusion.ids, bf16[512,1280]{1,0:T(8,128)(2,1)S(1)} %get-tuple-element.102.z, bf16[1280,2560]{1,0:T(8,128)(2,1)S(1)} %bitcast.14), custom_call_target="tpu_custom_call" | custom-call | flops 838860800 | bytes 9175040 | tf_op jit(solution)/shard_map/near_part/pallas_call | solution.py:59
  101.2 3.2 %collective-permute-done.14.b1.sq_r = bf16[272,640]{1,0:T(8,128)(2,1)S(1)} collective-permute-done((bf16[272,640]{1,0:T(8,128)(2,1)S(1)}, bf16[272,640]{1,0:T(8,128)(2,1)S(1)}, u32[]{:S(2)}, u32[]{:S(2)}) %collective-permute-start.14) | collective-permute-done | bytes 348192 | tf_op jit(solution)/shard_map/ppermute | solution.py:23
  104.4 0.7 add_part.1
  105.1 1.1 collective-permute-start.16
  106.3 2.5 %collective-permute-start.17 = (bf16[256,640]{1,0:T(8,128)(2,1)S(1)}, bf16[256,640]{1,0:T(8,128)(2,1)S(1)}, u32[]{:S(2)}, u32[]{:S(2)}) collective-permute-start(bf16[256,640]{1,0:T(8,128)(2,1)S(1)} %get-tuple-element.110), channel_id=1, source_target_pairs={{0,3},{1,0},{2,1},{3,2},{4,7},{5,4},{6,5},{7,6},{8,11},{9,8},{10,9... | collective-permute-start | bytes 983048 | tf_op jit(solution)/shard_map/ppermute | solution.py:23
  108.7 2.7 %collective-permute-done.12.low_r = bf16[256,640]{1,0:T(8,128)(2,1)S(1)} collective-permute-done((bf16[256,640]{1,0:T(8,128)(2,1)S(1)}, bf16[256,640]{1,0:T(8,128)(2,1)S(1)}, u32[]{:S(2)}, u32[]{:S(2)}) %collective-permute-start.12) | collective-permute-done | bytes 327712 | tf_op jit(solution)/shard_map/ppermute | solution.py:23
  111.5 2.9 %copy-done.5 = bf16[1280,2560]{1,0:T(8,128)(2,1)S(1)} copy-done((bf16[1280,2560]{1,0:T(8,128)(2,1)S(1)}, bf16[1280,2560]{1,0:T(8,128)(2,1)}, u32[]{:S(2)}) %copy-start.5) | copy-done | bytes 6553624
  114.3 1.7 %mine_part.1.own = f32[512,640]{1,0:T(8,128)S(1)} custom-call(s32[6]{0:T(128)S(1)} %pad_add_fusion.ids, bf16[512,1280]{1,0:T(8,128)(2,1)S(1)} %get-tuple-element.102.z, bf16[1280,2560]{1,0:T(8,128)(2,1)S(1)} %copy-done.5, bf16[256,640]{1,0:T(8,128)(2,1)S(1)} %collective-permute-done.12.low_r, bf16[256,640]{1,0:T(8,128)(2,1)S(1)} %collective-permute-done.13.top_l), custom_call_target="tpu_custom_call" | custom-call | flops 1677721600 | bytes 9830400 | tf_op jit(solution)/shard_map/mine_part/pallas_call | solution.py:59
  116.1 2.2 %collective-permute-done.17.low_l = bf16[256,640]{1,0:T(8,128)(2,1)S(1)} collective-permute-done((bf16[256,640]{1,0:T(8,128)(2,1)S(1)}, bf16[256,640]{1,0:T(8,128)(2,1)S(1)}, u32[]{:S(2)}, u32[]{:S(2)}) %collective-permute-start.17) | collective-permute-done | bytes 327712 | tf_op jit(solution)/shard_map/ppermute | solution.py:23
  118.3 0.7 collective-permute-done.16.top_r
  118.9 1.6 %final_part.1 = bf16[512,640]{1,0:T(8,128)(2,1)} custom-call(s32[6]{0:T(128)S(1)} %pad_add_fusion.ids, f32[512,640]{1,0:T(8,128)S(1)} %mine_part.1.own, bf16[272,640]{1,0:T(8,128)(2,1)S(1)} %collective-permute-done.16.top_r, bf16[256,640]{1,0:T(8,128)(2,1)S(1)} %collective-permute-done.17.low_l, f32[8,512]{1,0:T(8,128)S(1)} %get-tuple-element.111.mine, ...), custom_call_target="tpu_custom_call" | custom-call | flops 1310720 | bytes 3354624 | tf_op jit(solution)/shard_map/final_part/pallas_call | solution.py:59
  (70 shorter events, 0.8 us)
Async XLA Ops:
  0.0 1.1 copy-start
  1.1 10.6 %copy-start.15 = (f32[20]{0:T(128)S(1)}, f32[20]{0:T(128)}, u32[]{:S(2)}) copy-start(f32[20]{0:T(128)} %param.26) | copy-start | bytes 244
  1.1 10.6 %copy-start.10 = (s32[64]{0:T(128)S(1)}, s32[64]{0:T(128)}, u32[]{:S(2)}) copy-start(s32[64]{0:T(128)} %param.19) | copy-start | bytes 772
  3.3 9.8 %copy-start.13 = (f32[1280]{0:T(1024)S(1)}, f32[1280]{0:T(1024)}, u32[]{:S(2)}) copy-start(f32[1280]{0:T(1024)} %param.28) | copy-start | bytes 15364
  3.3 9.8 %copy-start.12 = (s32[32,32]{1,0:T(8,128)S(1)}, s32[32,32]{1,0:T(8,128)}, u32[]{:S(2)}) copy-start(s32[32,32]{1,0:T(8,128)} %param.18) | copy-start | bytes 12292
  3.3 28.3 %all-to-all-start = ((bf16[32,32,640]{2,1,0:T(8,128)(2,1)}), bf16[32,32,640]{2,1,0:T(8,128)(2,1)S(1)}, u32[]{:S(2)}, u32[]{:S(2)}) async-start(bf16[32,32,640]{2,1,0:T(8,128)(2,1)} %bitcast.16), calls=%async_computation | async-start | bytes 2621440 | tf_op jit(solution)/shard_map/all_to_all | solution.py:570
  13.7 4.7 %copy-start.7 = (bf16[2560,2,1280]{2,1,0:T(2,128)(2,1)S(1)}, bf16[2560,2,1280]{2,1,0:T(2,128)(2,1)}, u32[]{:S(2)}) copy-start(bf16[2560,2,1280]{2,1,0:T(2,128)(2,1)} %w.1) | copy-start | bytes 39321604
  18.5 9.1 %copy-start.16 = (f32[20]{0:T(128)S(1)}, f32[20]{0:T(128)}, u32[]{:S(2)}) copy-start(f32[20]{0:T(128)} %param.25) | copy-start | bytes 244
  18.5 9.1 %copy-start.14 = (f32[20]{0:T(128)S(1)}, f32[20]{0:T(128)}, u32[]{:S(2)}) copy-start(f32[20]{0:T(128)} %param.27) | copy-start | bytes 244
  18.5 17.8 %copy-start.11 = (bf16[2560,20]{0,1:T(8,128)(2,1)S(1)}, bf16[2560,20]{0,1:T(8,128)(2,1)}, u32[]{:S(2)}) copy-start(bf16[2560,20]{0,1:T(8,128)(2,1)} %param.22) | copy-start | bytes 307204
  22.8 4.7 %copy-start.2 = (bf16[2560,2560]{1,0:T(8,128)(2,1)}, bf16[2560,2560]{1,0:T(8,128)(2,1)S(1)}, u32[]{:S(2)}) copy-start(bf16[2560,2560]{1,0:T(8,128)(2,1)S(1)} %flat_part.1.wm) | copy-start | bytes 39321604
  27.6 10.8 %copy-start.6 = (bf16[2560,256]{1,0:T(8,128)(2,1)S(1)}, bf16[2560,256]{1,0:T(8,128)(2,1)}, u32[]{:S(2)}) copy-start(bf16[2560,256]{1,0:T(8,128)(2,1)} %sp.11) | copy-start | bytes 3932164
  33.1 12.0 %collective-permute-start.1 = (bf16[272,640]{1,0:T(8,128)(2,1)S(1)}, bf16[272,640]{1,0:T(8,128)(2,1)S(1)}, u32[]{:S(2)}, u32[]{:S(2)}) collective-permute-start(bf16[272,640]{1,0:T(8,128)(2,1)S(1)} %get-tuple-element.62.x), channel_id=1, source_target_pairs={{0,3},{1,0},{2,1},{3,2},{4,7},{5,4},{6,5},{7,6},{8,11},{9,8},{10,9... | collective-permute-start | bytes 1044488 | tf_op jit(solution)/shard_map/ppermute | solution.py:23
  36.2 11.1 %collective-permute-start = (bf16[272,640]{1,0:T(8,128)(2,1)S(1)}, bf16[272,640]{1,0:T(8,128)(2,1)S(1)}, u32[]{:S(2)}, u32[]{:S(2)}) collective-permute-start(bf16[272,640]{1,0:T(8,128)(2,1)S(1)} %get-tuple-element.62.x), channel_id=1, source_target_pairs={{0,1},{1,2},{2,3},{3,0},{4,5},{5,6},{6,7},{7,4},{8,9},{9,10},{10,1... | collective-permute-start | bytes 1044488 | tf_op jit(solution)/shard_map/ppermute | solution.py:23
  36.6 8.5 %collective-permute-start.2 = (bf16[16,640]{1,0:T(8,128)(2,1)S(1)}, bf16[16,640]{1,0:T(8,128)(2,1)S(1)}, u32[]{:S(2)}, u32[]{:S(2)}) collective-permute-start(bf16[16,640]{1,0:T(8,128)(2,1)S(1)} %get-tuple-element.64), channel_id=1, source_target_pairs={{0,4},{4,8},{8,12},{12,16},{16,20},{20,24},{24,28},{28,32},{32,36}... | collective-permute-start | bytes 61448 | tf_op jit(solution)/shard_map/ppermute | solution.py:28
  38.3 4.7 %copy-start.3 = (bf16[2560,2560]{1,0:T(8,128)(2,1)S(1)}, bf16[2560,2560]{1,0:T(8,128)(2,1)}, u32[]{:S(2)}) copy-start(bf16[2560,2560]{1,0:T(8,128)(2,1)} %copy-done.2) | copy-start | bytes 39321604
  43.1 6.4 %copy-start.4 = (bf16[2560,2560]{1,0:T(8,128)(2,1)S(1)}, bf16[2560,2560]{1,0:T(8,128)(2,1)}, u32[]{:S(2)}) copy-start(bf16[2560,2560]{1,0:T(8,128)(2,1)} %copy-done.2) | copy-start | bytes 39321604
  47.4 9.5 %collective-permute-start.6 = (bf16[128,640]{1,0:T(8,128)(2,1)S(1)}, bf16[128,640]{1,0:T(8,128)(2,1)S(1)}, u32[]{:S(2)}, u32[]{:S(2)}) collective-permute-start(bf16[128,640]{1,0:T(8,128)(2,1)S(1)} %slice.13), channel_id=1, source_target_pairs={{0,3},{1,0},{2,1},{3,2},{4,7},{5,4},{6,5},{7,6},{8,11},{9,8},{10,9... | collective-permute-start | bytes 491528 | tf_op jit(solution)/shard_map/ppermute | solution.py:23
  48.2 8.7 %collective-permute-start.5 = (bf16[144,640]{1,0:T(8,128)(2,1)S(1)}, bf16[144,640]{1,0:T(8,128)(2,1)S(1)}, u32[]{:S(2)}, u32[]{:S(2)}) collective-permute-start(bf16[144,640]{1,0:T(8,128)(2,1)S(1)} %slice.12), channel_id=1, source_target_pairs={{0,1},{1,2},{2,3},{3,0},{4,5},{5,6},{6,7},{7,4},{8,9},{9,10},{10,1... | collective-permute-start | bytes 552968 | tf_op jit(solution)/shard_map/ppermute | solution.py:23
  52.8 4.0 %copy-start.8 = (f32[4,1280]{1,0:T(4,128)S(1)}, f32[4,1280]{1,0:T(4,128)}, u32[]{:S(2)}) copy-start(f32[4,1280]{1,0:T(4,128)} %taps_v.3) | copy-start | bytes 61444
  52.8 4.0 %copy-start.9 = (f32[4,256]{1,0:T(4,128)S(1)}, f32[4,256]{1,0:T(4,128)}, u32[]{:S(2)}) copy-start(f32[4,256]{1,0:T(4,128)} %taps_s.3) | copy-start | bytes 12292
  52.9 10.0 %collective-permute-start.4 = (bf16[256,640]{1,0:T(8,128)(2,1)S(1)}, bf16[256,640]{1,0:T(8,128)(2,1)S(1)}, u32[]{:S(2)}, u32[]{:S(2)}) collective-permute-start(bf16[256,640]{1,0:T(8,128)(2,1)S(1)} %pad_maximum_fusion.x), channel_id=1, source_target_pairs={{0,3},{1,0},{2,1},{3,2},{4,7},{5,4},{6,5},{7,6},{8,11},{9,8},{10,9... | collective-permute-start | bytes 983048 | tf_op jit(solution)/shard_map/ppermute | solution.py:23
  54.9 10.6 %collective-permute-start.3 = (bf16[256,640]{1,0:T(8,128)(2,1)S(1)}, bf16[256,640]{1,0:T(8,128)(2,1)S(1)}, u32[]{:S(2)}, u32[]{:S(2)}) collective-permute-start(bf16[256,640]{1,0:T(8,128)(2,1)S(1)} %pad_maximum_fusion.x), channel_id=1, source_target_pairs={{0,1},{1,2},{2,3},{3,0},{4,5},{5,6},{6,7},{7,4},{8,9},{9,10},{10,1... | collective-permute-start | bytes 983048 | tf_op jit(solution)/shard_map/ppermute | solution.py:23
  61.2 11.0 %collective-permute-start.9 = (bf16[144,1280]{1,0:T(8,128)(2,1)S(1)}, bf16[144,1280]{1,0:T(8,128)(2,1)S(1)}, u32[]{:S(2)}, u32[]{:S(2)}) collective-permute-start(bf16[144,1280]{1,0:T(8,128)(2,1)S(1)} %get-tuple-element.77), channel_id=1, source_target_pairs={{0,4},{4,8},{8,12},{12,16},{16,20},{20,24},{24,28},{28,32},{32,36}... | collective-permute-start | bytes 1105928 | tf_op jit(solution)/shard_map/ppermute | solution.py:28
  65.6 6.6 %collective-permute-start.7 = (bf16[128,640]{1,0:T(8,128)(2,1)S(1)}, bf16[128,640]{1,0:T(8,128)(2,1)S(1)}, u32[]{:S(2)}, u32[]{:S(2)}) collective-permute-start(bf16[128,640]{1,0:T(8,128)(2,1)S(1)} %slice.14), channel_id=1, source_target_pairs={{0,1},{1,2},{2,3},{3,0},{4,5},{5,6},{6,7},{7,4},{8,9},{9,10},{10,1... | collective-permute-start | bytes 491528 | tf_op jit(solution)/shard_map/ppermute | solution.py:23
  65.6 6.5 %collective-permute-start.8 = (bf16[128,640]{1,0:T(8,128)(2,1)S(1)}, bf16[128,640]{1,0:T(8,128)(2,1)S(1)}, u32[]{:S(2)}, u32[]{:S(2)}) collective-permute-start(bf16[128,640]{1,0:T(8,128)(2,1)S(1)} %slice.15), channel_id=1, source_target_pairs={{0,3},{1,0},{2,1},{3,2},{4,7},{5,4},{6,5},{7,6},{8,11},{9,8},{10,9... | collective-permute-start | bytes 491528 | tf_op jit(solution)/shard_map/ppermute | solution.py:23
  76.4 12.9 %collective-permute-start.11 = (bf16[128,1280]{1,0:T(8,128)(2,1)S(1)}, bf16[128,1280]{1,0:T(8,128)(2,1)S(1)}, u32[]{:S(2)}, u32[]{:S(2)}) collective-permute-start(bf16[128,1280]{1,0:T(8,128)(2,1)S(1)} %get-tuple-element.98), channel_id=1, source_target_pairs={{0,8},{4,12},{8,16},{12,20},{16,24},{20,28},{24,32},{28,36},{32,40... | collective-permute-start | bytes 983048 | tf_op jit(solution)/shard_map/ppermute | solution.py:28
  80.3 9.0 %collective-permute-start.10 = (bf16[144,1280]{1,0:T(8,128)(2,1)S(1)}, bf16[144,1280]{1,0:T(8,128)(2,1)S(1)}, u32[]{:S(2)}, u32[]{:S(2)}) collective-permute-start(bf16[144,1280]{1,0:T(8,128)(2,1)S(1)} %get-tuple-element.97), channel_id=1, source_target_pairs={{0,4},{4,8},{8,12},{12,16},{16,20},{20,24},{24,28},{28,32},{32,36}... | collective-permute-start | bytes 1105928 | tf_op jit(solution)/shard_map/ppermute | solution.py:28
  81.8 7.5 %slice-start = ((s8[6553600]{0:T(1024)(128)(4,1)}), s8[4194304]{0:T(1024)(128)(4,1)S(1)}, s32[]{:S(2)}) async-start(s8[6553600]{0:T(1024)(128)(4,1)} %bitcast.13), calls=%async_computation.1 | async-start | bytes 8388608
  81.8 7.5 %slice-start.1 = ((s8[6553600]{0:T(1024)(128)(4,1)}), s8[2359296]{0:T(1024)(128)(4,1)S(1)}, s32[]{:S(2)}) async-start(s8[6553600]{0:T(1024)(128)(4,1)} %bitcast.13), calls=%async_computation.2 | async-start | bytes 4718592
  92.9 11.5 %collective-permute-start.14 = (bf16[272,640]{1,0:T(8,128)(2,1)S(1)}, bf16[272,640]{1,0:T(8,128)(2,1)S(1)}, u32[]{:S(2)}, u32[]{:S(2)}) collective-permute-start(bf16[272,640]{1,0:T(8,128)(2,1)S(1)} %get-tuple-element.106), channel_id=1, source_target_pairs={{0,1},{1,2},{2,3},{3,0},{4,5},{5,6},{6,7},{7,4},{8,9},{9,10},{10,1... | collective-permute-start | bytes 1044488 | tf_op jit(solution)/shard_map/ppermute | solution.py:23
  93.0 11.4 %collective-permute-start.15 = (bf16[272,640]{1,0:T(8,128)(2,1)S(1)}, bf16[272,640]{1,0:T(8,128)(2,1)S(1)}, u32[]{:S(2)}, u32[]{:S(2)}) collective-permute-start(bf16[272,640]{1,0:T(8,128)(2,1)S(1)} %get-tuple-element.108), channel_id=1, source_target_pairs={{0,3},{1,0},{2,1},{3,2},{4,7},{5,4},{6,5},{7,6},{8,11},{9,8},{10,9... | collective-permute-start | bytes 1044488 | tf_op jit(solution)/shard_map/ppermute | solution.py:23
  96.2 15.2 %collective-permute-start.12 = (bf16[256,640]{1,0:T(8,128)(2,1)S(1)}, bf16[256,640]{1,0:T(8,128)(2,1)S(1)}, u32[]{:S(2)}, u32[]{:S(2)}) collective-permute-start(bf16[256,640]{1,0:T(8,128)(2,1)S(1)} %get-tuple-element.103), channel_id=1, source_target_pairs={{0,1},{1,2},{2,3},{3,0},{4,5},{5,6},{6,7},{7,4},{8,9},{9,10},{10,1... | collective-permute-start | bytes 983048 | tf_op jit(solution)/shard_map/ppermute | solution.py:23
  96.2 15.2 %collective-permute-start.13 = (bf16[256,640]{1,0:T(8,128)(2,1)S(1)}, bf16[256,640]{1,0:T(8,128)(2,1)S(1)}, u32[]{:S(2)}, u32[]{:S(2)}) collective-permute-start(bf16[256,640]{1,0:T(8,128)(2,1)S(1)} %get-tuple-element.104), channel_id=1, source_target_pairs={{0,3},{1,0},{2,1},{3,2},{4,7},{5,4},{6,5},{7,6},{8,11},{9,8},{10,9... | collective-permute-start | bytes 983048 | tf_op jit(solution)/shard_map/ppermute | solution.py:23
  105.1 13.8 %collective-permute-start.16 = (bf16[272,640]{1,0:T(8,128)(2,1)S(1)}, bf16[272,640]{1,0:T(8,128)(2,1)S(1)}, u32[]{:S(2)}, u32[]{:S(2)}) collective-permute-start(bf16[272,640]{1,0:T(8,128)(2,1)S(1)} %get-tuple-element.109), channel_id=1, source_target_pairs={{0,1},{1,2},{2,3},{3,0},{4,5},{5,6},{6,7},{7,4},{8,9},{9,10},{10,1... | collective-permute-start | bytes 1044488 | tf_op jit(solution)/shard_map/ppermute | solution.py:23
  106.3 12.0 %collective-permute-start.17 = (bf16[256,640]{1,0:T(8,128)(2,1)S(1)}, bf16[256,640]{1,0:T(8,128)(2,1)S(1)}, u32[]{:S(2)}, u32[]{:S(2)}) collective-permute-start(bf16[256,640]{1,0:T(8,128)(2,1)S(1)} %get-tuple-element.110), channel_id=1, source_target_pairs={{0,3},{1,0},{2,1},{3,2},{4,7},{5,4},{6,5},{7,6},{8,11},{9,8},{10,9... | collective-permute-start | bytes 983048 | tf_op jit(solution)/shard_map/ppermute | solution.py:23
  111.5 2.9 %copy-start.5 = (bf16[1280,2560]{1,0:T(8,128)(2,1)S(1)}, bf16[1280,2560]{1,0:T(8,128)(2,1)}, u32[]{:S(2)}) copy-start(bf16[1280,2560]{1,0:T(8,128)(2,1)} %wo.5) | copy-start | bytes 19660804
  114.3 6.2 %copy-start.1 = (bf16[512,640]{1,0:T(8,128)(2,1)S(1)}, bf16[512,640]{1,0:T(8,128)(2,1)}, u32[]{:S(2)}) copy-start(bf16[512,640]{1,0:T(8,128)(2,1)} %param.16) | copy-start | bytes 1966084

commit v4 on v3

--- a/solution.py
+++ b/solution.py
@@ -405,7 +405,7 @@
 
 def gated_body(
     ids, p, q, bc0, bc1, got_s, got_v, got_w, state0, end_row, gain, wo,
-    z, far_r, far_l, dir_r, dir_l, squares,
+    z, far_r, far_l, squares,
 ):
     carry0 = jnp.where(ids[4] > 0, 1.0, 0.0)
     carry1 = jnp.where(ids[5] > 0, 1.0, 0.0)
@@ -433,8 +433,6 @@
     top, low = block_rows(0), block_rows(1)
     far_r[:STRETCH, :] = dot(z[top, :], wo[:, chunk_of(ids, 3, ncol)]).astype(BF)
     far_l[:STRETCH, :] = dot(z[low, :], wo[:, chunk_of(ids, 3, ncol)]).astype(BF)
-    dir_r[...] = dot(z[low, :], wo[:, chunk_of(ids, 2, ncol)]).astype(BF)
-    dir_l[...] = dot(z[top, :], wo[:, chunk_of(ids, 1, ncol)]).astype(BF)
     row = lax.broadcasted_iota(jnp.int32, (16, STRETCH), 0)
     for block in range(2):
         c = block_rows(block)
@@ -456,28 +454,27 @@
             shape((tok, nv), BF),
             shape((STRETCH + 16, ncol), BF),
             shape((STRETCH + 16, ncol), BF),
-            shape((STRETCH, ncol), BF),
-            shape((STRETCH, ncol), BF),
             shape((8, tok)),
         ],
         (ids, p, q, bc0, bc1, got_s, got_v, got_w, state0, end_row, gain, wo),
         "gated_part",
-        2 * tok * nv * (2 * ncol + 128),
-    )
-
-
-def near_body(ids, z, wo, top_r, low_l):
+        2 * tok * nv * (ncol + 128),
+    )
+
+
+def near_body(ids, z, wo, far_r, far_l, dir_r, dir_l, top_r, low_l):
     ncol = wo.shape[1] // RING
+    dir_r[...] = dot(z[STRETCH:, :], wo[:, chunk_of(ids, 2, ncol)]).astype(BF)
+    dir_l[...] = dot(z[:STRETCH, :], wo[:, chunk_of(ids, 1, ncol)]).astype(BF)
     top_r[...] = dot(z[:STRETCH, :], wo[:, chunk_of(ids, 2, ncol)])
     low_l[...] = dot(z[STRETCH:, :], wo[:, chunk_of(ids, 1, ncol)])
 
 
-def near_part(ids, z, wo):
+def near_part(ids, z, wo, far_r, far_l):
     tok, nv = z.shape
     ncol = wo.shape[1] // RING
-    return call(
-        near_body, [shape((STRETCH, ncol))] * 2, (ids, z, wo), "near_part", 2 * tok * nv * ncol
-    )
+    outs = [shape((STRETCH, ncol), BF)] * 2 + [shape((STRETCH, ncol))] * 2
+    return call(near_body, outs, (ids, z, wo, far_r, far_l), "near_part", 4 * tok * nv * ncol)
 
 
 def mine_body(ids, z, wo, low_r, top_l, own):
@@ -499,17 +496,17 @@
     )[0]
 
 
-def add_body(ids, a1, b1, a2, b2, o1, o2):
+def add_body(ids, a1, b1, a2, b2, sent_r, sent_l, o1, o2):
     o1[:STRETCH, :] = (a1[...] + b1[:STRETCH, :].astype(F32)).astype(BF)
     o1[STRETCH:, :] = b1[STRETCH:, :]
     o2[...] = (a2[...] + b2[:STRETCH, :].astype(F32)).astype(BF)
 
 
-def add_part(ids, a1, b1, a2, b2):
+def add_part(ids, a1, b1, a2, b2, sent_r, sent_l):
     return call(
         add_body,
         [shape(b1.shape, BF), shape(a2.shape, BF)],
-        (ids, a1, b1, a2, b2),
+        (ids, a1, b1, a2, b2, sent_r, sent_l),
         "add_part",
         2 * a1.size,
     )
@@ -626,15 +623,15 @@
     got_w = shifted(joined_low, 2)
     p, q = mix_part(ids, a1, a2, b1, b2, wm, acc0, acc1, head_rows, block0, block1)
 
-    z, far_r, far_l, dir_r, dir_l, squares = gated_part(
+    z, far_r, far_l, squares = gated_part(
         ids, p, q, block0[1], block1[1], got_s, got_v, got_w, state0, end_row, gain, out_proj
     )
     got_r = turned(far_r, 1)
     got_l = turned(far_l, -1)
+    dir_r, dir_l, top_r, low_l = near_part(ids, z, out_proj, far_r, far_l)
     low_r = turned(dir_r, 1)
     top_l = turned(dir_l, -1)
-    top_r, low_l = near_part(ids, z, out_proj)
-    sum_r, sum_l = add_part(ids, top_r, got_r, low_l, got_l)
+    sum_r, sum_l = add_part(ids, top_r, got_r, low_l, got_l, dir_r, dir_l)
     top_r = turned(sum_r, 1)
     low_l = turned(sum_l, -1)
     own = mine_part(ids, z, out_proj, low_r, top_l)

time: 123 us -> 121 us (0.984)
  local copies, waits for them, and re-layouts: 20 us -> 17.2 us
  waiting for transfers between devices: 17.9 us -> 19.5 us
    unnamed x39 -> x41, local copies, waits for them, and re-layouts: 17.7 us -> 14.9 us
    ppermute x14, waiting for transfers between devices: 13.8 us -> 15.5 us  [turned(): lax.ppermute(value, 'head', [(i, (i + steps) % RING) for i in range(RING)])]
  transfers between devices with their start and end apart: 19 -> 19, of which waited for: 8 -> 8; matrix products, arithmetic and copies ran while one was open for 2% -> 2% of each run, Pallas kernels for 25% -> 26%
where the time goes in v4:
time: 121 us; the launch traced here: 120 us
  Pallas kernels  41.6 us (34%)
  starting transfers between devices  38 us (31%)
  waiting for transfers between devices  19.5 us (16%)
  local copies, waits for them, and re-layouts  17.2 us (14%)
  matrix products  2.15 us (2%)
    pallas_call x14, Pallas kernels, call(): pl.pallas_call(body, in_specs=[pl.BlockSpec(memory_space=pltpu.SMEM)] + [...  41.6 us
    ppermute x14, starting transfers between devices, turned(): lax.ppermute(value, 'head', [(i, (i + steps) % RING) for i in range(RING)])  20.8 us
    ppermute x14, waiting for transfers between devices, turned(): lax.ppermute(value, 'head', [(i, (i + steps) % RING) for i in range(RING)])  15.5 us
    unnamed x41, local copies, waits for them, and re-layouts  14.9 us
    ppermute x4, starting transfers between devices, shifted(): lax.ppermute(value, 'ctx', [(i, i + steps) for i in range(count - steps)])  8.84 us
    all_to_all x1, starting transfers between devices, on_device(): lax.all_to_all(outgoing, 'ctx', split_axis=0, concat_axis=0, tiled=True)  8.38 us
    all_to_all x1, waiting for transfers between devices, on_device(): lax.all_to_all(outgoing, 'ctx', split_axis=0, concat_axis=0, tiled=True)  3.98 us
  transfers between devices with their start and end apart: 19, of which 8 were waited for; matrix products, arithmetic and copies ran while one was open for 2% of the time, Pallas kernels for 26%

profile of v4, /device:TPU:0, one launch (start us, length us, event | category | flops | bytes accessed | tf_op | source)
XLA Modules:
  0.0 119.6 jit_solution(16877006256210244565)
XLA Ops:
  0.0 0.9 eq.20
  0.9 0.2 copy-done
  1.1 2.2 %fusion.1 = bf16[1024,640]{1,0:T(8,128)(2,1)} fusion(bf16[512,640]{1,0:T(8,128)(2,1)S(1)} %copy-done, s32[1024]{0:T(1024)S(1)} %eq.20), kind=kOutput, calls=%fused_computation.4 | convolution fusion | flops 672268288 | bytes 1970176 | tf_op jit(solution)/shard_map/dot_general | solution.py:19
  3.3 8.4 %all-to-all-start = ((bf16[32,32,640]{2,1,0:T(8,128)(2,1)}), bf16[32,32,640]{2,1,0:T(8,128)(2,1)S(1)}, u32[]{:S(2)}, u32[]{:S(2)}) async-start(bf16[32,32,640]{2,1,0:T(8,128)(2,1)} %bitcast.18), calls=%async_computation | async-start | bytes 2621440 | tf_op jit(solution)/shard_map/all_to_all | solution.py:567
  11.7 0.6 gather_fusion
  12.4 0.6 gather_fusion.1
  13.0 0.2 fusion.4
  13.3 0.1 reduce.1
  13.6 0.1 and_select_fusion.1
  13.8 4.7 %copy-done.6 = bf16[2560,2,1280]{2,1,0:T(2,128)(2,1)S(1)} copy-done((bf16[2560,2,1280]{2,1,0:T(2,128)(2,1)S(1)}, bf16[2560,2,1280]{2,1,0:T(2,128)(2,1)}, u32[]{:S(2)}) %copy-start.6) | copy-done | bytes 13107224
  18.5 4.3 %flat_part.1.wm = bf16[2560,2560]{1,0:T(8,128)(2,1)S(1)} custom-call(s32[6]{0:T(128)S(1)} %pad_add_fusion.ids, bf16[2560,2,1280]{2,1,0:T(2,128)(2,1)S(1)} %copy-done.6), custom_call_target="tpu_custom_call" | custom-call | flops 1000000000 | bytes 26214400 | tf_op jit(solution)/shard_map/flat_part/pallas_call | solution.py:59
  22.8 4.7 %copy-done.2 = bf16[2560,2560]{1,0:T(8,128)(2,1)} copy-done((bf16[2560,2560]{1,0:T(8,128)(2,1)}, bf16[2560,2560]{1,0:T(8,128)(2,1)S(1)}, u32[]{:S(2)}) %copy-start.2) | copy-done | bytes 13107224
  27.6 4.0 %all-to-all-done = bf16[32,32,640]{2,1,0:T(8,128)(2,1)S(1)} async-done(((bf16[32,32,640]{2,1,0:T(8,128)(2,1)}), bf16[32,32,640]{2,1,0:T(8,128)(2,1)S(1)}, u32[]{:S(2)}, u32[]{:S(2)}) %all-to-all-start) | async-done | bytes 1310752 | tf_op jit(solution)/shard_map/all_to_all | solution.py:567
  31.6 1.5 %arrange_part.1 = (bf16[272,640]{1,0:T(8,128)(2,1)S(1)}, bf16[240,640]{1,0:T(8,128)(2,1)S(1)}, bf16[16,640]{1,0:T(8,128)(2,1)S(1)}) custom-call(s32[6]{0:T(128)S(1)} %pad_add_fusion.ids, s32[1,1024]{1,0:T(1,128)S(1)} %select_n.56.target, bf16[1024,640]{1,0:T(8,128)(2,1)S(1)} %bitcast.17), custom_call_target="tpu_custom_call" | custom-call | flops 671088640 | bytes 1990656 | tf_op jit(solution)/shard_map/arrange_part/pallas_call | solution.py:59
  33.1 3.1 %collective-permute-start.1 = (bf16[272,640]{1,0:T(8,128)(2,1)S(1)}, bf16[272,640]{1,0:T(8,128)(2,1)S(1)}, u32[]{:S(2)}, u32[]{:S(2)}) collective-permute-start(bf16[272,640]{1,0:T(8,128)(2,1)S(1)} %get-tuple-element.62.x), channel_id=1, source_target_pairs={{0,3},{1,0},{2,1},{3,2},{4,7},{5,4},{6,5},{7,6},{8,11},{9,8},{10,9... | collective-permute-start | bytes 1044488 | tf_op jit(solution)/shard_map/ppermute | solution.py:23
  36.2 0.4 copy.21.tp
  36.6 1.8 %collective-permute-start.2 = (bf16[16,640]{1,0:T(8,128)(2,1)S(1)}, bf16[16,640]{1,0:T(8,128)(2,1)S(1)}, u32[]{:S(2)}, u32[]{:S(2)}) collective-permute-start(bf16[16,640]{1,0:T(8,128)(2,1)S(1)} %get-tuple-element.64), channel_id=1, source_target_pairs={{0,4},{4,8},{8,12},{12,16},{16,20},{20,24},{24,28},{28,32},{32,36}... | collective-permute-start | bytes 61448 | tf_op jit(solution)/shard_map/ppermute | solution.py:28
  38.4 4.7 %copy-done.3 = bf16[2560,2560]{1,0:T(8,128)(2,1)S(1)} copy-done((bf16[2560,2560]{1,0:T(8,128)(2,1)S(1)}, bf16[2560,2560]{1,0:T(8,128)(2,1)}, u32[]{:S(2)}) %copy-start.3) | copy-done | bytes 13107224
  43.1 2.0 %own_part.2.before = f32[272,2944]{1,0:T(8,128)S(1)} custom-call(s32[6]{0:T(128)S(1)} %pad_add_fusion.ids, bf16[272,640]{1,0:T(8,128)(2,1)S(1)} %get-tuple-element.62.x, bf16[2560,256]{1,0:T(8,128)(2,1)S(1)} %copy-done.5, bf16[2560,20]{1,0:T(8,128)(2,1)S(1)} %copy.21.tp, bf16[2560,2560]{1,0:T(8,128)(2,1)S(1)} %copy-done.3), custom_call_target="tpu_custom_call" | custom-call | flops 1024983040 | bytes 18071552 | tf_op jit(solution)/shard_map/own_part/pallas_call | solution.py:59
  45.2 2.2 %collective-permute-done.r = bf16[272,640]{1,0:T(8,128)(2,1)S(1)} collective-permute-done((bf16[272,640]{1,0:T(8,128)(2,1)S(1)}, bf16[272,640]{1,0:T(8,128)(2,1)S(1)}, u32[]{:S(2)}, u32[]{:S(2)}) %collective-permute-start) | collective-permute-done | bytes 348192 | tf_op jit(solution)/shard_map/ppermute | solution.py:23
  47.4 0.8 collective-permute-start.6
  48.2 1.2 %collective-permute-start.5 = (bf16[144,640]{1,0:T(8,128)(2,1)S(1)}, bf16[144,640]{1,0:T(8,128)(2,1)S(1)}, u32[]{:S(2)}, u32[]{:S(2)}) collective-permute-start(bf16[144,640]{1,0:T(8,128)(2,1)S(1)} %slice.12), channel_id=1, source_target_pairs={{0,1},{1,2},{2,3},{3,0},{4,5},{5,6},{6,7},{7,4},{8,9},{9,10},{10,1... | collective-permute-start | bytes 552968 | tf_op jit(solution)/shard_map/ppermute | solution.py:23
  49.5 3.4 %next_part.2.acc.acc1 = f32[272,2944]{1,0:T(8,128)S(1)} custom-call(s32[6]{0:T(128)S(1)} %pad_add_fusion.ids, bf16[272,640]{1,0:T(8,128)(2,1)S(1)} %collective-permute-done.r, bf16[272,640]{1,0:T(8,128)(2,1)S(1)} %collective-permute-done.1.l, bf16[2560,256]{1,0:T(8,128)(2,1)S(1)} %copy-done.5, bf16[2560,20]{1,0:T(8,128)(2,1)S(1)} %copy.21.tp, ...), custom_call_target="tpu_custom_call" | custom-call | flops 2049966080 | bytes 21622784 | tf_op jit(solution)/shard_map/next_part/pallas_call | solution.py:59
  52.9 2.1 %collective-permute-start.4 = (bf16[256,640]{1,0:T(8,128)(2,1)S(1)}, bf16[256,640]{1,0:T(8,128)(2,1)S(1)}, u32[]{:S(2)}, u32[]{:S(2)}) collective-permute-start(bf16[256,640]{1,0:T(8,128)(2,1)S(1)} %pad_maximum_fusion.x), channel_id=1, source_target_pairs={{0,3},{1,0},{2,1},{3,2},{4,7},{5,4},{6,5},{7,6},{8,11},{9,8},{10,9... | collective-permute-start | bytes 983048 | tf_op jit(solution)/shard_map/ppermute | solution.py:23
  55.0 1.9 %own_part.3.before = f32[256,2944]{1,0:T(8,128)S(1)} custom-call(s32[6]{0:T(128)S(1)} %pad_add_fusion.ids, bf16[256,640]{1,0:T(8,128)(2,1)S(1)} %pad_maximum_fusion.x, bf16[2560,256]{1,0:T(8,128)(2,1)S(1)} %copy-done.5, bf16[2560,20]{1,0:T(8,128)(2,1)S(1)} %copy.21.tp, bf16[2560,2560]{1,0:T(8,128)(2,1)S(1)} %copy-done.4), custom_call_target="tpu_custom_call" | custom-call | flops 964689920 | bytes 17862656 | tf_op jit(solution)/shard_map/own_part/pallas_call | solution.py:59
  56.9 4.3 %second_part.1 = (bf16[256,1280]{1,0:T(8,128)(2,1)S(1)}, bf16[256,256]{1,0:T(8,128)(2,1)S(1)}, bf16[256,128]{1,0:T(8,128)(2,1)S(1)}, f32[32,256]{1,0:T(8,128)S(1...) custom-call(s32[6]{0:T(128)S(1)} %pad_add_fusion.ids, ...), custom_call_target="tpu_custom_call" | custom-call | flops 1090519040 | bytes 19558400 | tf_op jit(solution)/shard_map/second_part/pallas_call | solution.py:59
  61.2 1.6 %collective-permute-start.9 = (bf16[144,1280]{1,0:T(8,128)(2,1)S(1)}, bf16[144,1280]{1,0:T(8,128)(2,1)S(1)}, u32[]{:S(2)}, u32[]{:S(2)}) collective-permute-start(bf16[144,1280]{1,0:T(8,128)(2,1)S(1)} %get-tuple-element.77), channel_id=1, source_target_pairs={{0,4},{4,8},{8,12},{12,16},{16,20},{20,24},{24,28},{28,32},{32,36}... | collective-permute-start | bytes 1105928 | tf_op jit(solution)/shard_map/ppermute | solution.py:28
  62.9 2.6 %collective-permute-done.3.r = bf16[256,640]{1,0:T(8,128)(2,1)S(1)} collective-permute-done((bf16[256,640]{1,0:T(8,128)(2,1)S(1)}, bf16[256,640]{1,0:T(8,128)(2,1)S(1)}, u32[]{:S(2)}, u32[]{:S(2)}) %collective-permute-start.3) | collective-permute-done | bytes 327712 | tf_op jit(solution)/shard_map/ppermute | solution.py:23
  65.6 3.2 %collective-permute-start.8 = (bf16[128,640]{1,0:T(8,128)(2,1)S(1)}, bf16[128,640]{1,0:T(8,128)(2,1)S(1)}, u32[]{:S(2)}, u32[]{:S(2)}) collective-permute-start(bf16[128,640]{1,0:T(8,128)(2,1)S(1)} %slice.15), channel_id=1, source_target_pairs={{0,3},{1,0},{2,1},{3,2},{4,7},{5,4},{6,5},{7,6},{8,11},{9,8},{10,9... | collective-permute-start | bytes 491528 | tf_op jit(solution)/shard_map/ppermute | solution.py:23
  68.9 3.2 %next_part.3.acc.acc0 = f32[256,2944]{1,0:T(8,128)S(1)} custom-call(s32[6]{0:T(128)S(1)} %pad_add_fusion.ids, bf16[256,640]{1,0:T(8,128)(2,1)S(1)} %collective-permute-done.3.r, bf16[256,640]{1,0:T(8,128)(2,1)S(1)} %collective-permute-done.4.l, bf16[2560,256]{1,0:T(8,128)(2,1)S(1)} %copy-done.5, bf16[2560,20]{1,0:T(8,128)(2,1)S(1)} %copy.21.tp, ...), custom_call_target="tpu_custom_call" | custom-call | flops 1929379840 | bytes 21204992 | tf_op jit(solution)/shard_map/next_part/pallas_call | solution.py:59
  72.1 0.1 collective-permute-done.7.o1.a1
  72.2 4.2 %first_part.1 = (bf16[256,1280]{1,0:T(8,128)(2,1)S(1)}, bf16[256,256]{1,0:T(8,128)(2,1)S(1)}, bf16[256,128]{1,0:T(8,128)(2,1)S(1)}, f32[32,256]{1,0:T(8,128)S(1)...) custom-call(s32[6]{0:T(128)S(1)} %pad_add_fusion.ids, ...), custom_call_target="tpu_custom_call" | custom-call | flops 1090519040 | bytes 20742144 | tf_op jit(solution)/shard_map/first_part/pallas_call | solution.py:59
  76.4 3.9 %collective-permute-start.11 = (bf16[128,1280]{1,0:T(8,128)(2,1)S(1)}, bf16[128,1280]{1,0:T(8,128)(2,1)S(1)}, u32[]{:S(2)}, u32[]{:S(2)}) collective-permute-start(bf16[128,1280]{1,0:T(8,128)(2,1)S(1)} %get-tuple-element.98), channel_id=1, source_target_pairs={{0,8},{4,12},{8,16},{12,20},{16,24},{20,28},{24,32},{28,36},{32,40... | collective-permute-start | bytes 983048 | tf_op jit(solution)/shard_map/ppermute | solution.py:28
  80.3 1.5 %collective-permute-start.10 = (bf16[144,1280]{1,0:T(8,128)(2,1)S(1)}, bf16[144,1280]{1,0:T(8,128)(2,1)S(1)}, u32[]{:S(2)}, u32[]{:S(2)}) collective-permute-start(bf16[144,1280]{1,0:T(8,128)(2,1)S(1)} %get-tuple-element.97), channel_id=1, source_target_pairs={{0,4},{4,8},{8,12},{12,16},{16,20},{20,24},{24,28},{28,32},{32,36}... | collective-permute-start | bytes 1105928 | tf_op jit(solution)/shard_map/ppermute | solution.py:28
  81.9 7.4 %mix_part.1 = (f32[512,1280]{1,0:T(8,128)S(1)}, f32[512,1280]{1,0:T(8,128)S(1)}) custom-call(s32[6]{0:T(128)S(1)} %pad_add_fusion.ids, bf16[128,640]{1,0:T(8,128)(2,1)S(1)} %collective-permute-done.7.o1.a1, bf16[128,640]{1,0:T(8,128)(2,1)S(1)} %collective-permute-done.8.o2.a2, bf16[144,640]{1,0:T(8,128)(2,1)S(1)} %collective-permute-done.5.o1.b1, ...), custom_call_target="tpu_custom_call" | custom-call | flops 8000000000 | bytes 27213824 | tf_op jit(solution)/shard_map/mix_part/pallas_call | solution.py:59
  89.3 2.6 %gated_part.1 = (bf16[512,1280]{1,0:T(8,128)(2,1)S(1)}, bf16[272,640]{1,0:T(8,128)(2,1)S(1)}, bf16[272,640]{1,0:T(8,128)(2,1)S(1)}, f32[8,512]{1,0:T(8,128)S(1)}) custom-call(s32[6]{0:T(128)S(1)} %pad_add_fusion.ids, f32[512,1280]{1,0:T(8,128)S(1)} %get-tuple-element.95.p, f32[512,1280]{1,0:T(8,128)S(1)} %get-tuple-element.96.q, ...), custom_call_target="tpu_custom_call" | custom-call | flops 1006632960 | bytes 15848448 | tf_op jit(solution)/shard_map/gated_part/pallas_call | solution.py:59
  92.0 3.2 %collective-permute-start.15 = (bf16[272,640]{1,0:T(8,128)(2,1)S(1)}, bf16[272,640]{1,0:T(8,128)(2,1)S(1)}, u32[]{:S(2)}, u32[]{:S(2)}) collective-permute-start(bf16[272,640]{1,0:T(8,128)(2,1)S(1)} %get-tuple-element.104.far_l), channel_id=1, source_target_pairs={{0,3},{1,0},{2,1},{3,2},{4,7},{5,4},{6,5},{7,6},{8,11},{9,8},{10,9... | collective-permute-start | bytes 1044488 | tf_op jit(solution)/shard_map/ppermute | solution.py:23
  95.2 2.8 %near_part.1 = (bf16[256,640]{1,0:T(8,128)(2,1)S(1)}, bf16[256,640]{1,0:T(8,128)(2,1)S(1)}, f32[256,640]{1,0:T(8,128)S(1)}, f32[256,640]{1,0:T(8,128)S(1)}) custom-call(s32[6]{0:T(128)S(1)} %pad_add_fusion.ids, bf16[512,1280]{1,0:T(8,128)(2,1)S(1)} %get-tuple-element.102.z, bf16[1280,2560]{1,0:T(8,128)(2,1)S(1)} %bitcast.14, ...), custom_call_target="tpu_custom_call" | custom-call | flops 1677721600 | bytes 10526720 | tf_op jit(solution)/shard_map/near_part/pallas_call | solution.py:59
  98.1 3.2 %collective-permute-start.13 = (bf16[256,640]{1,0:T(8,128)(2,1)S(1)}, bf16[256,640]{1,0:T(8,128)(2,1)S(1)}, u32[]{:S(2)}, u32[]{:S(2)}) collective-permute-start(bf16[256,640]{1,0:T(8,128)(2,1)S(1)} %get-tuple-element.106.sent_l), channel_id=1, source_target_pairs={{0,3},{1,0},{2,1},{3,2},{4,7},{5,4},{6,5},{7,6},{8,11},{9,8},{10,9... | collective-permute-start | bytes 983048 | tf_op jit(solution)/shard_map/ppermute | solution.py:23
  101.3 2.1 %collective-permute-done.14.b1.sq_r = bf16[272,640]{1,0:T(8,128)(2,1)S(1)} collective-permute-done((bf16[272,640]{1,0:T(8,128)(2,1)S(1)}, bf16[272,640]{1,0:T(8,128)(2,1)S(1)}, u32[]{:S(2)}, u32[]{:S(2)}) %collective-permute-start.14) | collective-permute-done | bytes 348192 | tf_op jit(solution)/shard_map/ppermute | solution.py:23
  103.5 0.7 add_part.1
  104.2 1.2 %collective-permute-start.16 = (bf16[272,640]{1,0:T(8,128)(2,1)S(1)}, bf16[272,640]{1,0:T(8,128)(2,1)S(1)}, u32[]{:S(2)}, u32[]{:S(2)}) collective-permute-start(bf16[272,640]{1,0:T(8,128)(2,1)S(1)} %get-tuple-element.109), channel_id=1, source_target_pairs={{0,1},{1,2},{2,3},{3,0},{4,5},{5,6},{6,7},{7,4},{8,9},{9,10},{10,1... | collective-permute-start | bytes 1044488 | tf_op jit(solution)/shard_map/ppermute | solution.py:23
  105.4 2.4 %collective-permute-start.17 = (bf16[256,640]{1,0:T(8,128)(2,1)S(1)}, bf16[256,640]{1,0:T(8,128)(2,1)S(1)}, u32[]{:S(2)}, u32[]{:S(2)}) collective-permute-start(bf16[256,640]{1,0:T(8,128)(2,1)S(1)} %get-tuple-element.110), channel_id=1, source_target_pairs={{0,3},{1,0},{2,1},{3,2},{4,7},{5,4},{6,5},{7,6},{8,11},{9,8},{10,9... | collective-permute-start | bytes 983048 | tf_op jit(solution)/shard_map/ppermute | solution.py:23
  107.8 2.7 %collective-permute-done.12.low_r = bf16[256,640]{1,0:T(8,128)(2,1)S(1)} collective-permute-done((bf16[256,640]{1,0:T(8,128)(2,1)S(1)}, bf16[256,640]{1,0:T(8,128)(2,1)S(1)}, u32[]{:S(2)}, u32[]{:S(2)}) %collective-permute-start.12) | collective-permute-done | bytes 327712 | tf_op jit(solution)/shard_map/ppermute | solution.py:23
  110.5 1.7 %mine_part.1.own = f32[512,640]{1,0:T(8,128)S(1)} custom-call(s32[6]{0:T(128)S(1)} %pad_add_fusion.ids, bf16[512,1280]{1,0:T(8,128)(2,1)S(1)} %get-tuple-element.102.z, bf16[1280,2560]{1,0:T(8,128)(2,1)S(1)} %bitcast.16, bf16[256,640]{1,0:T(8,128)(2,1)S(1)} %collective-permute-done.12.low_r, bf16[256,640]{1,0:T(8,128)(2,1)S(1)} %collective-permute-done.13.top_l), custom_call_target="tpu_custom_call" | custom-call | flops 1677721600 | bytes 9830400 | tf_op jit(solution)/shard_map/mine_part/pallas_call | solution.py:59
  112.3 5.0 %collective-permute-done.17.low_l = bf16[256,640]{1,0:T(8,128)(2,1)S(1)} collective-permute-done((bf16[256,640]{1,0:T(8,128)(2,1)S(1)}, bf16[256,640]{1,0:T(8,128)(2,1)S(1)}, u32[]{:S(2)}, u32[]{:S(2)}) %collective-permute-start.17) | collective-permute-done | bytes 327712 | tf_op jit(solution)/shard_map/ppermute | solution.py:23
  117.3 0.7 collective-permute-done.16.top_r
  117.9 1.6 %final_part.1 = bf16[512,640]{1,0:T(8,128)(2,1)} custom-call(s32[6]{0:T(128)S(1)} %pad_add_fusion.ids, f32[512,640]{1,0:T(8,128)S(1)} %mine_part.1.own, bf16[272,640]{1,0:T(8,128)(2,1)S(1)} %collective-permute-done.16.top_r, bf16[256,640]{1,0:T(8,128)(2,1)S(1)} %collective-permute-done.17.low_l, f32[8,512]{1,0:T(8,128)S(1)} %get-tuple-element.111.mine, ...), custom_call_target="tpu_custom_call" | custom-call | flops 1310720 | bytes 3354624 | tf_op jit(solution)/shard_map/final_part/pallas_call | solution.py:59
  (73 shorter events, 0.8 us)
Async XLA Ops:
  0.0 1.1 copy-start
  1.1 10.6 %copy-start.14 = (f32[20]{0:T(128)S(1)}, f32[20]{0:T(128)}, u32[]{:S(2)}) copy-start(f32[20]{0:T(128)} %param.26) | copy-start | bytes 244
  1.1 10.6 %copy-start.9 = (s32[64]{0:T(128)S(1)}, s32[64]{0:T(128)}, u32[]{:S(2)}) copy-start(s32[64]{0:T(128)} %param.19) | copy-start | bytes 772
  3.3 9.8 %copy-start.12 = (f32[1280]{0:T(1024)S(1)}, f32[1280]{0:T(1024)}, u32[]{:S(2)}) copy-start(f32[1280]{0:T(1024)} %param.28) | copy-start | bytes 15364
  3.3 9.8 %copy-start.11 = (s32[32,32]{1,0:T(8,128)S(1)}, s32[32,32]{1,0:T(8,128)}, u32[]{:S(2)}) copy-start(s32[32,32]{1,0:T(8,128)} %param.18) | copy-start | bytes 12292
  3.3 28.3 %all-to-all-start = ((bf16[32,32,640]{2,1,0:T(8,128)(2,1)}), bf16[32,32,640]{2,1,0:T(8,128)(2,1)S(1)}, u32[]{:S(2)}, u32[]{:S(2)}) async-start(bf16[32,32,640]{2,1,0:T(8,128)(2,1)} %bitcast.18), calls=%async_computation | async-start | bytes 2621440 | tf_op jit(solution)/shard_map/all_to_all | solution.py:567
  13.8 4.7 %copy-start.6 = (bf16[2560,2,1280]{2,1,0:T(2,128)(2,1)S(1)}, bf16[2560,2,1280]{2,1,0:T(2,128)(2,1)}, u32[]{:S(2)}) copy-start(bf16[2560,2,1280]{2,1,0:T(2,128)(2,1)} %w.1) | copy-start | bytes 39321604
  18.5 9.1 %copy-start.15 = (f32[20]{0:T(128)S(1)}, f32[20]{0:T(128)}, u32[]{:S(2)}) copy-start(f32[20]{0:T(128)} %param.25) | copy-start | bytes 244
  18.5 9.1 %copy-start.13 = (f32[20]{0:T(128)S(1)}, f32[20]{0:T(128)}, u32[]{:S(2)}) copy-start(f32[20]{0:T(128)} %param.27) | copy-start | bytes 244
  18.5 17.8 %copy-start.10 = (bf16[2560,20]{0,1:T(8,128)(2,1)S(1)}, bf16[2560,20]{0,1:T(8,128)(2,1)}, u32[]{:S(2)}) copy-start(bf16[2560,20]{0,1:T(8,128)(2,1)} %param.22) | copy-start | bytes 307204
  22.8 4.8 %copy-start.2 = (bf16[2560,2560]{1,0:T(8,128)(2,1)}, bf16[2560,2560]{1,0:T(8,128)(2,1)S(1)}, u32[]{:S(2)}) copy-start(bf16[2560,2560]{1,0:T(8,128)(2,1)S(1)} %flat_part.1.wm) | copy-start | bytes 39321604
  27.6 10.8 %copy-start.5 = (bf16[2560,256]{1,0:T(8,128)(2,1)S(1)}, bf16[2560,256]{1,0:T(8,128)(2,1)}, u32[]{:S(2)}) copy-start(bf16[2560,256]{1,0:T(8,128)(2,1)} %sp.11) | copy-start | bytes 3932164
  33.1 12.0 %collective-permute-start.1 = (bf16[272,640]{1,0:T(8,128)(2,1)S(1)}, bf16[272,640]{1,0:T(8,128)(2,1)S(1)}, u32[]{:S(2)}, u32[]{:S(2)}) collective-permute-start(bf16[272,640]{1,0:T(8,128)(2,1)S(1)} %get-tuple-element.62.x), channel_id=1, source_target_pairs={{0,3},{1,0},{2,1},{3,2},{4,7},{5,4},{6,5},{7,6},{8,11},{9,8},{10,9... | collective-permute-start | bytes 1044488 | tf_op jit(solution)/shard_map/ppermute | solution.py:23
  36.2 11.1 %collective-permute-start = (bf16[272,640]{1,0:T(8,128)(2,1)S(1)}, bf16[272,640]{1,0:T(8,128)(2,1)S(1)}, u32[]{:S(2)}, u32[]{:S(2)}) collective-permute-start(bf16[272,640]{1,0:T(8,128)(2,1)S(1)} %get-tuple-element.62.x), channel_id=1, source_target_pairs={{0,1},{1,2},{2,3},{3,0},{4,5},{5,6},{6,7},{7,4},{8,9},{9,10},{10,1... | collective-permute-start | bytes 1044488 | tf_op jit(solution)/shard_map/ppermute | solution.py:23
  36.6 8.5 %collective-permute-start.2 = (bf16[16,640]{1,0:T(8,128)(2,1)S(1)}, bf16[16,640]{1,0:T(8,128)(2,1)S(1)}, u32[]{:S(2)}, u32[]{:S(2)}) collective-permute-start(bf16[16,640]{1,0:T(8,128)(2,1)S(1)} %get-tuple-element.64), channel_id=1, source_target_pairs={{0,4},{4,8},{8,12},{12,16},{16,20},{20,24},{24,28},{28,32},{32,36}... | collective-permute-start | bytes 61448 | tf_op jit(solution)/shard_map/ppermute | solution.py:28
  38.4 4.7 %copy-start.3 = (bf16[2560,2560]{1,0:T(8,128)(2,1)S(1)}, bf16[2560,2560]{1,0:T(8,128)(2,1)}, u32[]{:S(2)}) copy-start(bf16[2560,2560]{1,0:T(8,128)(2,1)} %copy-done.2) | copy-start | bytes 39321604
  43.1 6.4 %copy-start.4 = (bf16[2560,2560]{1,0:T(8,128)(2,1)S(1)}, bf16[2560,2560]{1,0:T(8,128)(2,1)}, u32[]{:S(2)}) copy-start(bf16[2560,2560]{1,0:T(8,128)(2,1)} %copy-done.2) | copy-start | bytes 39321604
  47.4 9.5 %collective-permute-start.6 = (bf16[128,640]{1,0:T(8,128)(2,1)S(1)}, bf16[128,640]{1,0:T(8,128)(2,1)S(1)}, u32[]{:S(2)}, u32[]{:S(2)}) collective-permute-start(bf16[128,640]{1,0:T(8,128)(2,1)S(1)} %slice.13), channel_id=1, source_target_pairs={{0,3},{1,0},{2,1},{3,2},{4,7},{5,4},{6,5},{7,6},{8,11},{9,8},{10,9... | collective-permute-start | bytes 491528 | tf_op jit(solution)/shard_map/ppermute | solution.py:23
  48.2 8.7 %collective-permute-start.5 = (bf16[144,640]{1,0:T(8,128)(2,1)S(1)}, bf16[144,640]{1,0:T(8,128)(2,1)S(1)}, u32[]{:S(2)}, u32[]{:S(2)}) collective-permute-start(bf16[144,640]{1,0:T(8,128)(2,1)S(1)} %slice.12), channel_id=1, source_target_pairs={{0,1},{1,2},{2,3},{3,0},{4,5},{5,6},{6,7},{7,4},{8,9},{9,10},{10,1... | collective-permute-start | bytes 552968 | tf_op jit(solution)/shard_map/ppermute | solution.py:23
  52.9 4.1 %copy-start.7 = (f32[4,1280]{1,0:T(4,128)S(1)}, f32[4,1280]{1,0:T(4,128)}, u32[]{:S(2)}) copy-start(f32[4,1280]{1,0:T(4,128)} %taps_v.3) | copy-start | bytes 61444
  52.9 4.1 %copy-start.8 = (f32[4,256]{1,0:T(4,128)S(1)}, f32[4,256]{1,0:T(4,128)}, u32[]{:S(2)}) copy-start(f32[4,256]{1,0:T(4,128)} %taps_s.3) | copy-start | bytes 12292
  52.9 10.0 %collective-permute-start.4 = (bf16[256,640]{1,0:T(8,128)(2,1)S(1)}, bf16[256,640]{1,0:T(8,128)(2,1)S(1)}, u32[]{:S(2)}, u32[]{:S(2)}) collective-permute-start(bf16[256,640]{1,0:T(8,128)(2,1)S(1)} %pad_maximum_fusion.x), channel_id=1, source_target_pairs={{0,3},{1,0},{2,1},{3,2},{4,7},{5,4},{6,5},{7,6},{8,11},{9,8},{10,9... | collective-permute-start | bytes 983048 | tf_op jit(solution)/shard_map/ppermute | solution.py:23
  54.9 10.6 %collective-permute-start.3 = (bf16[256,640]{1,0:T(8,128)(2,1)S(1)}, bf16[256,640]{1,0:T(8,128)(2,1)S(1)}, u32[]{:S(2)}, u32[]{:S(2)}) collective-permute-start(bf16[256,640]{1,0:T(8,128)(2,1)S(1)} %pad_maximum_fusion.x), channel_id=1, source_target_pairs={{0,1},{1,2},{2,3},{3,0},{4,5},{5,6},{6,7},{7,4},{8,9},{9,10},{10,1... | collective-permute-start | bytes 983048 | tf_op jit(solution)/shard_map/ppermute | solution.py:23
  61.2 11.0 %collective-permute-start.9 = (bf16[144,1280]{1,0:T(8,128)(2,1)S(1)}, bf16[144,1280]{1,0:T(8,128)(2,1)S(1)}, u32[]{:S(2)}, u32[]{:S(2)}) collective-permute-start(bf16[144,1280]{1,0:T(8,128)(2,1)S(1)} %get-tuple-element.77), channel_id=1, source_target_pairs={{0,4},{4,8},{8,12},{12,16},{16,20},{20,24},{24,28},{28,32},{32,36}... | collective-permute-start | bytes 1105928 | tf_op jit(solution)/shard_map/ppermute | solution.py:28
  65.6 6.6 %collective-permute-start.7 = (bf16[128,640]{1,0:T(8,128)(2,1)S(1)}, bf16[128,640]{1,0:T(8,128)(2,1)S(1)}, u32[]{:S(2)}, u32[]{:S(2)}) collective-permute-start(bf16[128,640]{1,0:T(8,128)(2,1)S(1)} %slice.14), channel_id=1, source_target_pairs={{0,1},{1,2},{2,3},{3,0},{4,5},{5,6},{6,7},{7,4},{8,9},{9,10},{10,1... | collective-permute-start | bytes 491528 | tf_op jit(solution)/shard_map/ppermute | solution.py:23
  65.6 6.5 %collective-permute-start.8 = (bf16[128,640]{1,0:T(8,128)(2,1)S(1)}, bf16[128,640]{1,0:T(8,128)(2,1)S(1)}, u32[]{:S(2)}, u32[]{:S(2)}) collective-permute-start(bf16[128,640]{1,0:T(8,128)(2,1)S(1)} %slice.15), channel_id=1, source_target_pairs={{0,3},{1,0},{2,1},{3,2},{4,7},{5,4},{6,5},{7,6},{8,11},{9,8},{10,9... | collective-permute-start | bytes 491528 | tf_op jit(solution)/shard_map/ppermute | solution.py:23
  76.4 12.9 %collective-permute-start.11 = (bf16[128,1280]{1,0:T(8,128)(2,1)S(1)}, bf16[128,1280]{1,0:T(8,128)(2,1)S(1)}, u32[]{:S(2)}, u32[]{:S(2)}) collective-permute-start(bf16[128,1280]{1,0:T(8,128)(2,1)S(1)} %get-tuple-element.98), channel_id=1, source_target_pairs={{0,8},{4,12},{8,16},{12,20},{16,24},{20,28},{24,32},{28,36},{32,40... | collective-permute-start | bytes 983048 | tf_op jit(solution)/shard_map/ppermute | solution.py:28
  80.3 9.0 %collective-permute-start.10 = (bf16[144,1280]{1,0:T(8,128)(2,1)S(1)}, bf16[144,1280]{1,0:T(8,128)(2,1)S(1)}, u32[]{:S(2)}, u32[]{:S(2)}) collective-permute-start(bf16[144,1280]{1,0:T(8,128)(2,1)S(1)} %get-tuple-element.97), channel_id=1, source_target_pairs={{0,4},{4,8},{8,12},{12,16},{16,20},{20,24},{24,28},{28,32},{32,36}... | collective-permute-start | bytes 1105928 | tf_op jit(solution)/shard_map/ppermute | solution.py:28
  81.8 7.4 %slice-start = ((s8[6553600]{0:T(1024)(128)(4,1)}), s8[4194304]{0:T(1024)(128)(4,1)S(1)}, s32[]{:S(2)}) async-start(s8[6553600]{0:T(1024)(128)(4,1)} %bitcast.13), calls=%async_computation.1 | async-start | bytes 8388608
  81.8 7.4 %slice-start.1 = ((s8[6553600]{0:T(1024)(128)(4,1)}), s8[2359296]{0:T(1024)(128)(4,1)S(1)}, s32[]{:S(2)}) async-start(s8[6553600]{0:T(1024)(128)(4,1)} %bitcast.13), calls=%async_computation.2 | async-start | bytes 4718592
  89.3 21.2 %slice-start.2 = ((s8[6553600]{0:T(1024)(128)(4,1)}), s8[4194304]{0:T(1024)(128)(4,1)S(1)}, s32[]{:S(2)}) async-start(s8[6553600]{0:T(1024)(128)(4,1)} %bitcast.15), calls=%async_computation.3 | async-start | bytes 8388608
  89.3 21.2 %slice-start.3 = ((s8[6553600]{0:T(1024)(128)(4,1)}), s8[2359296]{0:T(1024)(128)(4,1)S(1)}, s32[]{:S(2)}) async-start(s8[6553600]{0:T(1024)(128)(4,1)} %bitcast.15), calls=%async_computation.4 | async-start | bytes 4718592
  91.9 11.5 %collective-permute-start.14 = (bf16[272,640]{1,0:T(8,128)(2,1)S(1)}, bf16[272,640]{1,0:T(8,128)(2,1)S(1)}, u32[]{:S(2)}, u32[]{:S(2)}) collective-permute-start(bf16[272,640]{1,0:T(8,128)(2,1)S(1)} %get-tuple-element.103.far_r), channel_id=1, source_target_pairs={{0,1},{1,2},{2,3},{3,0},{4,5},{5,6},{6,7},{7,4},{8,9},{9,10},{10,1... | collective-permute-start | bytes 1044488 | tf_op jit(solution)/shard_map/ppermute | solution.py:23
  92.0 11.5 %collective-permute-start.15 = (bf16[272,640]{1,0:T(8,128)(2,1)S(1)}, bf16[272,640]{1,0:T(8,128)(2,1)S(1)}, u32[]{:S(2)}, u32[]{:S(2)}) collective-permute-start(bf16[272,640]{1,0:T(8,128)(2,1)S(1)} %get-tuple-element.104.far_l), channel_id=1, source_target_pairs={{0,3},{1,0},{2,1},{3,2},{4,7},{5,4},{6,5},{7,6},{8,11},{9,8},{10,9... | collective-permute-start | bytes 1044488 | tf_op jit(solution)/shard_map/ppermute | solution.py:23
  98.0 12.4 %collective-permute-start.12 = (bf16[256,640]{1,0:T(8,128)(2,1)S(1)}, bf16[256,640]{1,0:T(8,128)(2,1)S(1)}, u32[]{:S(2)}, u32[]{:S(2)}) collective-permute-start(bf16[256,640]{1,0:T(8,128)(2,1)S(1)} %get-tuple-element.105.sent_r), channel_id=1, source_target_pairs={{0,1},{1,2},{2,3},{3,0},{4,5},{5,6},{6,7},{7,4},{8,9},{9,10},{10,1... | collective-permute-start | bytes 983048 | tf_op jit(solution)/shard_map/ppermute | solution.py:23
  98.1 12.4 %collective-permute-start.13 = (bf16[256,640]{1,0:T(8,128)(2,1)S(1)}, bf16[256,640]{1,0:T(8,128)(2,1)S(1)}, u32[]{:S(2)}, u32[]{:S(2)}) collective-permute-start(bf16[256,640]{1,0:T(8,128)(2,1)S(1)} %get-tuple-element.106.sent_l), channel_id=1, source_target_pairs={{0,3},{1,0},{2,1},{3,2},{4,7},{5,4},{6,5},{7,6},{8,11},{9,8},{10,9... | collective-permute-start | bytes 983048 | tf_op jit(solution)/shard_map/ppermute | solution.py:23
  104.2 13.8 %collective-permute-start.16 = (bf16[272,640]{1,0:T(8,128)(2,1)S(1)}, bf16[272,640]{1,0:T(8,128)(2,1)S(1)}, u32[]{:S(2)}, u32[]{:S(2)}) collective-permute-start(bf16[272,640]{1,0:T(8,128)(2,1)S(1)} %get-tuple-element.109), channel_id=1, source_target_pairs={{0,1},{1,2},{2,3},{3,0},{4,5},{5,6},{6,7},{7,4},{8,9},{9,10},{10,1... | collective-permute-start | bytes 1044488 | tf_op jit(solution)/shard_map/ppermute | solution.py:23
  105.4 11.9 %collective-permute-start.17 = (bf16[256,640]{1,0:T(8,128)(2,1)S(1)}, bf16[256,640]{1,0:T(8,128)(2,1)S(1)}, u32[]{:S(2)}, u32[]{:S(2)}) collective-permute-start(bf16[256,640]{1,0:T(8,128)(2,1)S(1)} %get-tuple-element.110), channel_id=1, source_target_pairs={{0,3},{1,0},{2,1},{3,2},{4,7},{5,4},{6,5},{7,6},{8,11},{9,8},{10,9... | collective-permute-start | bytes 983048 | tf_op jit(solution)/shard_map/ppermute | solution.py:23
  110.5 9.1 %copy-start.1 = (bf16[512,640]{1,0:T(8,128)(2,1)S(1)}, bf16[512,640]{1,0:T(8,128)(2,1)}, u32[]{:S(2)}) copy-start(bf16[512,640]{1,0:T(8,128)(2,1)} %param.16) | copy-start | bytes 1966084

commit v5 on v4

--- a/solution.py
+++ b/solution.py
@@ -140,23 +140,43 @@
     return call(own_body, [shape((rows, n))], (ids, x, sp, tp, wm), "own_part", 2 * rows * k * n)[0]
 
 
-def next_body(ids, r, l, sp, tp, wm, before, acc):
-    k = r.shape[1]
-    at_r, at_l = chunk_of(ids, 1, k), chunk_of(ids, 2, k)
-    c = slice(2560, 2816)
-    acc[:, c] = before[:, c] + dot(r[...], sp[at_r, :]) + dot(l[...], sp[at_l, :])
-    c = slice(2816, 2816 + tp.shape[1])
-    acc[:, c] = before[:, c] + dot(r[...], tp[at_r, :]) + dot(l[...], tp[at_l, :])
+def more_part(ids, x, which, sp, tp, wm, acc):
+    rows, k = x.shape
+    n = acc.shape[1]
+
+    def body(ids, x, sp, tp, wm, before, acc):
+        at = chunk_of(ids, which, k)
+        c = slice(2560, 2816)
+        acc[:, c] = before[:, c] + dot(x[...], sp[at, :])
+        c = slice(2816, 2816 + tp.shape[1])
+        acc[:, c] = before[:, c] + dot(x[...], tp[at, :])
+        for j in range(10):
+            c = wide(j)
+            acc[:, c] = before[:, c] + dot(x[...], wm[at, c])
+
+    return call(
+        body, [shape((rows, n))], (ids, x, sp, tp, wm, acc), "more_part", 2 * rows * k * n
+    )[0]
+
+
+def three_body(ids, x, r, l, sp, tp, wm, acc):
+    k = x.shape[1]
+    pieces = [(p[...], chunk_of(ids, i, k)) for i, p in enumerate((x, r, l))]
+
+    def project(w, c):
+        return sum(dot(p, w[at, c]) for p, at in pieces)
+
     for j in range(10):
-        c = wide(j)
-        acc[:, c] = before[:, c] + dot(r[...], wm[at_r, c]) + dot(l[...], wm[at_l, c])
-
-
-def next_part(ids, r, l, sp, tp, wm, acc):
-    rows, k = r.shape
-    n = acc.shape[1]
-    return call(
-        next_body, [shape((rows, n))], (ids, r, l, sp, tp, wm, acc), "next_part", 4 * rows * k * n
+        acc[:, wide(j)] = project(wm, wide(j))
+    acc[:, 2560:2816] = project(sp, slice(0, 256))
+    acc[:, 2816 : 2816 + tp.shape[1]] = project(tp, slice(0, tp.shape[1]))
+
+
+def three_part(ids, x, r, l, sp, tp, wm):
+    rows, k = x.shape
+    n = 2944
+    return call(
+        three_body, [shape((rows, n))], (ids, x, r, l, sp, tp, wm), "three_part", 6 * rows * k * n
     )[0]
 
 
@@ -602,19 +622,19 @@
     cut = STRETCH // 2 + TAIL
     b1 = turned(r1[:cut], 1)
     b2 = turned(l1[cut:], -1)
-    acc1 = next_part(ids, r1, l1, *weights, acc1)
+    acc1 = more_part(ids, r1, 1, *weights, acc1)
     first, acc1 = lax.optimization_barrier((first, acc1))
     r0 = turned(first, 1)
     l0 = turned(first, -1)
-    acc0 = own_part(ids, first, *weights)
-    b1, b2, acc1, acc0 = lax.optimization_barrier((b1, b2, acc1, acc0))
+    acc1 = more_part(ids, l1, 2, *weights, acc1)
+    b1, b2, acc1 = lax.optimization_barrier((b1, b2, acc1))
     *block1, payload, mid, mid_step = second_part(ids, b1, b2, *weights, acc1, *taps)
     got_s = shifted(payload, 1)
-    r0, l0, acc0, payload = lax.optimization_barrier((r0, l0, acc0, payload))
+    r0, l0, payload = lax.optimization_barrier((r0, l0, payload))
     cut = STRETCH // 2
     a1 = turned(r0[:cut], 1)
     a2 = turned(l0[cut:], -1)
-    acc0 = next_part(ids, r0, l0, *weights, acc0)
+    acc0 = three_part(ids, first, r0, l0, *weights)
     *block0, joined, joined_low, state0, end_row = first_part(
         ids, a1, a2, *weights, acc0, *taps, mid, mid_step, got_s
     )

time: 121 us -> 122 us (level)
  waiting for transfers between devices: 19.5 us -> 21.6 us
  starting transfers between devices: 38 us -> 36.5 us
    ppermute x14, waiting for transfers between devices: 15.5 us -> 17.6 us  [turned(): lax.ppermute(value, 'head', [(i, (i + steps) % RING) for i in range(RING)])]
  transfers between devices with their start and end apart: 19 -> 19, of which waited for: 8 -> 9; matrix products, arithmetic and copies ran while one was open for 2% -> 2% of each run, Pallas kernels for 26% -> 26%
where the time goes in v5:
time: 122 us; the launch traced here: 120 us
  Pallas kernels  41.6 us (34%)
  starting transfers between devices  36.5 us (30%)
  waiting for transfers between devices  21.6 us (18%)
  local copies, waits for them, and re-layouts  17.2 us (14%)
  matrix products  2.15 us (2%)
    pallas_call x14, Pallas kernels, call(): pl.pallas_call(body, in_specs=[pl.BlockSpec(memory_space=pltpu.SMEM)] + [...  41.6 us
    ppermute x14, starting transfers between devices, turned(): lax.ppermute(value, 'head', [(i, (i + steps) % RING) for i in range(RING)])  19.7 us
    ppermute x14, waiting for transfers between devices, turned(): lax.ppermute(value, 'head', [(i, (i + steps) % RING) for i in range(RING)])  17.6 us
    unnamed x41, local copies, waits for them, and re-layouts  14.9 us
    all_to_all x1, starting transfers between devices, on_device(): lax.all_to_all(outgoing, 'ctx', split_axis=0, concat_axis=0, tiled=True)  8.38 us
    ppermute x4, starting transfers between devices, shifted(): lax.ppermute(value, 'ctx', [(i, i + steps) for i in range(count - steps)])  8.37 us
    all_to_all x1, waiting for transfers between devices, on_device(): lax.all_to_all(outgoing, 'ctx', split_axis=0, concat_axis=0, tiled=True)  3.98 us
  transfers between devices with their start and end apart: 19, of which 9 were waited for; matrix products, arithmetic and copies ran while one was open for 2% of the time, Pallas kernels for 26%

profile of v5, /device:TPU:0, one launch (start us, length us, event | category | flops | bytes accessed | tf_op | source)
XLA Modules:
  0.0 120.1 jit_solution(17813591472131406609)
XLA Ops:
  0.0 0.9 eq.20
  0.9 0.2 copy-done
  1.1 2.2 %fusion.1 = bf16[1024,640]{1,0:T(8,128)(2,1)} fusion(bf16[512,640]{1,0:T(8,128)(2,1)S(1)} %copy-done, s32[1024]{0:T(1024)S(1)} %eq.20), kind=kOutput, calls=%fused_computation.4 | convolution fusion | flops 672268288 | bytes 1970176 | tf_op jit(solution)/shard_map/dot_general | solution.py:19
  3.3 8.4 %all-to-all-start = ((bf16[32,32,640]{2,1,0:T(8,128)(2,1)}), bf16[32,32,640]{2,1,0:T(8,128)(2,1)S(1)}, u32[]{:S(2)}, u32[]{:S(2)}) async-start(bf16[32,32,640]{2,1,0:T(8,128)(2,1)} %bitcast.18), calls=%async_computation | async-start | bytes 2621440 | tf_op jit(solution)/shard_map/all_to_all | solution.py:587
  11.7 0.6 gather_fusion
  12.4 0.6 gather_fusion.1
  13.0 0.2 fusion.4
  13.3 0.1 reduce.1
  13.8 4.7 %copy-done.6 = bf16[2560,2,1280]{2,1,0:T(2,128)(2,1)S(1)} copy-done((bf16[2560,2,1280]{2,1,0:T(2,128)(2,1)S(1)}, bf16[2560,2,1280]{2,1,0:T(2,128)(2,1)}, u32[]{:S(2)}) %copy-start.6) | copy-done | bytes 13107224
  18.5 4.3 %flat_part.1.wm = bf16[2560,2560]{1,0:T(8,128)(2,1)S(1)} custom-call(s32[6]{0:T(128)S(1)} %pad_add_fusion.ids, bf16[2560,2,1280]{2,1,0:T(2,128)(2,1)S(1)} %copy-done.6), custom_call_target="tpu_custom_call" | custom-call | flops 1000000000 | bytes 26214400 | tf_op jit(solution)/shard_map/flat_part/pallas_call | solution.py:59
  22.8 4.7 %copy-done.2 = bf16[2560,2560]{1,0:T(8,128)(2,1)} copy-done((bf16[2560,2560]{1,0:T(8,128)(2,1)}, bf16[2560,2560]{1,0:T(8,128)(2,1)S(1)}, u32[]{:S(2)}) %copy-start.2) | copy-done | bytes 13107224
  27.6 4.0 %all-to-all-done = bf16[32,32,640]{2,1,0:T(8,128)(2,1)S(1)} async-done(((bf16[32,32,640]{2,1,0:T(8,128)(2,1)}), bf16[32,32,640]{2,1,0:T(8,128)(2,1)S(1)}, u32[]{:S(2)}, u32[]{:S(2)}) %all-to-all-start) | async-done | bytes 1310752 | tf_op jit(solution)/shard_map/all_to_all | solution.py:587
  31.6 1.5 %arrange_part.1 = (bf16[272,640]{1,0:T(8,128)(2,1)S(1)}, bf16[240,640]{1,0:T(8,128)(2,1)S(1)}, bf16[16,640]{1,0:T(8,128)(2,1)S(1)}) custom-call(s32[6]{0:T(128)S(1)} %pad_add_fusion.ids, s32[1,1024]{1,0:T(1,128)S(1)} %select_n.56.target, bf16[1024,640]{1,0:T(8,128)(2,1)S(1)} %bitcast.17), custom_call_target="tpu_custom_call" | custom-call | flops 671088640 | bytes 1990656 | tf_op jit(solution)/shard_map/arrange_part/pallas_call | solution.py:59
  33.1 3.1 %collective-permute-start.1 = (bf16[272,640]{1,0:T(8,128)(2,1)S(1)}, bf16[272,640]{1,0:T(8,128)(2,1)S(1)}, u32[]{:S(2)}, u32[]{:S(2)}) collective-permute-start(bf16[272,640]{1,0:T(8,128)(2,1)S(1)} %get-tuple-element.60.x), channel_id=1, source_target_pairs={{0,3},{1,0},{2,1},{3,2},{4,7},{5,4},{6,5},{7,6},{8,11},{9,8},{10,9... | collective-permute-start | bytes 1044488 | tf_op jit(solution)/shard_map/ppermute | solution.py:23
  36.2 0.4 copy.21.tp
  36.6 1.8 %collective-permute-start.2 = (bf16[16,640]{1,0:T(8,128)(2,1)S(1)}, bf16[16,640]{1,0:T(8,128)(2,1)S(1)}, u32[]{:S(2)}, u32[]{:S(2)}) collective-permute-start(bf16[16,640]{1,0:T(8,128)(2,1)S(1)} %get-tuple-element.62), channel_id=1, source_target_pairs={{0,4},{4,8},{8,12},{12,16},{16,20},{20,24},{24,28},{28,32},{32,36}... | collective-permute-start | bytes 61448 | tf_op jit(solution)/shard_map/ppermute | solution.py:28
  38.4 4.7 %copy-done.3 = bf16[2560,2560]{1,0:T(8,128)(2,1)S(1)} copy-done((bf16[2560,2560]{1,0:T(8,128)(2,1)S(1)}, bf16[2560,2560]{1,0:T(8,128)(2,1)}, u32[]{:S(2)}) %copy-start.3) | copy-done | bytes 13107224
  43.1 2.0 %own_part.1.before = f32[272,2944]{1,0:T(8,128)S(1)} custom-call(s32[6]{0:T(128)S(1)} %pad_add_fusion.ids, bf16[272,640]{1,0:T(8,128)(2,1)S(1)} %get-tuple-element.60.x, bf16[2560,256]{1,0:T(8,128)(2,1)S(1)} %copy-done.5, bf16[2560,20]{1,0:T(8,128)(2,1)S(1)} %copy.21.tp, bf16[2560,2560]{1,0:T(8,128)(2,1)S(1)} %copy-done.3), custom_call_target="tpu_custom_call" | custom-call | flops 1024983040 | bytes 18071552 | tf_op jit(solution)/shard_map/own_part/pallas_call | solution.py:59
  45.2 2.2 %collective-permute-done.x = bf16[272,640]{1,0:T(8,128)(2,1)S(1)} collective-permute-done((bf16[272,640]{1,0:T(8,128)(2,1)S(1)}, bf16[272,640]{1,0:T(8,128)(2,1)S(1)}, u32[]{:S(2)}, u32[]{:S(2)}) %collective-permute-start) | collective-permute-done | bytes 348192 | tf_op jit(solution)/shard_map/ppermute | solution.py:23
  47.4 0.8 collective-permute-start.6
  48.2 1.3 %collective-permute-start.5 = (bf16[144,640]{1,0:T(8,128)(2,1)S(1)}, bf16[144,640]{1,0:T(8,128)(2,1)S(1)}, u32[]{:S(2)}, u32[]{:S(2)}) collective-permute-start(bf16[144,640]{1,0:T(8,128)(2,1)S(1)} %slice.12), channel_id=1, source_target_pairs={{0,1},{1,2},{2,3},{3,0},{4,5},{5,6},{6,7},{7,4},{8,9},{9,10},{10,1... | collective-permute-start | bytes 552968 | tf_op jit(solution)/shard_map/ppermute | solution.py:23
  49.5 2.1 %more_part.2.before = f32[272,2944]{1,0:T(8,128)S(1)} custom-call(s32[6]{0:T(128)S(1)} %pad_add_fusion.ids, bf16[272,640]{1,0:T(8,128)(2,1)S(1)} %collective-permute-done.x, bf16[2560,256]{1,0:T(8,128)(2,1)S(1)} %copy-done.5, bf16[2560,20]{1,0:T(8,128)(2,1)S(1)} %copy.21.tp, bf16[2560,2560]{1,0:T(8,128)(2,1)S(1)} %copy-done.4, f32[272,2944]{1,0:T(8,128)S(1)} %own_part.1.before), custom_call_target="tpu_custom_call" | custom-call | flops 1024983040 | bytes 21274624 | tf_op jit(solution)/shard_map/more_part/pallas_call | solution.py:59
  51.7 2.1 %collective-permute-start.4 = (bf16[256,640]{1,0:T(8,128)(2,1)S(1)}, bf16[256,640]{1,0:T(8,128)(2,1)S(1)}, u32[]{:S(2)}, u32[]{:S(2)}) collective-permute-start(bf16[256,640]{1,0:T(8,128)(2,1)S(1)} %pad_maximum_fusion.x), channel_id=1, source_target_pairs={{0,3},{1,0},{2,1},{3,2},{4,7},{5,4},{6,5},{7,6},{8,11},{9,8},{10,9... | collective-permute-start | bytes 983048 | tf_op jit(solution)/shard_map/ppermute | solution.py:23
  53.7 2.0 %more_part.3.acc.acc1 = f32[272,2944]{1,0:T(8,128)S(1)} custom-call(s32[6]{0:T(128)S(1)} %pad_add_fusion.ids, bf16[272,640]{1,0:T(8,128)(2,1)S(1)} %collective-permute-done.1.x, bf16[2560,256]{1,0:T(8,128)(2,1)S(1)} %copy-done.5, bf16[2560,20]{1,0:T(8,128)(2,1)S(1)} %copy.21.tp, bf16[2560,2560]{1,0:T(8,128)(2,1)S(1)} %copy-done.4, ...), custom_call_target="tpu_custom_call" | custom-call | flops 1024983040 | bytes 21274624 | tf_op jit(solution)/shard_map/more_part/pallas_call | solution.py:59
  55.8 0.6 collective-permute-done.5.o1.b1
  56.4 4.2 %second_part.1 = (bf16[256,1280]{1,0:T(8,128)(2,1)S(1)}, bf16[256,256]{1,0:T(8,128)(2,1)S(1)}, bf16[256,128]{1,0:T(8,128)(2,1)S(1)}, f32[32,256]{1,0:T(8,128)S(1...) custom-call(s32[6]{0:T(128)S(1)} %pad_add_fusion.ids, ...), custom_call_target="tpu_custom_call" | custom-call | flops 1090519040 | bytes 19558400 | tf_op jit(solution)/shard_map/second_part/pallas_call | solution.py:59
  60.6 1.4 %collective-permute-start.9 = (bf16[144,1280]{1,0:T(8,128)(2,1)S(1)}, bf16[144,1280]{1,0:T(8,128)(2,1)S(1)}, u32[]{:S(2)}, u32[]{:S(2)}) collective-permute-start(bf16[144,1280]{1,0:T(8,128)(2,1)S(1)} %get-tuple-element.74), channel_id=1, source_target_pairs={{0,4},{4,8},{8,12},{12,16},{16,20},{20,24},{24,28},{28,32},{32,36}... | collective-permute-start | bytes 1105928 | tf_op jit(solution)/shard_map/ppermute | solution.py:28
  62.1 2.2 %collective-permute-done.3.r = bf16[256,640]{1,0:T(8,128)(2,1)S(1)} collective-permute-done((bf16[256,640]{1,0:T(8,128)(2,1)S(1)}, bf16[256,640]{1,0:T(8,128)(2,1)S(1)}, u32[]{:S(2)}, u32[]{:S(2)}) %collective-permute-start.3) | collective-permute-done | bytes 327712 | tf_op jit(solution)/shard_map/ppermute | solution.py:23
  64.3 0.5 collective-permute-start.8
  64.8 1.6 %collective-permute-start.7 = (bf16[128,640]{1,0:T(8,128)(2,1)S(1)}, bf16[128,640]{1,0:T(8,128)(2,1)S(1)}, u32[]{:S(2)}, u32[]{:S(2)}) collective-permute-start(bf16[128,640]{1,0:T(8,128)(2,1)S(1)} %slice.14), channel_id=1, source_target_pairs={{0,1},{1,2},{2,3},{3,0},{4,5},{5,6},{6,7},{7,4},{8,9},{9,10},{10,1... | collective-permute-start | bytes 491528 | tf_op jit(solution)/shard_map/ppermute | solution.py:23
  66.4 4.3 %three_part.1.acc.acc0 = f32[256,2944]{1,0:T(8,128)S(1)} custom-call(s32[6]{0:T(128)S(1)} %pad_add_fusion.ids, bf16[256,640]{1,0:T(8,128)(2,1)S(1)} %pad_maximum_fusion.x, bf16[256,640]{1,0:T(8,128)(2,1)S(1)} %collective-permute-done.3.r, bf16[256,640]{1,0:T(8,128)(2,1)S(1)} %collective-permute-done.4.l, bf16[2560,256]{1,0:T(8,128)(2,1)S(1)} %copy-done.5, ...), custom_call_target="tpu_custom_call" | custom-call | flops 2894069760 | bytes 18518016 | tf_op jit(solution)/shard_map/three_part/pallas_call | solution.py:59
  70.8 2.2 %collective-permute-done.7.o1.a1 = bf16[128,640]{1,0:T(8,128)(2,1)S(1)} collective-permute-done((bf16[128,640]{1,0:T(8,128)(2,1)S(1)}, bf16[128,640]{1,0:T(8,128)(2,1)S(1)}, u32[]{:S(2)}, u32[]{:S(2)}) %collective-permute-start.7) | collective-permute-done | bytes 163872 | tf_op jit(solution)/shard_map/ppermute | solution.py:23
  73.0 4.2 %first_part.1 = (bf16[256,1280]{1,0:T(8,128)(2,1)S(1)}, bf16[256,256]{1,0:T(8,128)(2,1)S(1)}, bf16[256,128]{1,0:T(8,128)(2,1)S(1)}, f32[32,256]{1,0:T(8,128)S(1)...) custom-call(s32[6]{0:T(128)S(1)} %pad_add_fusion.ids, ...), custom_call_target="tpu_custom_call" | custom-call | flops 1090519040 | bytes 20742144 | tf_op jit(solution)/shard_map/first_part/pallas_call | solution.py:59
  77.2 3.3 %collective-permute-start.11 = (bf16[128,1280]{1,0:T(8,128)(2,1)S(1)}, bf16[128,1280]{1,0:T(8,128)(2,1)S(1)}, u32[]{:S(2)}, u32[]{:S(2)}) collective-permute-start(bf16[128,1280]{1,0:T(8,128)(2,1)S(1)} %get-tuple-element.94), channel_id=1, source_target_pairs={{0,8},{4,12},{8,16},{12,20},{16,24},{20,28},{24,32},{28,36},{32,40... | collective-permute-start | bytes 983048 | tf_op jit(solution)/shard_map/ppermute | solution.py:28
  80.5 1.9 %collective-permute-start.10 = (bf16[144,1280]{1,0:T(8,128)(2,1)S(1)}, bf16[144,1280]{1,0:T(8,128)(2,1)S(1)}, u32[]{:S(2)}, u32[]{:S(2)}) collective-permute-start(bf16[144,1280]{1,0:T(8,128)(2,1)S(1)} %get-tuple-element.93), channel_id=1, source_target_pairs={{0,4},{4,8},{8,12},{12,16},{16,20},{20,24},{24,28},{28,32},{32,36}... | collective-permute-start | bytes 1105928 | tf_op jit(solution)/shard_map/ppermute | solution.py:28
  82.4 7.4 %mix_part.1 = (f32[512,1280]{1,0:T(8,128)S(1)}, f32[512,1280]{1,0:T(8,128)S(1)}) custom-call(s32[6]{0:T(128)S(1)} %pad_add_fusion.ids, bf16[128,640]{1,0:T(8,128)(2,1)S(1)} %collective-permute-done.7.o1.a1, bf16[128,640]{1,0:T(8,128)(2,1)S(1)} %collective-permute-done.8.o2.a2, bf16[144,640]{1,0:T(8,128)(2,1)S(1)} %collective-permute-done.5.o1.b1, ...), custom_call_target="tpu_custom_call" | custom-call | flops 8000000000 | bytes 27213824 | tf_op jit(solution)/shard_map/mix_part/pallas_call | solution.py:59
  89.9 2.6 %gated_part.1 = (bf16[512,1280]{1,0:T(8,128)(2,1)S(1)}, bf16[272,640]{1,0:T(8,128)(2,1)S(1)}, bf16[272,640]{1,0:T(8,128)(2,1)S(1)}, f32[8,512]{1,0:T(8,128)S(1)}) custom-call(s32[6]{0:T(128)S(1)} %pad_add_fusion.ids, f32[512,1280]{1,0:T(8,128)S(1)} %get-tuple-element.91.p, f32[512,1280]{1,0:T(8,128)S(1)} %get-tuple-element.92.q, ...), custom_call_target="tpu_custom_call" | custom-call | flops 1006632960 | bytes 15848448 | tf_op jit(solution)/shard_map/gated_part/pallas_call | solution.py:59
  92.6 3.2 %collective-permute-start.15 = (bf16[272,640]{1,0:T(8,128)(2,1)S(1)}, bf16[272,640]{1,0:T(8,128)(2,1)S(1)}, u32[]{:S(2)}, u32[]{:S(2)}) collective-permute-start(bf16[272,640]{1,0:T(8,128)(2,1)S(1)} %get-tuple-element.100.far_l), channel_id=1, source_target_pairs={{0,3},{1,0},{2,1},{3,2},{4,7},{5,4},{6,5},{7,6},{8,11},{9,8},{10,9... | collective-permute-start | bytes 1044488 | tf_op jit(solution)/shard_map/ppermute | solution.py:23
  95.8 2.8 %near_part.1 = (bf16[256,640]{1,0:T(8,128)(2,1)S(1)}, bf16[256,640]{1,0:T(8,128)(2,1)S(1)}, f32[256,640]{1,0:T(8,128)S(1)}, f32[256,640]{1,0:T(8,128)S(1)}) custom-call(s32[6]{0:T(128)S(1)} %pad_add_fusion.ids, bf16[512,1280]{1,0:T(8,128)(2,1)S(1)} %get-tuple-element.98.z, bf16[1280,2560]{1,0:T(8,128)(2,1)S(1)} %bitcast.14, ...), custom_call_target="tpu_custom_call" | custom-call | flops 1677721600 | bytes 10526720 | tf_op jit(solution)/shard_map/near_part/pallas_call | solution.py:59
  98.7 3.2 %collective-permute-start.13 = (bf16[256,640]{1,0:T(8,128)(2,1)S(1)}, bf16[256,640]{1,0:T(8,128)(2,1)S(1)}, u32[]{:S(2)}, u32[]{:S(2)}) collective-permute-start(bf16[256,640]{1,0:T(8,128)(2,1)S(1)} %get-tuple-element.102.sent_l), channel_id=1, source_target_pairs={{0,3},{1,0},{2,1},{3,2},{4,7},{5,4},{6,5},{7,6},{8,11},{9,8},{10,9... | collective-permute-start | bytes 983048 | tf_op jit(solution)/shard_map/ppermute | solution.py:23
  101.9 2.1 %collective-permute-done.14.b1.sq_r = bf16[272,640]{1,0:T(8,128)(2,1)S(1)} collective-permute-done((bf16[272,640]{1,0:T(8,128)(2,1)S(1)}, bf16[272,640]{1,0:T(8,128)(2,1)S(1)}, u32[]{:S(2)}, u32[]{:S(2)}) %collective-permute-start.14) | collective-permute-done | bytes 348192 | tf_op jit(solution)/shard_map/ppermute | solution.py:23
  104.0 0.7 add_part.1
  104.8 3.6 %collective-permute-start.17 = (bf16[256,640]{1,0:T(8,128)(2,1)S(1)}, bf16[256,640]{1,0:T(8,128)(2,1)S(1)}, u32[]{:S(2)}, u32[]{:S(2)}) collective-permute-start(bf16[256,640]{1,0:T(8,128)(2,1)S(1)} %get-tuple-element.106), channel_id=1, source_target_pairs={{0,3},{1,0},{2,1},{3,2},{4,7},{5,4},{6,5},{7,6},{8,11},{9,8},{10,9... | collective-permute-start | bytes 983048 | tf_op jit(solution)/shard_map/ppermute | solution.py:23
  108.4 2.6 %collective-permute-done.12.low_r = bf16[256,640]{1,0:T(8,128)(2,1)S(1)} collective-permute-done((bf16[256,640]{1,0:T(8,128)(2,1)S(1)}, bf16[256,640]{1,0:T(8,128)(2,1)S(1)}, u32[]{:S(2)}, u32[]{:S(2)}) %collective-permute-start.12) | collective-permute-done | bytes 327712 | tf_op jit(solution)/shard_map/ppermute | solution.py:23
  111.1 1.7 %mine_part.1.own = f32[512,640]{1,0:T(8,128)S(1)} custom-call(s32[6]{0:T(128)S(1)} %pad_add_fusion.ids, bf16[512,1280]{1,0:T(8,128)(2,1)S(1)} %get-tuple-element.98.z, bf16[1280,2560]{1,0:T(8,128)(2,1)S(1)} %bitcast.16, bf16[256,640]{1,0:T(8,128)(2,1)S(1)} %collective-permute-done.12.low_r, bf16[256,640]{1,0:T(8,128)(2,1)S(1)} %collective-permute-done.13.top_l), custom_call_target="tpu_custom_call" | custom-call | flops 1677721600 | bytes 9830400 | tf_op jit(solution)/shard_map/mine_part/pallas_call | solution.py:59
  112.8 5.1 %collective-permute-done.17.low_l = bf16[256,640]{1,0:T(8,128)(2,1)S(1)} collective-permute-done((bf16[256,640]{1,0:T(8,128)(2,1)S(1)}, bf16[256,640]{1,0:T(8,128)(2,1)S(1)}, u32[]{:S(2)}, u32[]{:S(2)}) %collective-permute-start.17) | collective-permute-done | bytes 327712 | tf_op jit(solution)/shard_map/ppermute | solution.py:23
  117.9 0.6 collective-permute-done.16.top_r
  118.5 1.6 %final_part.1 = bf16[512,640]{1,0:T(8,128)(2,1)} custom-call(s32[6]{0:T(128)S(1)} %pad_add_fusion.ids, f32[512,640]{1,0:T(8,128)S(1)} %mine_part.1.own, bf16[272,640]{1,0:T(8,128)(2,1)S(1)} %collective-permute-done.16.top_r, bf16[256,640]{1,0:T(8,128)(2,1)S(1)} %collective-permute-done.17.low_l, f32[8,512]{1,0:T(8,128)S(1)} %get-tuple-element.107.mine, ...), custom_call_target="tpu_custom_call" | custom-call | flops 1310720 | bytes 3354624 | tf_op jit(solution)/shard_map/final_part/pallas_call | solution.py:59
  (73 shorter events, 0.9 us)
Async XLA Ops:
  0.0 1.1 copy-start
  1.1 10.6 %copy-start.14 = (f32[20]{0:T(128)S(1)}, f32[20]{0:T(128)}, u32[]{:S(2)}) copy-start(f32[20]{0:T(128)} %param.26) | copy-start | bytes 244
  1.1 10.6 %copy-start.9 = (s32[64]{0:T(128)S(1)}, s32[64]{0:T(128)}, u32[]{:S(2)}) copy-start(s32[64]{0:T(128)} %param.19) | copy-start | bytes 772
  3.3 9.8 %copy-start.12 = (f32[1280]{0:T(1024)S(1)}, f32[1280]{0:T(1024)}, u32[]{:S(2)}) copy-start(f32[1280]{0:T(1024)} %param.28) | copy-start | bytes 15364
  3.3 9.8 %copy-start.11 = (s32[32,32]{1,0:T(8,128)S(1)}, s32[32,32]{1,0:T(8,128)}, u32[]{:S(2)}) copy-start(s32[32,32]{1,0:T(8,128)} %param.18) | copy-start | bytes 12292
  3.3 28.3 %all-to-all-start = ((bf16[32,32,640]{2,1,0:T(8,128)(2,1)}), bf16[32,32,640]{2,1,0:T(8,128)(2,1)S(1)}, u32[]{:S(2)}, u32[]{:S(2)}) async-start(bf16[32,32,640]{2,1,0:T(8,128)(2,1)} %bitcast.18), calls=%async_computation | async-start | bytes 2621440 | tf_op jit(solution)/shard_map/all_to_all | solution.py:587
  13.8 4.7 %copy-start.6 = (bf16[2560,2,1280]{2,1,0:T(2,128)(2,1)S(1)}, bf16[2560,2,1280]{2,1,0:T(2,128)(2,1)}, u32[]{:S(2)}) copy-start(bf16[2560,2,1280]{2,1,0:T(2,128)(2,1)} %w.1) | copy-start | bytes 39321604
  18.5 9.1 %copy-start.15 = (f32[20]{0:T(128)S(1)}, f32[20]{0:T(128)}, u32[]{:S(2)}) copy-start(f32[20]{0:T(128)} %param.25) | copy-start | bytes 244
  18.5 9.1 %copy-start.13 = (f32[20]{0:T(128)S(1)}, f32[20]{0:T(128)}, u32[]{:S(2)}) copy-start(f32[20]{0:T(128)} %param.27) | copy-start | bytes 244
  18.5 17.8 %copy-start.10 = (bf16[2560,20]{0,1:T(8,128)(2,1)S(1)}, bf16[2560,20]{0,1:T(8,128)(2,1)}, u32[]{:S(2)}) copy-start(bf16[2560,20]{0,1:T(8,128)(2,1)} %param.22) | copy-start | bytes 307204
  22.8 4.8 %copy-start.2 = (bf16[2560,2560]{1,0:T(8,128)(2,1)}, bf16[2560,2560]{1,0:T(8,128)(2,1)S(1)}, u32[]{:S(2)}) copy-start(bf16[2560,2560]{1,0:T(8,128)(2,1)S(1)} %flat_part.1.wm) | copy-start | bytes 39321604
  27.6 10.8 %copy-start.5 = (bf16[2560,256]{1,0:T(8,128)(2,1)S(1)}, bf16[2560,256]{1,0:T(8,128)(2,1)}, u32[]{:S(2)}) copy-start(bf16[2560,256]{1,0:T(8,128)(2,1)} %sp.11) | copy-start | bytes 3932164
  33.1 12.0 %collective-permute-start.1 = (bf16[272,640]{1,0:T(8,128)(2,1)S(1)}, bf16[272,640]{1,0:T(8,128)(2,1)S(1)}, u32[]{:S(2)}, u32[]{:S(2)}) collective-permute-start(bf16[272,640]{1,0:T(8,128)(2,1)S(1)} %get-tuple-element.60.x), channel_id=1, source_target_pairs={{0,3},{1,0},{2,1},{3,2},{4,7},{5,4},{6,5},{7,6},{8,11},{9,8},{10,9... | collective-permute-start | bytes 1044488 | tf_op jit(solution)/shard_map/ppermute | solution.py:23
  36.2 11.1 %collective-permute-start = (bf16[272,640]{1,0:T(8,128)(2,1)S(1)}, bf16[272,640]{1,0:T(8,128)(2,1)S(1)}, u32[]{:S(2)}, u32[]{:S(2)}) collective-permute-start(bf16[272,640]{1,0:T(8,128)(2,1)S(1)} %get-tuple-element.60.x), channel_id=1, source_target_pairs={{0,1},{1,2},{2,3},{3,0},{4,5},{5,6},{6,7},{7,4},{8,9},{9,10},{10,1... | collective-permute-start | bytes 1044488 | tf_op jit(solution)/shard_map/ppermute | solution.py:23
  36.6 8.5 %collective-permute-start.2 = (bf16[16,640]{1,0:T(8,128)(2,1)S(1)}, bf16[16,640]{1,0:T(8,128)(2,1)S(1)}, u32[]{:S(2)}, u32[]{:S(2)}) collective-permute-start(bf16[16,640]{1,0:T(8,128)(2,1)S(1)} %get-tuple-element.62), channel_id=1, source_target_pairs={{0,4},{4,8},{8,12},{12,16},{16,20},{20,24},{24,28},{28,32},{32,36}... | collective-permute-start | bytes 61448 | tf_op jit(solution)/shard_map/ppermute | solution.py:28
  38.4 4.7 %copy-start.3 = (bf16[2560,2560]{1,0:T(8,128)(2,1)S(1)}, bf16[2560,2560]{1,0:T(8,128)(2,1)}, u32[]{:S(2)}) copy-start(bf16[2560,2560]{1,0:T(8,128)(2,1)} %copy-done.2) | copy-start | bytes 39321604
  43.1 6.5 %copy-start.4 = (bf16[2560,2560]{1,0:T(8,128)(2,1)S(1)}, bf16[2560,2560]{1,0:T(8,128)(2,1)}, u32[]{:S(2)}) copy-start(bf16[2560,2560]{1,0:T(8,128)(2,1)} %copy-done.2) | copy-start | bytes 39321604
  47.4 8.4 %collective-permute-start.6 = (bf16[128,640]{1,0:T(8,128)(2,1)S(1)}, bf16[128,640]{1,0:T(8,128)(2,1)S(1)}, u32[]{:S(2)}, u32[]{:S(2)}) collective-permute-start(bf16[128,640]{1,0:T(8,128)(2,1)S(1)} %slice.13), channel_id=1, source_target_pairs={{0,3},{1,0},{2,1},{3,2},{4,7},{5,4},{6,5},{7,6},{8,11},{9,8},{10,9... | collective-permute-start | bytes 491528 | tf_op jit(solution)/shard_map/ppermute | solution.py:23
  48.2 8.1 %collective-permute-start.5 = (bf16[144,640]{1,0:T(8,128)(2,1)S(1)}, bf16[144,640]{1,0:T(8,128)(2,1)S(1)}, u32[]{:S(2)}, u32[]{:S(2)}) collective-permute-start(bf16[144,640]{1,0:T(8,128)(2,1)S(1)} %slice.12), channel_id=1, source_target_pairs={{0,1},{1,2},{2,3},{3,0},{4,5},{5,6},{6,7},{7,4},{8,9},{9,10},{10,1... | collective-permute-start | bytes 552968 | tf_op jit(solution)/shard_map/ppermute | solution.py:23
  51.6 4.7 %copy-start.7 = (f32[4,1280]{1,0:T(4,128)S(1)}, f32[4,1280]{1,0:T(4,128)}, u32[]{:S(2)}) copy-start(f32[4,1280]{1,0:T(4,128)} %taps_v.3) | copy-start | bytes 61444
  51.6 4.7 %copy-start.8 = (f32[4,256]{1,0:T(4,128)S(1)}, f32[4,256]{1,0:T(4,128)}, u32[]{:S(2)}) copy-start(f32[4,256]{1,0:T(4,128)} %taps_s.3) | copy-start | bytes 12292
  51.7 10.4 %collective-permute-start.4 = (bf16[256,640]{1,0:T(8,128)(2,1)S(1)}, bf16[256,640]{1,0:T(8,128)(2,1)S(1)}, u32[]{:S(2)}, u32[]{:S(2)}) collective-permute-start(bf16[256,640]{1,0:T(8,128)(2,1)S(1)} %pad_maximum_fusion.x), channel_id=1, source_target_pairs={{0,3},{1,0},{2,1},{3,2},{4,7},{5,4},{6,5},{7,6},{8,11},{9,8},{10,9... | collective-permute-start | bytes 983048 | tf_op jit(solution)/shard_map/ppermute | solution.py:23
  53.7 10.6 %collective-permute-start.3 = (bf16[256,640]{1,0:T(8,128)(2,1)S(1)}, bf16[256,640]{1,0:T(8,128)(2,1)S(1)}, u32[]{:S(2)}, u32[]{:S(2)}) collective-permute-start(bf16[256,640]{1,0:T(8,128)(2,1)S(1)} %pad_maximum_fusion.x), channel_id=1, source_target_pairs={{0,1},{1,2},{2,3},{3,0},{4,5},{5,6},{6,7},{7,4},{8,9},{9,10},{10,1... | collective-permute-start | bytes 983048 | tf_op jit(solution)/shard_map/ppermute | solution.py:23
  60.6 12.3 %collective-permute-start.9 = (bf16[144,1280]{1,0:T(8,128)(2,1)S(1)}, bf16[144,1280]{1,0:T(8,128)(2,1)S(1)}, u32[]{:S(2)}, u32[]{:S(2)}) collective-permute-start(bf16[144,1280]{1,0:T(8,128)(2,1)S(1)} %get-tuple-element.74), channel_id=1, source_target_pairs={{0,4},{4,8},{8,12},{12,16},{16,20},{20,24},{24,28},{28,32},{32,36}... | collective-permute-start | bytes 1105928 | tf_op jit(solution)/shard_map/ppermute | solution.py:28
  64.3 6.5 %collective-permute-start.8 = (bf16[128,640]{1,0:T(8,128)(2,1)S(1)}, bf16[128,640]{1,0:T(8,128)(2,1)S(1)}, u32[]{:S(2)}, u32[]{:S(2)}) collective-permute-start(bf16[128,640]{1,0:T(8,128)(2,1)S(1)} %slice.15), channel_id=1, source_target_pairs={{0,3},{1,0},{2,1},{3,2},{4,7},{5,4},{6,5},{7,6},{8,11},{9,8},{10,9... | collective-permute-start | bytes 491528 | tf_op jit(solution)/shard_map/ppermute | solution.py:23
  64.8 8.1 %collective-permute-start.7 = (bf16[128,640]{1,0:T(8,128)(2,1)S(1)}, bf16[128,640]{1,0:T(8,128)(2,1)S(1)}, u32[]{:S(2)}, u32[]{:S(2)}) collective-permute-start(bf16[128,640]{1,0:T(8,128)(2,1)S(1)} %slice.14), channel_id=1, source_target_pairs={{0,1},{1,2},{2,3},{3,0},{4,5},{5,6},{6,7},{7,4},{8,9},{9,10},{10,1... | collective-permute-start | bytes 491528 | tf_op jit(solution)/shard_map/ppermute | solution.py:23
  77.2 12.7 %collective-permute-start.11 = (bf16[128,1280]{1,0:T(8,128)(2,1)S(1)}, bf16[128,1280]{1,0:T(8,128)(2,1)S(1)}, u32[]{:S(2)}, u32[]{:S(2)}) collective-permute-start(bf16[128,1280]{1,0:T(8,128)(2,1)S(1)} %get-tuple-element.94), channel_id=1, source_target_pairs={{0,8},{4,12},{8,16},{12,20},{16,24},{20,28},{24,32},{28,36},{32,40... | collective-permute-start | bytes 983048 | tf_op jit(solution)/shard_map/ppermute | solution.py:28
  80.5 9.3 %collective-permute-start.10 = (bf16[144,1280]{1,0:T(8,128)(2,1)S(1)}, bf16[144,1280]{1,0:T(8,128)(2,1)S(1)}, u32[]{:S(2)}, u32[]{:S(2)}) collective-permute-start(bf16[144,1280]{1,0:T(8,128)(2,1)S(1)} %get-tuple-element.93), channel_id=1, source_target_pairs={{0,4},{4,8},{8,12},{12,16},{16,20},{20,24},{24,28},{28,32},{32,36}... | collective-permute-start | bytes 1105928 | tf_op jit(solution)/shard_map/ppermute | solution.py:28
  82.4 7.5 %slice-start = ((s8[6553600]{0:T(1024)(128)(4,1)}), s8[4194304]{0:T(1024)(128)(4,1)S(1)}, s32[]{:S(2)}) async-start(s8[6553600]{0:T(1024)(128)(4,1)} %bitcast.13), calls=%async_computation.1 | async-start | bytes 8388608
  82.4 7.5 %slice-start.1 = ((s8[6553600]{0:T(1024)(128)(4,1)}), s8[2359296]{0:T(1024)(128)(4,1)S(1)}, s32[]{:S(2)}) async-start(s8[6553600]{0:T(1024)(128)(4,1)} %bitcast.13), calls=%async_computation.2 | async-start | bytes 4718592
  89.8 21.2 %slice-start.2 = ((s8[6553600]{0:T(1024)(128)(4,1)}), s8[4194304]{0:T(1024)(128)(4,1)S(1)}, s32[]{:S(2)}) async-start(s8[6553600]{0:T(1024)(128)(4,1)} %bitcast.15), calls=%async_computation.3 | async-start | bytes 8388608
  89.9 21.2 %slice-start.3 = ((s8[6553600]{0:T(1024)(128)(4,1)}), s8[2359296]{0:T(1024)(128)(4,1)S(1)}, s32[]{:S(2)}) async-start(s8[6553600]{0:T(1024)(128)(4,1)} %bitcast.15), calls=%async_computation.4 | async-start | bytes 4718592
  92.5 11.5 %collective-permute-start.14 = (bf16[272,640]{1,0:T(8,128)(2,1)S(1)}, bf16[272,640]{1,0:T(8,128)(2,1)S(1)}, u32[]{:S(2)}, u32[]{:S(2)}) collective-permute-start(bf16[272,640]{1,0:T(8,128)(2,1)S(1)} %get-tuple-element.99.far_r), channel_id=1, source_target_pairs={{0,1},{1,2},{2,3},{3,0},{4,5},{5,6},{6,7},{7,4},{8,9},{9,10},{10,1... | collective-permute-start | bytes 1044488 | tf_op jit(solution)/shard_map/ppermute | solution.py:23
  92.6 11.5 %collective-permute-start.15 = (bf16[272,640]{1,0:T(8,128)(2,1)S(1)}, bf16[272,640]{1,0:T(8,128)(2,1)S(1)}, u32[]{:S(2)}, u32[]{:S(2)}) collective-permute-start(bf16[272,640]{1,0:T(8,128)(2,1)S(1)} %get-tuple-element.100.far_l), channel_id=1, source_target_pairs={{0,3},{1,0},{2,1},{3,2},{4,7},{5,4},{6,5},{7,6},{8,11},{9,8},{10,9... | collective-permute-start | bytes 1044488 | tf_op jit(solution)/shard_map/ppermute | solution.py:23
  98.6 12.4 %collective-permute-start.12 = (bf16[256,640]{1,0:T(8,128)(2,1)S(1)}, bf16[256,640]{1,0:T(8,128)(2,1)S(1)}, u32[]{:S(2)}, u32[]{:S(2)}) collective-permute-start(bf16[256,640]{1,0:T(8,128)(2,1)S(1)} %get-tuple-element.101.sent_r), channel_id=1, source_target_pairs={{0,1},{1,2},{2,3},{3,0},{4,5},{5,6},{6,7},{7,4},{8,9},{9,10},{10,1... | collective-permute-start | bytes 983048 | tf_op jit(solution)/shard_map/ppermute | solution.py:23
  98.7 12.4 %collective-permute-start.13 = (bf16[256,640]{1,0:T(8,128)(2,1)S(1)}, bf16[256,640]{1,0:T(8,128)(2,1)S(1)}, u32[]{:S(2)}, u32[]{:S(2)}) collective-permute-start(bf16[256,640]{1,0:T(8,128)(2,1)S(1)} %get-tuple-element.102.sent_l), channel_id=1, source_target_pairs={{0,3},{1,0},{2,1},{3,2},{4,7},{5,4},{6,5},{7,6},{8,11},{9,8},{10,9... | collective-permute-start | bytes 983048 | tf_op jit(solution)/shard_map/ppermute | solution.py:23
  104.7 13.8 %collective-permute-start.16 = (bf16[272,640]{1,0:T(8,128)(2,1)S(1)}, bf16[272,640]{1,0:T(8,128)(2,1)S(1)}, u32[]{:S(2)}, u32[]{:S(2)}) collective-permute-start(bf16[272,640]{1,0:T(8,128)(2,1)S(1)} %get-tuple-element.105), channel_id=1, source_target_pairs={{0,1},{1,2},{2,3},{3,0},{4,5},{5,6},{6,7},{7,4},{8,9},{9,10},{10,1... | collective-permute-start | bytes 1044488 | tf_op jit(solution)/shard_map/ppermute | solution.py:23
  104.8 13.1 %collective-permute-start.17 = (bf16[256,640]{1,0:T(8,128)(2,1)S(1)}, bf16[256,640]{1,0:T(8,128)(2,1)S(1)}, u32[]{:S(2)}, u32[]{:S(2)}) collective-permute-start(bf16[256,640]{1,0:T(8,128)(2,1)S(1)} %get-tuple-element.106), channel_id=1, source_target_pairs={{0,3},{1,0},{2,1},{3,2},{4,7},{5,4},{6,5},{7,6},{8,11},{9,8},{10,9... | collective-permute-start | bytes 983048 | tf_op jit(solution)/shard_map/ppermute | solution.py:23
  111.1 9.1 %copy-start.1 = (bf16[512,640]{1,0:T(8,128)(2,1)S(1)}, bf16[512,640]{1,0:T(8,128)(2,1)}, u32[]{:S(2)}) copy-start(bf16[512,640]{1,0:T(8,128)(2,1)} %param.16) | copy-start | bytes 1966084

commit v6 on v4

--- a/solution.py
+++ b/solution.py
@@ -586,8 +586,8 @@
     slot = jnp.arange(slots, dtype=jnp.int32)[None, :]
     target = jnp.where(slot < column[:, None], begins[:, None] + slot, -1)
     target = target.reshape(1, sources * slots)
-    arrived, wm, target, head_rows, gain, ids = lax.optimization_barrier(
-        (arrived, wm, target, head_rows, gain, ids)
+    arrived, wm, target, head_rows, gain, ids, step_proj = lax.optimization_barrier(
+        (arrived, wm, target, head_rows, gain, ids, step_proj)
     )
     second, first, last = arrange_part(ids, target, arrived.reshape(sources * slots, width))
     weights = (state_proj, step_proj, wm)

time: 121 us -> 122 us (level)
    unnamed x41 -> x40, local copies, waits for them, and re-layouts: 14.9 us -> 14.5 us
where the time goes in v6:
time: 122 us; the launch traced here: 120 us
  Pallas kernels  41.6 us (34%)
  starting transfers between devices  38 us (31%)
  waiting for transfers between devices  19.5 us (16%)
  local copies, waits for them, and re-layouts  17.2 us (14%)
  matrix products  2.15 us (2%)
    pallas_call x14, Pallas kernels, call(): pl.pallas_call(body, in_specs=[pl.BlockSpec(memory_space=pltpu.SMEM)] + [...  41.6 us
    ppermute x14, starting transfers between devices, turned(): lax.ppermute(value, 'head', [(i, (i + steps) % RING) for i in range(RING)])  20.8 us
    ppermute x14, waiting for transfers between devices, turned(): lax.ppermute(value, 'head', [(i, (i + steps) % RING) for i in range(RING)])  15.5 us
    unnamed x40, local copies, waits for them, and re-layouts  14.5 us
    ppermute x4, starting transfers between devices, shifted(): lax.ppermute(value, 'ctx', [(i, i + steps) for i in range(count - steps)])  8.82 us
    all_to_all x1, starting transfers between devices, on_device(): lax.all_to_all(outgoing, 'ctx', split_axis=0, concat_axis=0, tiled=True)  8.38 us
    all_to_all x1, waiting for transfers between devices, on_device(): lax.all_to_all(outgoing, 'ctx', split_axis=0, concat_axis=0, tiled=True)  3.98 us
  transfers between devices with their start and end apart: 19, of which 8 were waited for; matrix products, arithmetic and copies ran while one was open for 2% of the time, Pallas kernels for 26%

profile of v6, /device:TPU:0, one launch (start us, length us, event | category | flops | bytes accessed | tf_op | source)
XLA Modules:
  0.0 119.6 jit_solution(6047137390930044857)
XLA Ops:
  0.0 0.9 eq.20
  0.9 0.2 copy-done
  1.1 2.2 %fusion.1 = bf16[1024,640]{1,0:T(8,128)(2,1)} fusion(bf16[512,640]{1,0:T(8,128)(2,1)S(1)} %copy-done, s32[1024]{0:T(1024)S(1)} %eq.20), kind=kOutput, calls=%fused_computation.4 | convolution fusion | flops 672268288 | bytes 1970176 | tf_op jit(solution)/shard_map/dot_general | solution.py:19
  3.3 8.4 %all-to-all-start = ((bf16[32,32,640]{2,1,0:T(8,128)(2,1)}), bf16[32,32,640]{2,1,0:T(8,128)(2,1)S(1)}, u32[]{:S(2)}, u32[]{:S(2)}) async-start(bf16[32,32,640]{2,1,0:T(8,128)(2,1)} %bitcast.18), calls=%async_computation | async-start | bytes 2621440 | tf_op jit(solution)/shard_map/all_to_all | solution.py:567
  11.7 0.6 gather_fusion
  12.4 0.6 gather_fusion.1
  13.0 0.2 fusion.4
  13.3 0.1 reduce.1
  13.6 0.1 and_select_fusion.1
  13.8 4.7 %copy-done.6 = bf16[2560,2,1280]{2,1,0:T(2,128)(2,1)S(1)} copy-done((bf16[2560,2,1280]{2,1,0:T(2,128)(2,1)S(1)}, bf16[2560,2,1280]{2,1,0:T(2,128)(2,1)}, u32[]{:S(2)}) %copy-start.6) | copy-done | bytes 13107224
  18.5 4.3 %flat_part.1.wm = bf16[2560,2560]{1,0:T(8,128)(2,1)S(1)} custom-call(s32[6]{0:T(128)S(1)} %pad_add_fusion.ids, bf16[2560,2,1280]{2,1,0:T(2,128)(2,1)S(1)} %copy-done.6), custom_call_target="tpu_custom_call" | custom-call | flops 1000000000 | bytes 26214400 | tf_op jit(solution)/shard_map/flat_part/pallas_call | solution.py:59
  22.8 4.7 %copy-done.2 = bf16[2560,2560]{1,0:T(8,128)(2,1)} copy-done((bf16[2560,2560]{1,0:T(8,128)(2,1)}, bf16[2560,2560]{1,0:T(8,128)(2,1)S(1)}, u32[]{:S(2)}) %copy-start.2) | copy-done | bytes 13107224
  27.6 4.0 %all-to-all-done = bf16[32,32,640]{2,1,0:T(8,128)(2,1)S(1)} async-done(((bf16[32,32,640]{2,1,0:T(8,128)(2,1)}), bf16[32,32,640]{2,1,0:T(8,128)(2,1)S(1)}, u32[]{:S(2)}, u32[]{:S(2)}) %all-to-all-start) | async-done | bytes 1310752 | tf_op jit(solution)/shard_map/all_to_all | solution.py:567
  31.6 1.5 %arrange_part.1 = (bf16[272,640]{1,0:T(8,128)(2,1)S(1)}, bf16[240,640]{1,0:T(8,128)(2,1)S(1)}, bf16[16,640]{1,0:T(8,128)(2,1)S(1)}) custom-call(s32[6]{0:T(128)S(1)} %pad_add_fusion.ids, s32[1,1024]{1,0:T(1,128)S(1)} %select_n.56.target, bf16[1024,640]{1,0:T(8,128)(2,1)S(1)} %bitcast.17), custom_call_target="tpu_custom_call" | custom-call | flops 671088640 | bytes 1990656 | tf_op jit(solution)/shard_map/arrange_part/pallas_call | solution.py:59
  33.1 3.1 %collective-permute-start.1 = (bf16[272,640]{1,0:T(8,128)(2,1)S(1)}, bf16[272,640]{1,0:T(8,128)(2,1)S(1)}, u32[]{:S(2)}, u32[]{:S(2)}) collective-permute-start(bf16[272,640]{1,0:T(8,128)(2,1)S(1)} %get-tuple-element.63.x), channel_id=1, source_target_pairs={{0,3},{1,0},{2,1},{3,2},{4,7},{5,4},{6,5},{7,6},{8,11},{9,8},{10,9... | collective-permute-start | bytes 1044488 | tf_op jit(solution)/shard_map/ppermute | solution.py:23
  36.2 1.7 %collective-permute-start.2 = (bf16[16,640]{1,0:T(8,128)(2,1)S(1)}, bf16[16,640]{1,0:T(8,128)(2,1)S(1)}, u32[]{:S(2)}, u32[]{:S(2)}) collective-permute-start(bf16[16,640]{1,0:T(8,128)(2,1)S(1)} %get-tuple-element.66), channel_id=1, source_target_pairs={{0,4},{4,8},{8,12},{12,16},{16,20},{20,24},{24,28},{28,32},{32,36}... | collective-permute-start | bytes 61448 | tf_op jit(solution)/shard_map/ppermute | solution.py:28
  38.0 0.4 copy.21.tp
  38.4 4.7 %copy-done.3 = bf16[2560,2560]{1,0:T(8,128)(2,1)S(1)} copy-done((bf16[2560,2560]{1,0:T(8,128)(2,1)S(1)}, bf16[2560,2560]{1,0:T(8,128)(2,1)}, u32[]{:S(2)}) %copy-start.3) | copy-done | bytes 13107224
  43.1 2.0 %own_part.2.before = f32[272,2944]{1,0:T(8,128)S(1)} custom-call(s32[6]{0:T(128)S(1)} %pad_add_fusion.ids, bf16[272,640]{1,0:T(8,128)(2,1)S(1)} %get-tuple-element.63.x, bf16[2560,256]{1,0:T(8,128)(2,1)S(1)} %copy-done.5, bf16[2560,20]{1,0:T(8,128)(2,1)S(1)} %copy.21.tp, bf16[2560,2560]{1,0:T(8,128)(2,1)S(1)} %copy-done.3), custom_call_target="tpu_custom_call" | custom-call | flops 1024983040 | bytes 18071552 | tf_op jit(solution)/shard_map/own_part/pallas_call | solution.py:59
  45.1 2.2 %collective-permute-done.r = bf16[272,640]{1,0:T(8,128)(2,1)S(1)} collective-permute-done((bf16[272,640]{1,0:T(8,128)(2,1)S(1)}, bf16[272,640]{1,0:T(8,128)(2,1)S(1)}, u32[]{:S(2)}, u32[]{:S(2)}) %collective-permute-start) | collective-permute-done | bytes 348192 | tf_op jit(solution)/shard_map/ppermute | solution.py:23
  47.4 0.8 collective-permute-start.6
  48.2 1.2 %collective-permute-start.5 = (bf16[144,640]{1,0:T(8,128)(2,1)S(1)}, bf16[144,640]{1,0:T(8,128)(2,1)S(1)}, u32[]{:S(2)}, u32[]{:S(2)}) collective-permute-start(bf16[144,640]{1,0:T(8,128)(2,1)S(1)} %slice.12), channel_id=1, source_target_pairs={{0,1},{1,2},{2,3},{3,0},{4,5},{5,6},{6,7},{7,4},{8,9},{9,10},{10,1... | collective-permute-start | bytes 552968 | tf_op jit(solution)/shard_map/ppermute | solution.py:23
  49.5 3.4 %next_part.2.acc.acc1 = f32[272,2944]{1,0:T(8,128)S(1)} custom-call(s32[6]{0:T(128)S(1)} %pad_add_fusion.ids, bf16[272,640]{1,0:T(8,128)(2,1)S(1)} %collective-permute-done.r, bf16[272,640]{1,0:T(8,128)(2,1)S(1)} %collective-permute-done.1.l, bf16[2560,256]{1,0:T(8,128)(2,1)S(1)} %copy-done.5, bf16[2560,20]{1,0:T(8,128)(2,1)S(1)} %copy.21.tp, ...), custom_call_target="tpu_custom_call" | custom-call | flops 2049966080 | bytes 21622784 | tf_op jit(solution)/shard_map/next_part/pallas_call | solution.py:59
  52.9 2.1 %collective-permute-start.4 = (bf16[256,640]{1,0:T(8,128)(2,1)S(1)}, bf16[256,640]{1,0:T(8,128)(2,1)S(1)}, u32[]{:S(2)}, u32[]{:S(2)}) collective-permute-start(bf16[256,640]{1,0:T(8,128)(2,1)S(1)} %pad_maximum_fusion.x), channel_id=1, source_target_pairs={{0,3},{1,0},{2,1},{3,2},{4,7},{5,4},{6,5},{7,6},{8,11},{9,8},{10,9... | collective-permute-start | bytes 983048 | tf_op jit(solution)/shard_map/ppermute | solution.py:23
  55.0 1.9 %own_part.3.before = f32[256,2944]{1,0:T(8,128)S(1)} custom-call(s32[6]{0:T(128)S(1)} %pad_add_fusion.ids, bf16[256,640]{1,0:T(8,128)(2,1)S(1)} %pad_maximum_fusion.x, bf16[2560,256]{1,0:T(8,128)(2,1)S(1)} %copy-done.5, bf16[2560,20]{1,0:T(8,128)(2,1)S(1)} %copy.21.tp, bf16[2560,2560]{1,0:T(8,128)(2,1)S(1)} %copy-done.4), custom_call_target="tpu_custom_call" | custom-call | flops 964689920 | bytes 17862656 | tf_op jit(solution)/shard_map/own_part/pallas_call | solution.py:59
  56.9 4.3 %second_part.1 = (bf16[256,1280]{1,0:T(8,128)(2,1)S(1)}, bf16[256,256]{1,0:T(8,128)(2,1)S(1)}, bf16[256,128]{1,0:T(8,128)(2,1)S(1)}, f32[32,256]{1,0:T(8,128)S(1...) custom-call(s32[6]{0:T(128)S(1)} %pad_add_fusion.ids, ...), custom_call_target="tpu_custom_call" | custom-call | flops 1090519040 | bytes 19558400 | tf_op jit(solution)/shard_map/second_part/pallas_call | solution.py:59
  61.2 1.6 %collective-permute-start.9 = (bf16[144,1280]{1,0:T(8,128)(2,1)S(1)}, bf16[144,1280]{1,0:T(8,128)(2,1)S(1)}, u32[]{:S(2)}, u32[]{:S(2)}) collective-permute-start(bf16[144,1280]{1,0:T(8,128)(2,1)S(1)} %get-tuple-element.79), channel_id=1, source_target_pairs={{0,4},{4,8},{8,12},{12,16},{16,20},{20,24},{24,28},{28,32},{32,36}... | collective-permute-start | bytes 1105928 | tf_op jit(solution)/shard_map/ppermute | solution.py:28
  62.9 2.6 %collective-permute-done.3.r = bf16[256,640]{1,0:T(8,128)(2,1)S(1)} collective-permute-done((bf16[256,640]{1,0:T(8,128)(2,1)S(1)}, bf16[256,640]{1,0:T(8,128)(2,1)S(1)}, u32[]{:S(2)}, u32[]{:S(2)}) %collective-permute-start.3) | collective-permute-done | bytes 327712 | tf_op jit(solution)/shard_map/ppermute | solution.py:23
  65.6 3.2 %collective-permute-start.8 = (bf16[128,640]{1,0:T(8,128)(2,1)S(1)}, bf16[128,640]{1,0:T(8,128)(2,1)S(1)}, u32[]{:S(2)}, u32[]{:S(2)}) collective-permute-start(bf16[128,640]{1,0:T(8,128)(2,1)S(1)} %slice.15), channel_id=1, source_target_pairs={{0,3},{1,0},{2,1},{3,2},{4,7},{5,4},{6,5},{7,6},{8,11},{9,8},{10,9... | collective-permute-start | bytes 491528 | tf_op jit(solution)/shard_map/ppermute | solution.py:23
  68.9 3.2 %next_part.3.acc.acc0 = f32[256,2944]{1,0:T(8,128)S(1)} custom-call(s32[6]{0:T(128)S(1)} %pad_add_fusion.ids, bf16[256,640]{1,0:T(8,128)(2,1)S(1)} %collective-permute-done.3.r, bf16[256,640]{1,0:T(8,128)(2,1)S(1)} %collective-permute-done.4.l, bf16[2560,256]{1,0:T(8,128)(2,1)S(1)} %copy-done.5, bf16[2560,20]{1,0:T(8,128)(2,1)S(1)} %copy.21.tp, ...), custom_call_target="tpu_custom_call" | custom-call | flops 1929379840 | bytes 21204992 | tf_op jit(solution)/shard_map/next_part/pallas_call | solution.py:59
  72.1 0.1 collective-permute-done.7.o1.a1
  72.2 4.2 %first_part.1 = (bf16[256,1280]{1,0:T(8,128)(2,1)S(1)}, bf16[256,256]{1,0:T(8,128)(2,1)S(1)}, bf16[256,128]{1,0:T(8,128)(2,1)S(1)}, f32[32,256]{1,0:T(8,128)S(1)...) custom-call(s32[6]{0:T(128)S(1)} %pad_add_fusion.ids, ...), custom_call_target="tpu_custom_call" | custom-call | flops 1090519040 | bytes 20742144 | tf_op jit(solution)/shard_map/first_part/pallas_call | solution.py:59
  76.4 3.9 %collective-permute-start.11 = (bf16[128,1280]{1,0:T(8,128)(2,1)S(1)}, bf16[128,1280]{1,0:T(8,128)(2,1)S(1)}, u32[]{:S(2)}, u32[]{:S(2)}) collective-permute-start(bf16[128,1280]{1,0:T(8,128)(2,1)S(1)} %get-tuple-element.100), channel_id=1, source_target_pairs={{0,8},{4,12},{8,16},{12,20},{16,24},{20,28},{24,32},{28,36},{32,40... | collective-permute-start | bytes 983048 | tf_op jit(solution)/shard_map/ppermute | solution.py:28
  80.3 1.5 %collective-permute-start.10 = (bf16[144,1280]{1,0:T(8,128)(2,1)S(1)}, bf16[144,1280]{1,0:T(8,128)(2,1)S(1)}, u32[]{:S(2)}, u32[]{:S(2)}) collective-permute-start(bf16[144,1280]{1,0:T(8,128)(2,1)S(1)} %get-tuple-element.99), channel_id=1, source_target_pairs={{0,4},{4,8},{8,12},{12,16},{16,20},{20,24},{24,28},{28,32},{32,36}... | collective-permute-start | bytes 1105928 | tf_op jit(solution)/shard_map/ppermute | solution.py:28
  81.9 7.4 %mix_part.1 = (f32[512,1280]{1,0:T(8,128)S(1)}, f32[512,1280]{1,0:T(8,128)S(1)}) custom-call(s32[6]{0:T(128)S(1)} %pad_add_fusion.ids, bf16[128,640]{1,0:T(8,128)(2,1)S(1)} %collective-permute-done.7.o1.a1, bf16[128,640]{1,0:T(8,128)(2,1)S(1)} %collective-permute-done.8.o2.a2, bf16[144,640]{1,0:T(8,128)(2,1)S(1)} %collective-permute-done.5.o1.b1, ...), custom_call_target="tpu_custom_call" | custom-call | flops 8000000000 | bytes 27213824 | tf_op jit(solution)/shard_map/mix_part/pallas_call | solution.py:59
  89.3 2.6 %gated_part.1 = (bf16[512,1280]{1,0:T(8,128)(2,1)S(1)}, bf16[272,640]{1,0:T(8,128)(2,1)S(1)}, bf16[272,640]{1,0:T(8,128)(2,1)S(1)}, f32[8,512]{1,0:T(8,128)S(1)}) custom-call(s32[6]{0:T(128)S(1)} %pad_add_fusion.ids, f32[512,1280]{1,0:T(8,128)S(1)} %get-tuple-element.97.p, f32[512,1280]{1,0:T(8,128)S(1)} %get-tuple-element.98.q, ...), custom_call_target="tpu_custom_call" | custom-call | flops 1006632960 | bytes 15848448 | tf_op jit(solution)/shard_map/gated_part/pallas_call | solution.py:59
  92.0 3.2 %collective-permute-start.15 = (bf16[272,640]{1,0:T(8,128)(2,1)S(1)}, bf16[272,640]{1,0:T(8,128)(2,1)S(1)}, u32[]{:S(2)}, u32[]{:S(2)}) collective-permute-start(bf16[272,640]{1,0:T(8,128)(2,1)S(1)} %get-tuple-element.106.far_l), channel_id=1, source_target_pairs={{0,3},{1,0},{2,1},{3,2},{4,7},{5,4},{6,5},{7,6},{8,11},{9,8},{10,9... | collective-permute-start | bytes 1044488 | tf_op jit(solution)/shard_map/ppermute | solution.py:23
  95.2 2.8 %near_part.1 = (bf16[256,640]{1,0:T(8,128)(2,1)S(1)}, bf16[256,640]{1,0:T(8,128)(2,1)S(1)}, f32[256,640]{1,0:T(8,128)S(1)}, f32[256,640]{1,0:T(8,128)S(1)}) custom-call(s32[6]{0:T(128)S(1)} %pad_add_fusion.ids, bf16[512,1280]{1,0:T(8,128)(2,1)S(1)} %get-tuple-element.104.z, bf16[1280,2560]{1,0:T(8,128)(2,1)S(1)} %bitcast.14, ...), custom_call_target="tpu_custom_call" | custom-call | flops 1677721600 | bytes 10526720 | tf_op jit(solution)/shard_map/near_part/pallas_call | solution.py:59
  98.1 3.2 %collective-permute-start.13 = (bf16[256,640]{1,0:T(8,128)(2,1)S(1)}, bf16[256,640]{1,0:T(8,128)(2,1)S(1)}, u32[]{:S(2)}, u32[]{:S(2)}) collective-permute-start(bf16[256,640]{1,0:T(8,128)(2,1)S(1)} %get-tuple-element.108.sent_l), channel_id=1, source_target_pairs={{0,3},{1,0},{2,1},{3,2},{4,7},{5,4},{6,5},{7,6},{8,11},{9,8},{10,9... | collective-permute-start | bytes 983048 | tf_op jit(solution)/shard_map/ppermute | solution.py:23
  101.3 2.2 %collective-permute-done.14.b1.sq_r = bf16[272,640]{1,0:T(8,128)(2,1)S(1)} collective-permute-done((bf16[272,640]{1,0:T(8,128)(2,1)S(1)}, bf16[272,640]{1,0:T(8,128)(2,1)S(1)}, u32[]{:S(2)}, u32[]{:S(2)}) %collective-permute-start.14) | collective-permute-done | bytes 348192 | tf_op jit(solution)/shard_map/ppermute | solution.py:23
  103.5 0.7 add_part.1
  104.2 1.2 %collective-permute-start.16 = (bf16[272,640]{1,0:T(8,128)(2,1)S(1)}, bf16[272,640]{1,0:T(8,128)(2,1)S(1)}, u32[]{:S(2)}, u32[]{:S(2)}) collective-permute-start(bf16[272,640]{1,0:T(8,128)(2,1)S(1)} %get-tuple-element.111), channel_id=1, source_target_pairs={{0,1},{1,2},{2,3},{3,0},{4,5},{5,6},{6,7},{7,4},{8,9},{9,10},{10,1... | collective-permute-start | bytes 1044488 | tf_op jit(solution)/shard_map/ppermute | solution.py:23
  105.4 2.4 %collective-permute-start.17 = (bf16[256,640]{1,0:T(8,128)(2,1)S(1)}, bf16[256,640]{1,0:T(8,128)(2,1)S(1)}, u32[]{:S(2)}, u32[]{:S(2)}) collective-permute-start(bf16[256,640]{1,0:T(8,128)(2,1)S(1)} %get-tuple-element.112), channel_id=1, source_target_pairs={{0,3},{1,0},{2,1},{3,2},{4,7},{5,4},{6,5},{7,6},{8,11},{9,8},{10,9... | collective-permute-start | bytes 983048 | tf_op jit(solution)/shard_map/ppermute | solution.py:23
  107.8 2.7 %collective-permute-done.12.low_r = bf16[256,640]{1,0:T(8,128)(2,1)S(1)} collective-permute-done((bf16[256,640]{1,0:T(8,128)(2,1)S(1)}, bf16[256,640]{1,0:T(8,128)(2,1)S(1)}, u32[]{:S(2)}, u32[]{:S(2)}) %collective-permute-start.12) | collective-permute-done | bytes 327712 | tf_op jit(solution)/shard_map/ppermute | solution.py:23
  110.6 1.7 %mine_part.1.own = f32[512,640]{1,0:T(8,128)S(1)} custom-call(s32[6]{0:T(128)S(1)} %pad_add_fusion.ids, bf16[512,1280]{1,0:T(8,128)(2,1)S(1)} %get-tuple-element.104.z, bf16[1280,2560]{1,0:T(8,128)(2,1)S(1)} %bitcast.16, bf16[256,640]{1,0:T(8,128)(2,1)S(1)} %collective-permute-done.12.low_r, bf16[256,640]{1,0:T(8,128)(2,1)S(1)} %collective-permute-done.13.top_l), custom_call_target="tpu_custom_call" | custom-call | flops 1677721600 | bytes 9830400 | tf_op jit(solution)/shard_map/mine_part/pallas_call | solution.py:59
  112.3 5.0 %collective-permute-done.17.low_l = bf16[256,640]{1,0:T(8,128)(2,1)S(1)} collective-permute-done((bf16[256,640]{1,0:T(8,128)(2,1)S(1)}, bf16[256,640]{1,0:T(8,128)(2,1)S(1)}, u32[]{:S(2)}, u32[]{:S(2)}) %collective-permute-start.17) | collective-permute-done | bytes 327712 | tf_op jit(solution)/shard_map/ppermute | solution.py:23
  117.3 0.7 collective-permute-done.16.top_r
  118.0 1.6 %final_part.1 = bf16[512,640]{1,0:T(8,128)(2,1)} custom-call(s32[6]{0:T(128)S(1)} %pad_add_fusion.ids, f32[512,640]{1,0:T(8,128)S(1)} %mine_part.1.own, bf16[272,640]{1,0:T(8,128)(2,1)S(1)} %collective-permute-done.16.top_r, bf16[256,640]{1,0:T(8,128)(2,1)S(1)} %collective-permute-done.17.low_l, f32[8,512]{1,0:T(8,128)S(1)} %get-tuple-element.113.mine, ...), custom_call_target="tpu_custom_call" | custom-call | flops 1310720 | bytes 3354624 | tf_op jit(solution)/shard_map/final_part/pallas_call | solution.py:59
  (73 shorter events, 0.8 us)
Async XLA Ops:
  0.0 1.1 copy-start
  1.1 10.6 %copy-start.14 = (f32[20]{0:T(128)S(1)}, f32[20]{0:T(128)}, u32[]{:S(2)}) copy-start(f32[20]{0:T(128)} %param.26) | copy-start | bytes 244
  1.1 10.6 %copy-start.9 = (s32[64]{0:T(128)S(1)}, s32[64]{0:T(128)}, u32[]{:S(2)}) copy-start(s32[64]{0:T(128)} %param.19) | copy-start | bytes 772
  3.3 9.8 %copy-start.12 = (f32[1280]{0:T(1024)S(1)}, f32[1280]{0:T(1024)}, u32[]{:S(2)}) copy-start(f32[1280]{0:T(1024)} %param.28) | copy-start | bytes 15364
  3.3 9.8 %copy-start.11 = (s32[32,32]{1,0:T(8,128)S(1)}, s32[32,32]{1,0:T(8,128)}, u32[]{:S(2)}) copy-start(s32[32,32]{1,0:T(8,128)} %param.18) | copy-start | bytes 12292
  3.3 28.3 %all-to-all-start = ((bf16[32,32,640]{2,1,0:T(8,128)(2,1)}), bf16[32,32,640]{2,1,0:T(8,128)(2,1)S(1)}, u32[]{:S(2)}, u32[]{:S(2)}) async-start(bf16[32,32,640]{2,1,0:T(8,128)(2,1)} %bitcast.18), calls=%async_computation | async-start | bytes 2621440 | tf_op jit(solution)/shard_map/all_to_all | solution.py:567
  13.8 4.7 %copy-start.6 = (bf16[2560,2,1280]{2,1,0:T(2,128)(2,1)S(1)}, bf16[2560,2,1280]{2,1,0:T(2,128)(2,1)}, u32[]{:S(2)}) copy-start(bf16[2560,2,1280]{2,1,0:T(2,128)(2,1)} %w.1) | copy-start | bytes 39321604
  18.5 9.1 %copy-start.15 = (f32[20]{0:T(128)S(1)}, f32[20]{0:T(128)}, u32[]{:S(2)}) copy-start(f32[20]{0:T(128)} %param.25) | copy-start | bytes 244
  18.5 9.1 %copy-start.13 = (f32[20]{0:T(128)S(1)}, f32[20]{0:T(128)}, u32[]{:S(2)}) copy-start(f32[20]{0:T(128)} %param.27) | copy-start | bytes 244
  18.5 19.5 %copy-start.10 = (bf16[2560,20]{0,1:T(8,128)(2,1)S(1)}, bf16[2560,20]{0,1:T(8,128)(2,1)}, u32[]{:S(2)}) copy-start(bf16[2560,20]{0,1:T(8,128)(2,1)} %param.22) | copy-start | bytes 307204
  22.8 4.8 %copy-start.2 = (bf16[2560,2560]{1,0:T(8,128)(2,1)}, bf16[2560,2560]{1,0:T(8,128)(2,1)S(1)}, u32[]{:S(2)}) copy-start(bf16[2560,2560]{1,0:T(8,128)(2,1)S(1)} %flat_part.1.wm) | copy-start | bytes 39321604
  27.6 10.8 %copy-start.5 = (bf16[2560,256]{1,0:T(8,128)(2,1)S(1)}, bf16[2560,256]{1,0:T(8,128)(2,1)}, u32[]{:S(2)}) copy-start(bf16[2560,256]{1,0:T(8,128)(2,1)} %sp.11) | copy-start | bytes 3932164
  33.1 12.0 %collective-permute-start.1 = (bf16[272,640]{1,0:T(8,128)(2,1)S(1)}, bf16[272,640]{1,0:T(8,128)(2,1)S(1)}, u32[]{:S(2)}, u32[]{:S(2)}) collective-permute-start(bf16[272,640]{1,0:T(8,128)(2,1)S(1)} %get-tuple-element.63.x), channel_id=1, source_target_pairs={{0,3},{1,0},{2,1},{3,2},{4,7},{5,4},{6,5},{7,6},{8,11},{9,8},{10,9... | collective-permute-start | bytes 1044488 | tf_op jit(solution)/shard_map/ppermute | solution.py:23
  36.2 11.1 %collective-permute-start = (bf16[272,640]{1,0:T(8,128)(2,1)S(1)}, bf16[272,640]{1,0:T(8,128)(2,1)S(1)}, u32[]{:S(2)}, u32[]{:S(2)}) collective-permute-start(bf16[272,640]{1,0:T(8,128)(2,1)S(1)} %get-tuple-element.63.x), channel_id=1, source_target_pairs={{0,1},{1,2},{2,3},{3,0},{4,5},{5,6},{6,7},{7,4},{8,9},{9,10},{10,1... | collective-permute-start | bytes 1044488 | tf_op jit(solution)/shard_map/ppermute | solution.py:23
  36.2 8.9 %collective-permute-start.2 = (bf16[16,640]{1,0:T(8,128)(2,1)S(1)}, bf16[16,640]{1,0:T(8,128)(2,1)S(1)}, u32[]{:S(2)}, u32[]{:S(2)}) collective-permute-start(bf16[16,640]{1,0:T(8,128)(2,1)S(1)} %get-tuple-element.66), channel_id=1, source_target_pairs={{0,4},{4,8},{8,12},{12,16},{16,20},{20,24},{24,28},{28,32},{32,36}... | collective-permute-start | bytes 61448 | tf_op jit(solution)/shard_map/ppermute | solution.py:28
  38.4 4.7 %copy-start.3 = (bf16[2560,2560]{1,0:T(8,128)(2,1)S(1)}, bf16[2560,2560]{1,0:T(8,128)(2,1)}, u32[]{:S(2)}) copy-start(bf16[2560,2560]{1,0:T(8,128)(2,1)} %copy-done.2) | copy-start | bytes 39321604
  43.1 6.4 %copy-start.4 = (bf16[2560,2560]{1,0:T(8,128)(2,1)S(1)}, bf16[2560,2560]{1,0:T(8,128)(2,1)}, u32[]{:S(2)}) copy-start(bf16[2560,2560]{1,0:T(8,128)(2,1)} %copy-done.2) | copy-start | bytes 39321604
  47.4 9.5 %collective-permute-start.6 = (bf16[128,640]{1,0:T(8,128)(2,1)S(1)}, bf16[128,640]{1,0:T(8,128)(2,1)S(1)}, u32[]{:S(2)}, u32[]{:S(2)}) collective-permute-start(bf16[128,640]{1,0:T(8,128)(2,1)S(1)} %slice.13), channel_id=1, source_target_pairs={{0,3},{1,0},{2,1},{3,2},{4,7},{5,4},{6,5},{7,6},{8,11},{9,8},{10,9... | collective-permute-start | bytes 491528 | tf_op jit(solution)/shard_map/ppermute | solution.py:23
  48.2 8.7 %collective-permute-start.5 = (bf16[144,640]{1,0:T(8,128)(2,1)S(1)}, bf16[144,640]{1,0:T(8,128)(2,1)S(1)}, u32[]{:S(2)}, u32[]{:S(2)}) collective-permute-start(bf16[144,640]{1,0:T(8,128)(2,1)S(1)} %slice.12), channel_id=1, source_target_pairs={{0,1},{1,2},{2,3},{3,0},{4,5},{5,6},{6,7},{7,4},{8,9},{9,10},{10,1... | collective-permute-start | bytes 552968 | tf_op jit(solution)/shard_map/ppermute | solution.py:23
  52.9 4.1 %copy-start.7 = (f32[4,1280]{1,0:T(4,128)S(1)}, f32[4,1280]{1,0:T(4,128)}, u32[]{:S(2)}) copy-start(f32[4,1280]{1,0:T(4,128)} %taps_v.3) | copy-start | bytes 61444
  52.9 4.1 %copy-start.8 = (f32[4,256]{1,0:T(4,128)S(1)}, f32[4,256]{1,0:T(4,128)}, u32[]{:S(2)}) copy-start(f32[4,256]{1,0:T(4,128)} %taps_s.3) | copy-start | bytes 12292
  52.9 10.0 %collective-permute-start.4 = (bf16[256,640]{1,0:T(8,128)(2,1)S(1)}, bf16[256,640]{1,0:T(8,128)(2,1)S(1)}, u32[]{:S(2)}, u32[]{:S(2)}) collective-permute-start(bf16[256,640]{1,0:T(8,128)(2,1)S(1)} %pad_maximum_fusion.x), channel_id=1, source_target_pairs={{0,3},{1,0},{2,1},{3,2},{4,7},{5,4},{6,5},{7,6},{8,11},{9,8},{10,9... | collective-permute-start | bytes 983048 | tf_op jit(solution)/shard_map/ppermute | solution.py:23
  54.9 10.6 %collective-permute-start.3 = (bf16[256,640]{1,0:T(8,128)(2,1)S(1)}, bf16[256,640]{1,0:T(8,128)(2,1)S(1)}, u32[]{:S(2)}, u32[]{:S(2)}) collective-permute-start(bf16[256,640]{1,0:T(8,128)(2,1)S(1)} %pad_maximum_fusion.x), channel_id=1, source_target_pairs={{0,1},{1,2},{2,3},{3,0},{4,5},{5,6},{6,7},{7,4},{8,9},{9,10},{10,1... | collective-permute-start | bytes 983048 | tf_op jit(solution)/shard_map/ppermute | solution.py:23
  61.2 11.0 %collective-permute-start.9 = (bf16[144,1280]{1,0:T(8,128)(2,1)S(1)}, bf16[144,1280]{1,0:T(8,128)(2,1)S(1)}, u32[]{:S(2)}, u32[]{:S(2)}) collective-permute-start(bf16[144,1280]{1,0:T(8,128)(2,1)S(1)} %get-tuple-element.79), channel_id=1, source_target_pairs={{0,4},{4,8},{8,12},{12,16},{16,20},{20,24},{24,28},{28,32},{32,36}... | collective-permute-start | bytes 1105928 | tf_op jit(solution)/shard_map/ppermute | solution.py:28
  65.5 6.6 %collective-permute-start.7 = (bf16[128,640]{1,0:T(8,128)(2,1)S(1)}, bf16[128,640]{1,0:T(8,128)(2,1)S(1)}, u32[]{:S(2)}, u32[]{:S(2)}) collective-permute-start(bf16[128,640]{1,0:T(8,128)(2,1)S(1)} %slice.14), channel_id=1, source_target_pairs={{0,1},{1,2},{2,3},{3,0},{4,5},{5,6},{6,7},{7,4},{8,9},{9,10},{10,1... | collective-permute-start | bytes 491528 | tf_op jit(solution)/shard_map/ppermute | solution.py:23
  65.6 6.5 %collective-permute-start.8 = (bf16[128,640]{1,0:T(8,128)(2,1)S(1)}, bf16[128,640]{1,0:T(8,128)(2,1)S(1)}, u32[]{:S(2)}, u32[]{:S(2)}) collective-permute-start(bf16[128,640]{1,0:T(8,128)(2,1)S(1)} %slice.15), channel_id=1, source_target_pairs={{0,3},{1,0},{2,1},{3,2},{4,7},{5,4},{6,5},{7,6},{8,11},{9,8},{10,9... | collective-permute-start | bytes 491528 | tf_op jit(solution)/shard_map/ppermute | solution.py:23
  76.4 12.9 %collective-permute-start.11 = (bf16[128,1280]{1,0:T(8,128)(2,1)S(1)}, bf16[128,1280]{1,0:T(8,128)(2,1)S(1)}, u32[]{:S(2)}, u32[]{:S(2)}) collective-permute-start(bf16[128,1280]{1,0:T(8,128)(2,1)S(1)} %get-tuple-element.100), channel_id=1, source_target_pairs={{0,8},{4,12},{8,16},{12,20},{16,24},{20,28},{24,32},{28,36},{32,40... | collective-permute-start | bytes 983048 | tf_op jit(solution)/shard_map/ppermute | solution.py:28
  80.3 9.0 %collective-permute-start.10 = (bf16[144,1280]{1,0:T(8,128)(2,1)S(1)}, bf16[144,1280]{1,0:T(8,128)(2,1)S(1)}, u32[]{:S(2)}, u32[]{:S(2)}) collective-permute-start(bf16[144,1280]{1,0:T(8,128)(2,1)S(1)} %get-tuple-element.99), channel_id=1, source_target_pairs={{0,4},{4,8},{8,12},{12,16},{16,20},{20,24},{24,28},{28,32},{32,36}... | collective-permute-start | bytes 1105928 | tf_op jit(solution)/shard_map/ppermute | solution.py:28
  81.8 7.5 %slice-start = ((s8[6553600]{0:T(1024)(128)(4,1)}), s8[4194304]{0:T(1024)(128)(4,1)S(1)}, s32[]{:S(2)}) async-start(s8[6553600]{0:T(1024)(128)(4,1)} %bitcast.13), calls=%async_computation.1 | async-start | bytes 8388608
  81.8 7.5 %slice-start.1 = ((s8[6553600]{0:T(1024)(128)(4,1)}), s8[2359296]{0:T(1024)(128)(4,1)S(1)}, s32[]{:S(2)}) async-start(s8[6553600]{0:T(1024)(128)(4,1)} %bitcast.13), calls=%async_computation.2 | async-start | bytes 4718592
  89.3 21.3 %slice-start.2 = ((s8[6553600]{0:T(1024)(128)(4,1)}), s8[4194304]{0:T(1024)(128)(4,1)S(1)}, s32[]{:S(2)}) async-start(s8[6553600]{0:T(1024)(128)(4,1)} %bitcast.15), calls=%async_computation.3 | async-start | bytes 8388608
  89.3 21.2 %slice-start.3 = ((s8[6553600]{0:T(1024)(128)(4,1)}), s8[2359296]{0:T(1024)(128)(4,1)S(1)}, s32[]{:S(2)}) async-start(s8[6553600]{0:T(1024)(128)(4,1)} %bitcast.15), calls=%async_computation.4 | async-start | bytes 4718592
  91.9 11.6 %collective-permute-start.14 = (bf16[272,640]{1,0:T(8,128)(2,1)S(1)}, bf16[272,640]{1,0:T(8,128)(2,1)S(1)}, u32[]{:S(2)}, u32[]{:S(2)}) collective-permute-start(bf16[272,640]{1,0:T(8,128)(2,1)S(1)} %get-tuple-element.105.far_r), channel_id=1, source_target_pairs={{0,1},{1,2},{2,3},{3,0},{4,5},{5,6},{6,7},{7,4},{8,9},{9,10},{10,1... | collective-permute-start | bytes 1044488 | tf_op jit(solution)/shard_map/ppermute | solution.py:23
  92.0 11.5 %collective-permute-start.15 = (bf16[272,640]{1,0:T(8,128)(2,1)S(1)}, bf16[272,640]{1,0:T(8,128)(2,1)S(1)}, u32[]{:S(2)}, u32[]{:S(2)}) collective-permute-start(bf16[272,640]{1,0:T(8,128)(2,1)S(1)} %get-tuple-element.106.far_l), channel_id=1, source_target_pairs={{0,3},{1,0},{2,1},{3,2},{4,7},{5,4},{6,5},{7,6},{8,11},{9,8},{10,9... | collective-permute-start | bytes 1044488 | tf_op jit(solution)/shard_map/ppermute | solution.py:23
  98.0 12.5 %collective-permute-start.12 = (bf16[256,640]{1,0:T(8,128)(2,1)S(1)}, bf16[256,640]{1,0:T(8,128)(2,1)S(1)}, u32[]{:S(2)}, u32[]{:S(2)}) collective-permute-start(bf16[256,640]{1,0:T(8,128)(2,1)S(1)} %get-tuple-element.107.sent_r), channel_id=1, source_target_pairs={{0,1},{1,2},{2,3},{3,0},{4,5},{5,6},{6,7},{7,4},{8,9},{9,10},{10,1... | collective-permute-start | bytes 983048 | tf_op jit(solution)/shard_map/ppermute | solution.py:23
  98.1 12.4 %collective-permute-start.13 = (bf16[256,640]{1,0:T(8,128)(2,1)S(1)}, bf16[256,640]{1,0:T(8,128)(2,1)S(1)}, u32[]{:S(2)}, u32[]{:S(2)}) collective-permute-start(bf16[256,640]{1,0:T(8,128)(2,1)S(1)} %get-tuple-element.108.sent_l), channel_id=1, source_target_pairs={{0,3},{1,0},{2,1},{3,2},{4,7},{5,4},{6,5},{7,6},{8,11},{9,8},{10,9... | collective-permute-start | bytes 983048 | tf_op jit(solution)/shard_map/ppermute | solution.py:23
  104.2 13.8 %collective-permute-start.16 = (bf16[272,640]{1,0:T(8,128)(2,1)S(1)}, bf16[272,640]{1,0:T(8,128)(2,1)S(1)}, u32[]{:S(2)}, u32[]{:S(2)}) collective-permute-start(bf16[272,640]{1,0:T(8,128)(2,1)S(1)} %get-tuple-element.111), channel_id=1, source_target_pairs={{0,1},{1,2},{2,3},{3,0},{4,5},{5,6},{6,7},{7,4},{8,9},{9,10},{10,1... | collective-permute-start | bytes 1044488 | tf_op jit(solution)/shard_map/ppermute | solution.py:23
  105.4 11.9 %collective-permute-start.17 = (bf16[256,640]{1,0:T(8,128)(2,1)S(1)}, bf16[256,640]{1,0:T(8,128)(2,1)S(1)}, u32[]{:S(2)}, u32[]{:S(2)}) collective-permute-start(bf16[256,640]{1,0:T(8,128)(2,1)S(1)} %get-tuple-element.112), channel_id=1, source_target_pairs={{0,3},{1,0},{2,1},{3,2},{4,7},{5,4},{6,5},{7,6},{8,11},{9,8},{10,9... | collective-permute-start | bytes 983048 | tf_op jit(solution)/shard_map/ppermute | solution.py:23
  110.6 9.1 %copy-start.1 = (bf16[512,640]{1,0:T(8,128)(2,1)S(1)}, bf16[512,640]{1,0:T(8,128)(2,1)}, u32[]{:S(2)}) copy-start(bf16[512,640]{1,0:T(8,128)(2,1)} %param.16) | copy-start | bytes 1966084
